TPU v7x, 32 devices: a whole 2x2x4 slice. The times are simulated.
32 devices in a mesh: groups: 2 (over x), fsdp: 4 (over y, core), tensor: 4 (over z).
Axes of the slice: x: 2, y: 2, z: 4, core: 2. Of those that a mesh axis runs over, the one named last changes fastest.
Arguments:
- tokens: bfloat16 [8192, 5120], P(('groups', 'fsdp', 'tensor')), parts along dimension 0, may hold values from -6 to 6
- w_qkv: bfloat16 [10240, 6144], P(('groups', 'fsdp', 'tensor')), parts along dimension 0, may hold values from -0.078125 to 0.078125
- norm_gain: float32 [5120], replicated, may hold values from 0.1 to 1.9
- q_gain: float32 [128], replicated, may hold values from 0.5 to 3
- k_gain: float32 [128], replicated, may hold values from 0.5 to 3
- lengths: int32 [8], P(('groups', 'fsdp')), parts along dimension 0, may hold values from 256 to 1024, as said below
Outputs:
- attended: bfloat16 [8192, 4096], P(('groups', 'fsdp'), 'tensor'), parts along dimension 0
There are 2 independent parts, one for each index of `groups`. A program takes and returns all parts, laid end to end along the dimension named above; an argument that names none is the same for every part. Nothing has to cross between parts.
Inputs may be any that keep to these rules, and one draw needn't show every extreme that they name: `lengths`: one prompt has the full length 1024.
All inputs are finite; a program needn't handle non-finite values.
Results may differ from a plain program's by a relative error of at most 0.012.
The roundings to bfloat16 on the way count: a program that leaves them out, or rounds other values in their place, can miss the bound.
Values may be sent and summed in bfloat16 or wider, within the bound.
No kernel may reach another device: no remote copies, remote signals or barrier semaphores. Data moves between devices by JAX's collectives and lax.ppermute only.
A program may use at most 192 MiB of HBM per device.

v0:
```python
import functools
import jax
import jax.numpy as jnp
from jax import lax
from jax.experimental import pallas as pl
from jax.experimental.pallas import tpu as pltpu
from jax.sharding import PartitionSpec as P

KV = 8
HD = 128
GQ = 4
LOG2E = 1.4426950408889634
VMEM_BYTES = 48 * 1024 * 1024


def head_norm(vec, gain):
    scale = lax.rsqrt(jnp.mean(vec * vec, axis=-1, keepdims=True) + 1e-06)
    return vec * scale * gain


def angles(positions):
    half = HD // 2
    freqs = 1000000.0 ** (-2.0 * jnp.arange(half, dtype=jnp.float32) / HD)
    return positions.astype(jnp.float32)[:, None] * freqs[None, :]


def rotate(vec, positions):
    half = vec.shape[-1] // 2
    angle = angles(positions)
    cosine = jnp.cos(angle)[:, None, None, :]
    sine = jnp.sin(angle)[:, None, None, :]
    first = vec[..., :half]
    second = vec[..., half:]
    return jnp.concatenate(
        [first * cosine - second * sine, second * cosine + first * sine], axis=-1
    )


def attend(qkv, q_gain, k_gain, length):
    rows = qkv.shape[0]
    group = qkv.shape[2] - 2
    positions = jnp.arange(rows, dtype=jnp.int32)
    query = rotate(head_norm(qkv[:, :, :group], q_gain), positions).astype(jnp.bfloat16)
    keyed = rotate(head_norm(qkv[:, :, group : group + 1], k_gain), positions)[:, :, 0].astype(
        jnp.bfloat16
    )
    value = qkv[:, :, group + 1].astype(jnp.bfloat16)
    scores = jnp.einsum(
        "ikgd,jkd->kgij", query, keyed, preferred_element_type=jnp.float32
    ) / jnp.sqrt(jnp.float32(qkv.shape[3]))
    allowed = (positions[None, :] <= positions[:, None]) & (positions[None, :] < length)
    scores = jnp.where(allowed[None, None], scores, jnp.float32(-1e30))
    top = jnp.max(scores, axis=-1, keepdims=True)
    weights = jnp.exp(scores - top)
    probs = (weights / jnp.sum(weights, axis=-1, keepdims=True)).astype(jnp.bfloat16)
    out = jnp.einsum("kgij,jkd->ikgd", probs, value, preferred_element_type=jnp.float32)
    return out.reshape(rows, -1).astype(jnp.bfloat16)


def any_mesh(tokens, w_qkv, norm_gain, q_gain, k_gain, lengths):
    tensor_count = lax.axis_size("tensor")
    moved = lax.all_to_all(w_qkv, "tensor", split_axis=1, concat_axis=0, tiled=True)
    weight_cols = lax.all_gather(moved, "fsdp", axis=0, tiled=True)
    normed = head_norm(tokens.astype(jnp.float32), norm_gain).astype(jnp.bfloat16)
    qkv = jnp.dot(
        lax.all_gather(normed, "tensor", axis=0, tiled=True),
        weight_cols,
        preferred_element_type=jnp.float32,
    )
    qkv = qkv.reshape(qkv.shape[0], KV // tensor_count, GQ + 2, HD)
    return attend(qkv, q_gain, k_gain, lengths[0])


def project_kernel(counts, tile, scal, *refs):
    blocks = len(counts)
    rows_refs = refs[:blocks]
    pieces = refs[blocks : blocks + 16]
    cos_ref, sin_ref, gain_ref, out = refs[blocks + 16 : blocks + 20]
    taken, held, made, row_sems, sems, out_sems = refs[blocks + 20 :]
    depth = pieces[0].shape[0]
    columns = made.shape[1]
    steps = columns // tile

    def copies(step):
        listed = []
        for index in range(16):
            start = pl.multiple_of((scal[4 + index // 4] * 4 + scal[index % 4]) * depth, 16)
            listed.append(
                pltpu.make_async_copy(
                    pieces[index].at[:, step * tile : (step + 1) * tile],
                    held.at[step % 2, pl.ds(start, depth), :],
                    sems.at[step % 2, index],
                )
            )
        return listed

    starts = [sum(counts[:n]) for n in range(blocks)]
    row_copies = [
        pltpu.make_async_copy(ref, taken.at[first : first + rows, :], row_sems.at[number])
        for number, (ref, first, rows) in enumerate(zip(rows_refs, starts, counts))
    ]
    out_copies = []
    for copy in copies(0) + row_copies:
        copy.start()
    for step in range(steps):
        if step + 1 < steps:
            for copy in copies(step + 1):
                copy.start()
        if step == 0:
            for copy in row_copies:
                copy.wait()
        for copy in copies(step):
            copy.wait()
        total = jnp.dot(taken[...], held[step % 2], preferred_element_type=jnp.float32)
        for number, (first, rows) in enumerate(zip(starts, counts)):
            place = pl.ds(pl.multiple_of(scal[8 + number], 128), rows)
            cosine = cos_ref[place, :]
            sine = sin_ref[place, :]
            for head in range(tile // HD):
                kind = (step * (tile // HD) + head) % (GQ + 2)
                vec = total[first : first + rows, head * HD : (head + 1) * HD]
                if kind <= GQ:
                    scale = lax.rsqrt(jnp.mean(vec * vec, axis=-1, keepdims=True) + 1e-06)
                    gain = gain_ref[0:1, :] if kind < GQ else gain_ref[1:2, :]
                    vec = vec * scale * gain
                    vec = vec * cosine + pltpu.roll(vec, HD // 2, 1) * sine
                at = step * tile + head * HD
                made[first : first + rows, at : at + HD] = vec.astype(made.dtype)
        at = slice(step * tile, (step + 1) * tile)
        out_copies.append(pltpu.make_async_copy(made.at[:, at], out.at[:, at], out_sems.at[step]))
        out_copies[-1].start()
    for copy in out_copies:
        copy.wait()


def project(rows_list, places, pieces, scal, cos, sin, gains):
    counts = [r.shape[0] for r in rows_list]
    columns = pieces[0].shape[1]
    steps = 3
    tile = columns // steps
    count = sum(counts)
    width = rows_list[0].shape[1]
    scal = jnp.concatenate([scal, jnp.stack(places)]).astype(jnp.int32)
    vmem = pl.BlockSpec(memory_space=pltpu.VMEM)
    hbm = pl.BlockSpec(memory_space=pltpu.HBM)
    return pl.pallas_call(
        functools.partial(project_kernel, counts, tile),
        out_shape=pltpu.HBM((count, columns), jnp.bfloat16),
        in_specs=[pl.BlockSpec(memory_space=pltpu.SMEM)]
        + [hbm] * (len(counts) + 16)
        + [vmem] * 3,
        out_specs=hbm,
        scratch_shapes=[
            pltpu.VMEM((count, width), jnp.bfloat16),
            pltpu.VMEM((2, width, tile), jnp.bfloat16),
            pltpu.VMEM((count, columns), jnp.bfloat16),
            pltpu.SemaphoreType.DMA((len(counts),)),
            pltpu.SemaphoreType.DMA((2, 16)),
            pltpu.SemaphoreType.DMA((steps,)),
        ],
        compiler_params=pltpu.CompilerParams(vmem_limit_bytes=VMEM_BYTES),
        cost_estimate=pl.CostEstimate(
            flops=2 * count * width * columns,
            bytes_accessed=2 * (width * columns + count * (width + columns)),
            transcendentals=0,
        ),
        name="project",
    )(scal, *rows_list, *pieces, cos, sin, gains)


def attend_kernel(near_parts, far_parts, block, scal, *refs):
    near = refs[: len(near_parts)]
    far = refs[len(near_parts) : len(near_parts) + len(far_parts)]
    out, held, sems = refs[len(near_parts) + len(far_parts) :]
    middle = scal[0]
    length = scal[1]

    def fetch(sources, parts):
        copies = []
        for ref, blocks in zip(sources, parts):
            for first, rows, number in blocks:
                place = pl.ds(pl.multiple_of(scal[2 + number], 128), rows)
                copies.append(
                    pltpu.make_async_copy(
                        ref.at[first : first + rows, :], held.at[place, :], sems.at[number]
                    )
                )
        for copy in copies:
            copy.start()
        for copy in copies:
            copy.wait()

    @pl.when(middle == 1)
    def _():
        fetch(near, near_parts)

    @pl.when(middle == 0)
    def _():
        fetch(far, far_parts)

    total = held.shape[0]
    heads = held.shape[1] // ((GQ + 2) * HD)
    factor = LOG2E / float(HD) ** 0.5
    row = lax.broadcasted_iota(jnp.int32, (block, block), 0)
    col = lax.broadcasted_iota(jnp.int32, (block, block), 1)
    contract = (((1,), (1,)), ((), ()))
    for group in range(heads):
        base = group * (GQ + 2) * HD
        key_at = slice(base + GQ * HD, base + (GQ + 1) * HD)
        value_at = slice(base + (GQ + 1) * HD, base + (GQ + 2) * HD)

        @pl.loop(0, GQ)
        def _(j, base=base, key_at=key_at, value_at=value_at, group=group):
            query_at = pl.ds(pl.multiple_of(base + j * HD, HD), HD)
            out_at = pl.ds(pl.multiple_of((group * GQ + j) * HD, HD), HD)
            for step in range(total // block):
                low = step * block
                high = low + block
                query = held[low:high, query_at]
                last = lax.dot_general(
                    query, held[low:high, key_at], contract, preferred_element_type=jnp.float32
                )
                last = jnp.where((col <= row) & (col + low < length), last, -1e30)
                top = jnp.max(last, axis=-1, keepdims=True)
                if step:
                    rest = lax.dot_general(
                        query, held[:low, key_at], contract, preferred_element_type=jnp.float32
                    )
                    keys = lax.broadcasted_iota(jnp.int32, (1, low), 1)
                    rest = rest + jnp.where(keys < length, 0.0, -1e30)
                    top = jnp.maximum(top, jnp.max(rest, axis=-1, keepdims=True))
                shift = top * factor
                probs = jnp.exp2(last * factor - shift)
                norm = jnp.sum(probs, axis=-1, keepdims=True)
                value = jnp.dot(
                    probs.astype(jnp.bfloat16),
                    held[low:high, value_at],
                    preferred_element_type=jnp.float32,
                )
                if step:
                    probs = jnp.exp2(rest * factor - shift)
                    norm = norm + jnp.sum(probs, axis=-1, keepdims=True)
                    value = value + jnp.dot(
                        probs.astype(jnp.bfloat16),
                        held[:low, value_at],
                        preferred_element_type=jnp.float32,
                    )
                out[low:high, out_at] = (value / norm).astype(out.dtype)


def attend_blocks(near, far, near_parts, far_parts, places, middle, length):
    rows = sum(n.shape[0] for n in near)
    columns = near[0].shape[1]
    wide = columns // (GQ + 2) * GQ
    scal = jnp.stack([middle, length] + list(places)).astype(jnp.int32)
    hbm = pl.BlockSpec(memory_space=pltpu.HBM)
    return pl.pallas_call(
        functools.partial(attend_kernel, near_parts, far_parts, 256),
        out_shape=jax.ShapeDtypeStruct((rows, wide), jnp.bfloat16),
        in_specs=[pl.BlockSpec(memory_space=pltpu.SMEM)] + [hbm] * (len(near) + len(far)),
        out_specs=pl.BlockSpec(memory_space=pltpu.VMEM),
        scratch_shapes=[
            pltpu.VMEM((rows, columns), jnp.bfloat16),
            pltpu.SemaphoreType.DMA((len(places),)),
        ],
        compiler_params=pltpu.CompilerParams(vmem_limit_bytes=VMEM_BYTES),
        cost_estimate=pl.CostEstimate(
            flops=4 * rows * rows * wide,
            bytes_accessed=2 * rows * (columns + wide),
            transcendentals=rows * rows * wide // HD // 2,
        ),
        name="attend",
    )(scal, *near, *far)


def after(x, *earlier):
    return lax.optimization_barrier((x,) + earlier)[0]


def four_planes(tokens, w_qkv, norm_gain, q_gain, k_gain, lengths):
    t = lax.axis_index("tensor")
    f = lax.axis_index("fsdp")
    rows = tokens.shape[0]
    columns = w_qkv.shape[1] // 4
    side = t // 2
    end = 3 * side
    mid = 1 + side
    far_end = 3 * (1 - side)
    far_mid = 2 - side

    def slab(block):
        return lax.dynamic_slice(w_qkv, (0, block * columns), (w_qkv.shape[0], columns))

    def across(x, pairs):
        return lax.ppermute(x, "tensor", pairs)

    def beside(x, bit):
        return lax.ppermute(x, "fsdp", [(i, i ^ bit) for i in range(4)])

    inward = [(0, 1), (3, 2)]
    swap = [(1, 2), (2, 1)]
    far = [(0, 2), (3, 1)]
    outward = [(1, 0), (2, 3)]

    same_e, same_o, other_e, other_o = slab(end), slab(mid), slab(far_end), slab(far_mid)
    normed = head_norm(tokens.astype(jnp.float32), norm_gain).astype(jnp.bfloat16)

    swap_e = across(other_e, swap)
    far_e = across(other_e, far)
    end_e = across(same_e, inward)
    swap_o = across(after(other_o, swap_e), swap)
    rows_b = across(after(normed, swap_o), swap)
    rows_a = across(after(normed, far_e, end_e), inward)
    far_o = across(after(other_o, far_e, end_e), far)
    end_o = across(after(same_o, far_o), inward)
    rows_c = across(rows_a, swap)

    over = []
    for piece in (same_e, swap_e, far_e, end_e, same_o, swap_o, far_o, end_o):
        over.append(beside(after(piece, *over[-2:-1]), 2))

    def all_pieces(mine, theirs):
        return mine + theirs + [beside(x, 1) for x in mine] + [beside(x, 1) for x in theirs]

    end_pieces = all_pieces([same_e, swap_e, far_e, end_e], over[:4])
    mid_pieces = all_pieces([same_o, swap_o, far_o, end_o], over[4:])
    scal = jnp.stack([mid, far_mid, far_end, end] + [jnp.bitwise_xor(f, m) for m in (0, 2, 1, 3)])

    positions = jnp.arange(4 * rows, dtype=jnp.int32)
    angle = angles(positions)
    cos = jnp.concatenate([jnp.cos(angle)] * 2, axis=1)
    sin = jnp.concatenate([-jnp.sin(angle), jnp.sin(angle)], axis=1)
    gains = jnp.stack([q_gain, k_gain])

    blocks = [normed, rows_b, rows_a, rows_c]
    places = [mid * rows, far_mid * rows, end * rows, far_end * rows]

    def run(picked, pieces):
        return project(
            [blocks[i] for i in picked], [places[i] for i in picked], pieces, scal, cos, sin, gains
        )

    sent = [across(run(picked, end_pieces), outward) for picked in ([0, 1], [2, 3])]
    near = [run([0, 1, 2, 3], mid_pieces)]
    near_parts = [[(i * rows, rows, i) for i in range(4)]]
    far_parts = [[(i * rows, rows, 2 * n + i) for i in range(2)] for n in range(2)]
    middle = jnp.where((t == 1) | (t == 2), 1, 0)
    return attend_blocks(near, sent, near_parts, far_parts, places, middle, lengths[0])


def solution(mesh):
    placed = (
        P(("groups", "fsdp", "tensor"), None),
        P(("groups", "fsdp", "tensor"), None),
        P(),
        P(),
        P(),
        P(("groups", "fsdp")),
    )
    sizes = dict(mesh.shape)
    body = four_planes if sizes["tensor"] == 4 and sizes["fsdp"] == 4 else any_mesh
    return jax.shard_map(
        body,
        mesh=mesh,
        in_specs=placed,
        out_specs=P(("groups", "fsdp"), "tensor"),
        check_vma=False,
    )
```

profile of v0, /device:TPU:0, one launch (start us, length us, event | category | flops | bytes accessed | tf_op | source)
XLA Modules:
  0.0 383.8 jit_solution(9615207121267219559)
XLA Ops:
  0.0 2.6 constant_dynamic-slice_fusion
  2.6 0.0 copy-start.13
  2.6 0.7 collective-permute-start
  3.4 7.6 %collective-permute-start.3 = (bf16[320,1536]{1,0:T(8,128)(2,1)S(1)}, bf16[320,1536]{1,0:T(8,128)(2,1)S(1)}, u32[]{:S(2)}, u32[]{:S(2)}) collective-permute-start(bf16[320,1536]{1,0:T(8,128)(2,1)S(1)} %get-tuple-element.28), channel_id=1, source_target_pairs={{0,2},{3,1},{4,6},{7,5},{8,10},{11,9},{12,14},{15,13},{16,18},{19,... | collective-permute-start | bytes 2949128 | tf_op jit(solution)/shard_map/ppermute | solution.py:295
  11.0 1.6 collective-permute-start.9
  12.6 1.4 collective-permute-start.4
  14.0 0.1 collective-permute-start.25
  14.1 0.6 fusion
  14.7 0.0 copy-start.2
  14.7 0.0 copy-start.14
  14.7 0.0 copy-start.15
  14.7 0.6 collective-permute-start.17
  15.3 17.8 %collective-permute-done.3.refs_4_ = bf16[320,1536]{1,0:T(8,128)(2,1)S(1)} collective-permute-done((bf16[320,1536]{1,0:T(8,128)(2,1)S(1)}, bf16[320,1536]{1,0:T(8,128)(2,1)S(1)}, u32[]{:S(2)}, u32[]{:S(2)}) %collective-permute-start.3) | collective-permute-done | bytes 983072 | tf_op jit(solution)/shard_map/ppermute | solution.py:295
  33.1 1.5 collective-permute-start.12
  34.6 0.3 collective-permute-done.9.refs_6_
  34.9 1.5 collective-permute-start.10
  36.5 2.2 fusion.2.refs_0_
  38.7 14.1 %collective-permute-done.4.refs_5_ = bf16[320,1536]{1,0:T(8,128)(2,1)S(1)} collective-permute-done((bf16[320,1536]{1,0:T(8,128)(2,1)S(1)}, bf16[320,1536]{1,0:T(8,128)(2,1)S(1)}, u32[]{:S(2)}, u32[]{:S(2)}) %collective-permute-start.4) | collective-permute-done | bytes 983072 | tf_op jit(solution)/shard_map/ppermute | solution.py:295
  52.8 7.1 %collective-permute-start.5 = (bf16[256,5120]{1,0:T(8,128)(2,1)}, bf16[256,5120]{1,0:T(8,128)(2,1)}, u32[]{:S(2)}, u32[]{:S(2)}) collective-permute-start(bf16[256,5120]{1,0:T(8,128)(2,1)} %fusion.2.refs_0_), channel_id=1, source_target_pairs={{0,1},{3,2},{4,5},{7,6},{8,9},{11,10},{12,13},{15,14},{16,17},{19,... | collective-permute-start | bytes 7864328 | tf_op jit(solution)/shard_map/ppermute | solution.py:295
  59.9 0.0 collective-permute-start.26
  59.9 0.0 collective-permute-done.17.refs_12_
  59.9 0.7 collective-permute-start.1
  60.6 20.0 %collective-permute-start.7 = (bf16[320,1536]{1,0:T(8,128)(2,1)S(1)}, bf16[320,1536]{1,0:T(8,128)(2,1)}, u32[]{:S(2)}, u32[]{:S(2)}) collective-permute-start(bf16[320,1536]{1,0:T(8,128)(2,1)S(1)} %get-tuple-element.19), channel_id=1, source_target_pairs={{0,2},{3,1},{4,6},{7,5},{8,10},{11,9},{12,14},{15,13},{16,18},{19,... | collective-permute-start | bytes 2949128 | tf_op jit(solution)/shard_map/ppermute | solution.py:295
  80.6 1.5 collective-permute-start.13
  82.2 0.1 collective-permute-start.27
  82.3 0.5 collective-permute-start.28
  82.7 1.0 copy-done.8
  83.7 52.1 %collective-permute-done.7.refs_6_ = bf16[320,1536]{1,0:T(8,128)(2,1)} collective-permute-done((bf16[320,1536]{1,0:T(8,128)(2,1)S(1)}, bf16[320,1536]{1,0:T(8,128)(2,1)}, u32[]{:S(2)}, u32[]{:S(2)}) %collective-permute-start.7) | collective-permute-done | bytes 983072 | tf_op jit(solution)/shard_map/ppermute | solution.py:295
  135.8 0.5 collective-permute-start.31
  136.3 6.5 %collective-permute-start.8 = (bf16[320,1536]{1,0:T(8,128)(2,1)S(1)}, bf16[320,1536]{1,0:T(8,128)(2,1)}, u32[]{:S(2)}, u32[]{:S(2)}) collective-permute-start(bf16[320,1536]{1,0:T(8,128)(2,1)S(1)} %get-tuple-element.22.refs_4_), channel_id=1, source_target_pairs={{0,1},{3,2},{4,5},{7,6},{8,9},{11,10},{12,13},{15,14},{16,17},{19,... | collective-permute-start | bytes 2949128 | tf_op jit(solution)/shard_map/ppermute | solution.py:295
  142.9 1.5 collective-permute-start.11
  144.4 1.0 collective-permute-start.14
  145.4 2.1 collective-permute-start.2
  147.5 2.2 collective-permute-start.6
  149.7 13.3 %collective-permute-done.8.refs_7_ = bf16[320,1536]{1,0:T(8,128)(2,1)} collective-permute-done((bf16[320,1536]{1,0:T(8,128)(2,1)S(1)}, bf16[320,1536]{1,0:T(8,128)(2,1)}, u32[]{:S(2)}, u32[]{:S(2)}) %collective-permute-start.8) | collective-permute-done | bytes 983072 | tf_op jit(solution)/shard_map/ppermute | solution.py:295
  163.1 4.4 %collective-permute-done.11.refs_8_ = bf16[320,1536]{1,0:T(8,128)(2,1)S(1)} collective-permute-done((bf16[320,1536]{1,0:T(8,128)(2,1)S(1)}, bf16[320,1536]{1,0:T(8,128)(2,1)S(1)}, u32[]{:S(2)}, u32[]{:S(2)}) %collective-permute-start.11) | collective-permute-done | bytes 983072 | tf_op jit(solution)/shard_map/ppermute | solution.py:298
  167.5 19.9 %collective-permute-done.14.refs_9_ = bf16[320,1536]{1,0:T(8,128)(2,1)S(1)} collective-permute-done((bf16[320,1536]{1,0:T(8,128)(2,1)S(1)}, bf16[320,1536]{1,0:T(8,128)(2,1)S(1)}, u32[]{:S(2)}, u32[]{:S(2)}) %collective-permute-start.14) | collective-permute-done | bytes 983072 | tf_op jit(solution)/shard_map/ppermute | solution.py:298
  187.4 1.0 copy-done
  188.3 0.5 collective-permute-start.32
  188.8 1.5 collective-permute-start.15
  190.4 0.9 copy-done.25
  191.4 1.1 collective-permute-start.16
  192.5 0.1 concatenate.22.scal
  192.6 0.1 concatenate.21.scal
  192.8 1.9 fusion.3
  194.7 0.3 pad_maximum_fusion
  195.0 0.1 collective-permute-start.20
  195.1 18.7 %collective-permute-done.15.refs_10_ = bf16[320,1536]{1,0:T(8,128)(2,1)} collective-permute-done((bf16[320,1536]{1,0:T(8,128)(2,1)}, bf16[320,1536]{1,0:T(8,128)(2,1)}, u32[]{:S(2)}, u32[]{:S(2)}) %collective-permute-start.15) | collective-permute-done | bytes 983072 | tf_op jit(solution)/shard_map/ppermute | solution.py:298
  213.8 0.5 collective-permute-start.22
  214.3 19.7 %collective-permute-done.16.refs_11_ = bf16[320,1536]{1,0:T(8,128)(2,1)} collective-permute-done((bf16[320,1536]{1,0:T(8,128)(2,1)}, bf16[320,1536]{1,0:T(8,128)(2,1)}, u32[]{:S(2)}, u32[]{:S(2)}) %collective-permute-start.16) | collective-permute-done | bytes 983072 | tf_op jit(solution)/shard_map/ppermute | solution.py:298
  234.0 0.5 collective-permute-start.24
  234.5 17.3 %project.4 = bf16[512,1536]{1,0:T(8,128)(2,1)} custom-call(s32[10]{0:T(128)S(1)} %concatenate.21.scal, bf16[256,5120]{1,0:T(8,128)(2,1)} %fusion.2.refs_0_, bf16[256,5120]{1,0:T(8,128)(2,1)} %collective-permute-done.2.refs_1_, bf16[320,1536]{1,0:T(8,128)(2,1)S(1)} %get-tuple-element.30.refs_2_, bf16[320,1536]{1,0:T(8,128)(2,1)S(1)} %copy-done.3, ...), custom_call_target="tpu_custom_call" | custom-call | flops 8053063680 | bytes 22544384 | tf_op jit(solution)/shard_map/project/pallas_call | solution.py:146
  251.8 17.4 %project.5 = bf16[512,1536]{1,0:T(8,128)(2,1)} custom-call(s32[10]{0:T(128)S(1)} %concatenate.22.scal, bf16[256,5120]{1,0:T(8,128)(2,1)} %collective-permute-done.5.refs_2_.refs_0_, bf16[256,5120]{1,0:T(8,128)(2,1)} %collective-permute-done.6.refs_3_.refs_1_, bf16[320,1536]{1,0:T(8,128)(2,1)S(1)} %get-tuple-element.30.refs_2_, ...), custom_call_target="tpu_custom_call" | custom-call | flops 8053063680 | bytes 22544384 | tf_op jit(solution)/shard_map/project/pallas_call | solution.py:146
  269.2 1.3 collective-permute-start.33
  270.6 0.9 copy-done.30
  271.5 1.3 collective-permute-start.34
  272.8 0.1 concatenate.18.scal
  273.5 0.1 stack.65.scal
  273.7 1.2 copy-done.1
  274.8 1.2 copy-done.11
  276.0 32.5 %project.3.refs_0_ = bf16[1024,1536]{1,0:T(8,128)(2,1)} custom-call(s32[12]{0:T(128)S(1)} %concatenate.18.scal, bf16[256,5120]{1,0:T(8,128)(2,1)} %fusion.2.refs_0_, bf16[256,5120]{1,0:T(8,128)(2,1)} %collective-permute-done.2.refs_1_, bf16[256,5120]{1,0:T(8,128)(2,1)} %collective-permute-done.5.refs_2_.refs_0_, ...), custom_call_target="tpu_custom_call" | custom-call | flops 16106127360 | bytes 29360128 | tf_op jit(solution)/shard_map/project/pallas_call | solution.py:146
  308.5 23.8 %collective-permute-done.33.refs_1_ = bf16[512,1536]{1,0:T(8,128)(2,1)} collective-permute-done((bf16[512,1536]{1,0:T(8,128)(2,1)}, bf16[512,1536]{1,0:T(8,128)(2,1)}, u32[]{:S(2)}, u32[]{:S(2)}) %collective-permute-start.33) | collective-permute-done | bytes 1572896 | tf_op jit(solution)/shard_map/ppermute | solution.py:295
  332.3 33.5 %collective-permute-done.34.refs_2_ = bf16[512,1536]{1,0:T(8,128)(2,1)} collective-permute-done((bf16[512,1536]{1,0:T(8,128)(2,1)}, bf16[512,1536]{1,0:T(8,128)(2,1)}, u32[]{:S(2)}, u32[]{:S(2)}) %collective-permute-start.34) | collective-permute-done | bytes 1572896 | tf_op jit(solution)/shard_map/ppermute | solution.py:295
  365.8 17.6 %attend.1 = bf16[1024,1024]{1,0:T(8,128)(2,1)} custom-call(s32[6]{0:T(128)S(1)} %stack.65.scal, bf16[1024,1536]{1,0:T(8,128)(2,1)} %project.3.refs_0_, bf16[512,1536]{1,0:T(8,128)(2,1)} %collective-permute-done.33.refs_1_, bf16[512,1536]{1,0:T(8,128)(2,1)} %collective-permute-done.34.refs_2_), custom_call_target="tpu_custom_call" | custom-call | flops 4294967296 | bytes 5242880 | tf_op jit(solution)/shard_map/attend/pallas_call | solution.py:257
  (85 shorter events, 0.2 us)
Async XLA Ops:
  0.0 14.1 %copy-start.12 = (bf16[256,5120]{1,0:T(8,128)(2,1)S(1)}, bf16[256,5120]{1,0:T(8,128)(2,1)}, u32[]{:S(2)}) copy-start(bf16[256,5120]{1,0:T(8,128)(2,1)} %param.6) | copy-start | bytes 7864324
  2.6 33.9 %copy-start.13 = (f32[5120]{0:T(1024)S(1)}, f32[5120]{0:T(1024)}, u32[]{:S(2)}) copy-start(f32[5120]{0:T(1024)} %param.8) | copy-start | bytes 61444
  2.6 12.1 %collective-permute-start = (bf16[320,1536]{1,0:T(8,128)(2,1)S(1)}, bf16[320,1536]{1,0:T(8,128)(2,1)S(1)}, u32[]{:S(2)}, u32[]{:S(2)}) collective-permute-start(bf16[320,1536]{1,0:T(8,128)(2,1)S(1)} %get-tuple-element.28), channel_id=1, source_target_pairs={{1,2},{2,1},{5,6},{6,5},{9,10},{10,9},{13,14},{14,13},{17,18},{18,... | collective-permute-start | bytes 2949128 | tf_op jit(solution)/shard_map/ppermute | solution.py:295
  3.4 29.8 %collective-permute-start.3 = (bf16[320,1536]{1,0:T(8,128)(2,1)S(1)}, bf16[320,1536]{1,0:T(8,128)(2,1)S(1)}, u32[]{:S(2)}, u32[]{:S(2)}) collective-permute-start(bf16[320,1536]{1,0:T(8,128)(2,1)S(1)} %get-tuple-element.28), channel_id=1, source_target_pairs={{0,2},{3,1},{4,6},{7,5},{8,10},{11,9},{12,14},{15,13},{16,18},{19,... | collective-permute-start | bytes 2949128 | tf_op jit(solution)/shard_map/ppermute | solution.py:295
  11.0 23.9 %collective-permute-start.9 = (bf16[320,1536]{1,0:T(8,128)(2,1)S(1)}, bf16[320,1536]{1,0:T(8,128)(2,1)S(1)}, u32[]{:S(2)}, u32[]{:S(2)}) collective-permute-start(bf16[320,1536]{1,0:T(8,128)(2,1)S(1)} %get-tuple-element.30.refs_2_), channel_id=1, source_target_pairs={{0,8},{4,12},{8,0},{12,4},{1,9},{5,13},{9,1},{13,5},{2,10},{6,14},... | collective-permute-start | bytes 2949128 | tf_op jit(solution)/shard_map/ppermute | solution.py:298
  12.6 40.2 %collective-permute-start.4 = (bf16[320,1536]{1,0:T(8,128)(2,1)S(1)}, bf16[320,1536]{1,0:T(8,128)(2,1)S(1)}, u32[]{:S(2)}, u32[]{:S(2)}) collective-permute-start(bf16[320,1536]{1,0:T(8,128)(2,1)S(1)} %get-tuple-element.30.refs_2_), channel_id=1, source_target_pairs={{0,1},{3,2},{4,5},{7,6},{8,9},{11,10},{12,13},{15,14},{16,17},{19,... | collective-permute-start | bytes 2949128 | tf_op jit(solution)/shard_map/ppermute | solution.py:295
  14.0 45.9 %collective-permute-start.25 = (bf16[320,1536]{1,0:T(8,128)(2,1)S(1)}, bf16[320,1536]{1,0:T(8,128)(2,1)S(1)}, u32[]{:S(2)}, u32[]{:S(2)}) collective-permute-start(bf16[320,1536]{1,0:T(8,128)(2,1)S(1)} %get-tuple-element.30.refs_2_), channel_id=1, source_target_pairs={{0,4},{4,0},{8,12},{12,8},{1,5},{5,1},{9,13},{13,9},{2,6},{6,2},{1... | collective-permute-start | bytes 2949128 | tf_op jit(solution)/shard_map/ppermute | solution.py:298
  14.7 45.2 %copy-start.2 = (bf16[320,1536]{1,0:T(8,128)(2,1)}, bf16[320,1536]{1,0:T(8,128)(2,1)S(1)}, u32[]{:S(2)}) copy-start(bf16[320,1536]{1,0:T(8,128)(2,1)S(1)} %collective-permute-done.refs_3_) | copy-start | bytes 2949124
  14.7 178.0 %copy-start.14 = (f32[128]{0:T(128)S(1)}, f32[128]{0:T(128)}, u32[]{:S(2)}) copy-start(f32[128]{0:T(128)} %param.10) | copy-start | bytes 1540
  14.7 178.0 %copy-start.15 = (f32[128]{0:T(128)S(1)}, f32[128]{0:T(128)}, u32[]{:S(2)}) copy-start(f32[128]{0:T(128)} %param.9) | copy-start | bytes 1540
  14.7 45.1 %collective-permute-start.17 = (bf16[320,1536]{1,0:T(8,128)(2,1)S(1)}, bf16[320,1536]{1,0:T(8,128)(2,1)S(1)}, u32[]{:S(2)}, u32[]{:S(2)}) collective-permute-start(bf16[320,1536]{1,0:T(8,128)(2,1)S(1)} %get-tuple-element.22.refs_4_), channel_id=1, source_target_pairs={{0,4},{4,0},{8,12},{12,8},{1,5},{5,1},{9,13},{13,9},{2,6},{6,2},{1... | collective-permute-start | bytes 2949128 | tf_op jit(solution)/shard_map/ppermute | solution.py:298
  33.1 49.0 %copy-start.4 = (bf16[320,1536]{1,0:T(8,128)(2,1)}, bf16[320,1536]{1,0:T(8,128)(2,1)S(1)}, u32[]{:S(2)}) copy-start(bf16[320,1536]{1,0:T(8,128)(2,1)S(1)} %collective-permute-done.3.refs_4_) | copy-start | bytes 2949124
  33.1 27.5 %collective-permute-start.12 = (bf16[320,1536]{1,0:T(8,128)(2,1)S(1)}, bf16[320,1536]{1,0:T(8,128)(2,1)S(1)}, u32[]{:S(2)}, u32[]{:S(2)}) collective-permute-start(bf16[320,1536]{1,0:T(8,128)(2,1)S(1)} %collective-permute-done.refs_3_), channel_id=1, source_target_pairs={{0,8},{4,12},{8,0},{12,4},{1,9},{5,13},{9,1},{13,5},{2,10},{6,14},... | collective-permute-start | bytes 2949128 | tf_op jit(solution)/shard_map/ppermute | solution.py:298
  34.9 100.9 %copy-start.6 = (bf16[320,1536]{1,0:T(8,128)(2,1)}, bf16[320,1536]{1,0:T(8,128)(2,1)S(1)}, u32[]{:S(2)}) copy-start(bf16[320,1536]{1,0:T(8,128)(2,1)S(1)} %collective-permute-done.9.refs_6_) | copy-start | bytes 2949124
  34.9 45.7 %collective-permute-start.10 = (bf16[320,1536]{1,0:T(8,128)(2,1)S(1)}, bf16[320,1536]{1,0:T(8,128)(2,1)S(1)}, u32[]{:S(2)}, u32[]{:S(2)}) collective-permute-start(bf16[320,1536]{1,0:T(8,128)(2,1)S(1)} %collective-permute-done.3.refs_4_), channel_id=1, source_target_pairs={{0,8},{4,12},{8,0},{12,4},{1,9},{5,13},{9,1},{13,5},{2,10},{6,14},... | collective-permute-start | bytes 2949128 | tf_op jit(solution)/shard_map/ppermute | solution.py:298
  52.8 94.7 %collective-permute-start.5 = (bf16[256,5120]{1,0:T(8,128)(2,1)}, bf16[256,5120]{1,0:T(8,128)(2,1)}, u32[]{:S(2)}, u32[]{:S(2)}) collective-permute-start(bf16[256,5120]{1,0:T(8,128)(2,1)} %fusion.2.refs_0_), channel_id=1, source_target_pairs={{0,1},{3,2},{4,5},{7,6},{8,9},{11,10},{12,13},{15,14},{16,17},{19,... | collective-permute-start | bytes 7864328 | tf_op jit(solution)/shard_map/ppermute | solution.py:295
  59.9 130.5 %copy-start.17 = (bf16[320,1536]{1,0:T(8,128)(2,1)}, bf16[320,1536]{1,0:T(8,128)(2,1)S(1)}, u32[]{:S(2)}) copy-start(bf16[320,1536]{1,0:T(8,128)(2,1)S(1)} %collective-permute-done.25.refs_10_) | copy-start | bytes 2949124
  59.9 22.3 %collective-permute-start.26 = (bf16[320,1536]{1,0:T(8,128)(2,1)S(1)}, bf16[320,1536]{1,0:T(8,128)(2,1)S(1)}, u32[]{:S(2)}, u32[]{:S(2)}) collective-permute-start(bf16[320,1536]{1,0:T(8,128)(2,1)S(1)} %collective-permute-done.refs_3_), channel_id=1, source_target_pairs={{0,4},{4,0},{8,12},{12,8},{1,5},{5,1},{9,13},{13,9},{2,6},{6,2},{1... | collective-permute-start | bytes 2949128 | tf_op jit(solution)/shard_map/ppermute | solution.py:298
  59.9 130.5 %copy-start.16 = (bf16[320,1536]{1,0:T(8,128)(2,1)}, bf16[320,1536]{1,0:T(8,128)(2,1)S(1)}, u32[]{:S(2)}) copy-start(bf16[320,1536]{1,0:T(8,128)(2,1)S(1)} %collective-permute-done.17.refs_12_) | copy-start | bytes 2949124
  59.9 22.4 %collective-permute-start.1 = (bf16[320,1536]{1,0:T(8,128)(2,1)S(1)}, bf16[320,1536]{1,0:T(8,128)(2,1)S(1)}, u32[]{:S(2)}, u32[]{:S(2)}) collective-permute-start(bf16[320,1536]{1,0:T(8,128)(2,1)S(1)} %get-tuple-element.19), channel_id=1, source_target_pairs={{1,2},{2,1},{5,6},{6,5},{9,10},{10,9},{13,14},{14,13},{17,18},{18,... | collective-permute-start | bytes 2949128 | tf_op jit(solution)/shard_map/ppermute | solution.py:295
  60.6 129.7 %copy-start.18 = (bf16[320,1536]{1,0:T(8,128)(2,1)}, bf16[320,1536]{1,0:T(8,128)(2,1)S(1)}, u32[]{:S(2)}) copy-start(bf16[320,1536]{1,0:T(8,128)(2,1)S(1)} %collective-permute-done.12.refs_7_) | copy-start | bytes 2949124
  60.6 75.2 %collective-permute-start.7 = (bf16[320,1536]{1,0:T(8,128)(2,1)S(1)}, bf16[320,1536]{1,0:T(8,128)(2,1)}, u32[]{:S(2)}, u32[]{:S(2)}) collective-permute-start(bf16[320,1536]{1,0:T(8,128)(2,1)S(1)} %get-tuple-element.19), channel_id=1, source_target_pairs={{0,2},{3,1},{4,6},{7,5},{8,10},{11,9},{12,14},{15,13},{16,18},{19,... | collective-permute-start | bytes 2949128 | tf_op jit(solution)/shard_map/ppermute | solution.py:295
  80.6 109.7 %copy-start.19 = (bf16[320,1536]{1,0:T(8,128)(2,1)}, bf16[320,1536]{1,0:T(8,128)(2,1)S(1)}, u32[]{:S(2)}) copy-start(bf16[320,1536]{1,0:T(8,128)(2,1)S(1)} %collective-permute-done.10.refs_8_) | copy-start | bytes 2949124
  80.6 55.2 %collective-permute-start.13 = (bf16[320,1536]{1,0:T(8,128)(2,1)S(1)}, bf16[320,1536]{1,0:T(8,128)(2,1)}, u32[]{:S(2)}, u32[]{:S(2)}) collective-permute-start(bf16[320,1536]{1,0:T(8,128)(2,1)S(1)} %collective-permute-done.4.refs_5_), channel_id=1, source_target_pairs={{0,8},{4,12},{8,0},{12,4},{1,9},{5,13},{9,1},{13,5},{2,10},{6,14},... | collective-permute-start | bytes 2949128 | tf_op jit(solution)/shard_map/ppermute | solution.py:298
  82.2 108.2 %copy-start.20 = (bf16[320,1536]{1,0:T(8,128)(2,1)}, bf16[320,1536]{1,0:T(8,128)(2,1)S(1)}, u32[]{:S(2)}) copy-start(bf16[320,1536]{1,0:T(8,128)(2,1)S(1)} %collective-permute-done.26.refs_11_) | copy-start | bytes 2949124
  82.2 54.1 %collective-permute-start.27 = (bf16[320,1536]{1,0:T(8,128)(2,1)S(1)}, bf16[320,1536]{1,0:T(8,128)(2,1)S(1)}, u32[]{:S(2)}, u32[]{:S(2)}) collective-permute-start(bf16[320,1536]{1,0:T(8,128)(2,1)S(1)} %collective-permute-done.3.refs_4_), channel_id=1, source_target_pairs={{0,4},{4,0},{8,12},{12,8},{1,5},{5,1},{9,13},{13,9},{2,6},{6,2},{1... | collective-permute-start | bytes 2949128 | tf_op jit(solution)/shard_map/ppermute | solution.py:298
  82.3 60.6 %collective-permute-start.28 = (bf16[320,1536]{1,0:T(8,128)(2,1)S(1)}, bf16[320,1536]{1,0:T(8,128)(2,1)S(1)}, u32[]{:S(2)}, u32[]{:S(2)}) collective-permute-start(bf16[320,1536]{1,0:T(8,128)(2,1)S(1)} %collective-permute-done.4.refs_5_), channel_id=1, source_target_pairs={{0,4},{4,0},{8,12},{12,8},{1,5},{5,1},{9,13},{13,9},{2,6},{6,2},{1... | collective-permute-start | bytes 2949128 | tf_op jit(solution)/shard_map/ppermute | solution.py:298
  135.8 8.6 %collective-permute-start.29 = (bf16[320,1536]{1,0:T(8,128)(2,1)S(1)}, bf16[320,1536]{1,0:T(8,128)(2,1)S(1)}, u32[]{:S(2)}, u32[]{:S(2)}) collective-permute-start(bf16[320,1536]{1,0:T(8,128)(2,1)S(1)} %collective-permute-done.9.refs_6_), channel_id=1, source_target_pairs={{0,4},{4,0},{8,12},{12,8},{1,5},{5,1},{9,13},{13,9},{2,6},{6,2},{1... | collective-permute-start | bytes 2949128 | tf_op jit(solution)/shard_map/ppermute | solution.py:298
  135.8 9.6 %collective-permute-start.31 = (bf16[320,1536]{1,0:T(8,128)(2,1)S(1)}, bf16[320,1536]{1,0:T(8,128)(2,1)S(1)}, u32[]{:S(2)}, u32[]{:S(2)}) collective-permute-start(bf16[320,1536]{1,0:T(8,128)(2,1)S(1)} %collective-permute-done.10.refs_8_), channel_id=1, source_target_pairs={{0,4},{4,0},{8,12},{12,8},{1,5},{5,1},{9,13},{13,9},{2,6},{6,2},{1... | collective-permute-start | bytes 2949128 | tf_op jit(solution)/shard_map/ppermute | solution.py:298
  136.3 6.5 %copy-start.22 = (bf16[320,1536]{1,0:T(8,128)(2,1)}, bf16[320,1536]{1,0:T(8,128)(2,1)S(1)}, u32[]{:S(2)}) copy-start(bf16[320,1536]{1,0:T(8,128)(2,1)S(1)} %collective-permute-done.27.refs_12_) | copy-start | bytes 2949124
  136.3 26.7 %collective-permute-start.8 = (bf16[320,1536]{1,0:T(8,128)(2,1)S(1)}, bf16[320,1536]{1,0:T(8,128)(2,1)}, u32[]{:S(2)}, u32[]{:S(2)}) collective-permute-start(bf16[320,1536]{1,0:T(8,128)(2,1)S(1)} %get-tuple-element.22.refs_4_), channel_id=1, source_target_pairs={{0,1},{3,2},{4,5},{7,6},{8,9},{11,10},{12,13},{15,14},{16,17},{19,... | collective-permute-start | bytes 2949128 | tf_op jit(solution)/shard_map/ppermute | solution.py:295
  142.9 1.5 copy-start.24
  142.9 24.7 %collective-permute-start.11 = (bf16[320,1536]{1,0:T(8,128)(2,1)S(1)}, bf16[320,1536]{1,0:T(8,128)(2,1)S(1)}, u32[]{:S(2)}, u32[]{:S(2)}) collective-permute-start(bf16[320,1536]{1,0:T(8,128)(2,1)S(1)} %get-tuple-element.22.refs_4_), channel_id=1, source_target_pairs={{0,8},{4,12},{8,0},{12,4},{1,9},{5,13},{9,1},{13,5},{2,10},{6,14},... | collective-permute-start | bytes 2949128 | tf_op jit(solution)/shard_map/ppermute | solution.py:298
  144.4 18.7 %copy-start.26 = (bf16[320,1536]{1,0:T(8,128)(2,1)}, bf16[320,1536]{1,0:T(8,128)(2,1)S(1)}, u32[]{:S(2)}) copy-start(bf16[320,1536]{1,0:T(8,128)(2,1)S(1)} %collective-permute-done.29.refs_14_) | copy-start | bytes 2949124
  144.4 43.0 %collective-permute-start.14 = (bf16[320,1536]{1,0:T(8,128)(2,1)S(1)}, bf16[320,1536]{1,0:T(8,128)(2,1)S(1)}, u32[]{:S(2)}, u32[]{:S(2)}) collective-permute-start(bf16[320,1536]{1,0:T(8,128)(2,1)S(1)} %collective-permute-done.1.refs_5_), channel_id=1, source_target_pairs={{0,8},{4,12},{8,0},{12,4},{1,9},{5,13},{9,1},{13,5},{2,10},{6,14},... | collective-permute-start | bytes 2949128 | tf_op jit(solution)/shard_map/ppermute | solution.py:298
  145.4 22.1 %copy-start.27 = (bf16[320,1536]{1,0:T(8,128)(2,1)}, bf16[320,1536]{1,0:T(8,128)(2,1)S(1)}, u32[]{:S(2)}) copy-start(bf16[320,1536]{1,0:T(8,128)(2,1)S(1)} %collective-permute-done.31.refs_16_) | copy-start | bytes 2949124
  145.4 68.4 %collective-permute-start.2 = (bf16[256,5120]{1,0:T(8,128)(2,1)}, bf16[256,5120]{1,0:T(8,128)(2,1)}, u32[]{:S(2)}, u32[]{:S(2)}) collective-permute-start(bf16[256,5120]{1,0:T(8,128)(2,1)} %fusion.2.refs_0_), channel_id=1, source_target_pairs={{1,2},{2,1},{5,6},{6,5},{9,10},{10,9},{13,14},{14,13},{17,18},{18,... | collective-permute-start | bytes 7864328 | tf_op jit(solution)/shard_map/ppermute | solution.py:295
  147.5 86.5 %collective-permute-start.6 = (bf16[256,5120]{1,0:T(8,128)(2,1)}, bf16[256,5120]{1,0:T(8,128)(2,1)}, u32[]{:S(2)}, u32[]{:S(2)}) collective-permute-start(bf16[256,5120]{1,0:T(8,128)(2,1)} %collective-permute-done.5.refs_2_.refs_0_), channel_id=1, source_target_pairs={{1,2},{2,1},{5,6},{6,5},{9,10},{10,9},{13,14},{14,13},{17,18},{18,... | collective-permute-start | bytes 7864328 | tf_op jit(solution)/shard_map/ppermute | solution.py:295
  163.1 25.3 %collective-permute-start.30 = (bf16[320,1536]{1,0:T(8,128)(2,1)S(1)}, bf16[320,1536]{1,0:T(8,128)(2,1)S(1)}, u32[]{:S(2)}, u32[]{:S(2)}) collective-permute-start(bf16[320,1536]{1,0:T(8,128)(2,1)S(1)} %collective-permute-done.12.refs_7_), channel_id=1, source_target_pairs={{0,4},{4,0},{8,12},{12,8},{1,5},{5,1},{9,13},{13,9},{2,6},{6,2},{1... | collective-permute-start | bytes 2949128 | tf_op jit(solution)/shard_map/ppermute | solution.py:298
  167.5 22.9 %copy-start.10 = (bf16[320,1536]{1,0:T(8,128)(2,1)}, bf16[320,1536]{1,0:T(8,128)(2,1)S(1)}, u32[]{:S(2)}) copy-start(bf16[320,1536]{1,0:T(8,128)(2,1)S(1)} %collective-permute-done.11.refs_8_) | copy-start | bytes 2949124
  167.5 21.3 %collective-permute-start.19 = (bf16[320,1536]{1,0:T(8,128)(2,1)}, bf16[320,1536]{1,0:T(8,128)(2,1)S(1)}, u32[]{:S(2)}, u32[]{:S(2)}) collective-permute-start(bf16[320,1536]{1,0:T(8,128)(2,1)} %collective-permute-done.7.refs_6_), channel_id=1, source_target_pairs={{0,4},{4,0},{8,12},{12,8},{1,5},{5,1},{9,13},{13,9},{2,6},{6,2},{1... | collective-permute-start | bytes 2949128 | tf_op jit(solution)/shard_map/ppermute | solution.py:298
  187.4 3.0 copy-start.21
  187.4 3.0 collective-permute-start.18
  187.4 1.0 copy-start
  188.3 2.1 copy-start.28
  188.3 6.7 %collective-permute-start.32 = (bf16[320,1536]{1,0:T(8,128)(2,1)}, bf16[320,1536]{1,0:T(8,128)(2,1)}, u32[]{:S(2)}, u32[]{:S(2)}) collective-permute-start(bf16[320,1536]{1,0:T(8,128)(2,1)} %collective-permute-done.13.refs_9_), channel_id=1, source_target_pairs={{0,4},{4,0},{8,12},{12,8},{1,5},{5,1},{9,13},{13,9},{2,6},{6,2},{1... | collective-permute-start | bytes 2949128 | tf_op jit(solution)/shard_map/ppermute | solution.py:298
  188.8 1.6 copy-start.23
  188.8 24.9 %collective-permute-start.15 = (bf16[320,1536]{1,0:T(8,128)(2,1)}, bf16[320,1536]{1,0:T(8,128)(2,1)}, u32[]{:S(2)}, u32[]{:S(2)}) collective-permute-start(bf16[320,1536]{1,0:T(8,128)(2,1)} %collective-permute-done.7.refs_6_), channel_id=1, source_target_pairs={{0,8},{4,12},{8,0},{12,4},{1,9},{5,13},{9,1},{13,5},{2,10},{6,14},... | collective-permute-start | bytes 2949128 | tf_op jit(solution)/shard_map/ppermute | solution.py:298
  191.4 42.6 %collective-permute-start.16 = (bf16[320,1536]{1,0:T(8,128)(2,1)}, bf16[320,1536]{1,0:T(8,128)(2,1)}, u32[]{:S(2)}, u32[]{:S(2)}) collective-permute-start(bf16[320,1536]{1,0:T(8,128)(2,1)} %collective-permute-done.8.refs_7_), channel_id=1, source_target_pairs={{0,8},{4,12},{8,0},{12,4},{1,9},{5,13},{9,1},{13,5},{2,10},{6,14},... | collective-permute-start | bytes 2949128 | tf_op jit(solution)/shard_map/ppermute | solution.py:298
  192.7 41.8 %copy-start.3 = (bf16[320,1536]{1,0:T(8,128)(2,1)S(1)}, bf16[320,1536]{1,0:T(8,128)(2,1)}, u32[]{:S(2)}) copy-start(bf16[320,1536]{1,0:T(8,128)(2,1)} %copy-done.2) | copy-start | bytes 2949124
  192.7 41.8 %copy-start.5 = (bf16[320,1536]{1,0:T(8,128)(2,1)S(1)}, bf16[320,1536]{1,0:T(8,128)(2,1)}, u32[]{:S(2)}) copy-start(bf16[320,1536]{1,0:T(8,128)(2,1)} %copy-done.4) | copy-start | bytes 2949124
  192.7 41.8 %copy-start.7 = (bf16[320,1536]{1,0:T(8,128)(2,1)S(1)}, bf16[320,1536]{1,0:T(8,128)(2,1)}, u32[]{:S(2)}) copy-start(bf16[320,1536]{1,0:T(8,128)(2,1)} %copy-done.6) | copy-start | bytes 2949124
  192.7 41.8 %copy-start.9 = (bf16[320,1536]{1,0:T(8,128)(2,1)S(1)}, bf16[320,1536]{1,0:T(8,128)(2,1)}, u32[]{:S(2)}) copy-start(bf16[320,1536]{1,0:T(8,128)(2,1)} %copy-done.8) | copy-start | bytes 2949124
  195.0 74.2 %collective-permute-start.20 = (bf16[320,1536]{1,0:T(8,128)(2,1)}, bf16[320,1536]{1,0:T(8,128)(2,1)S(1)}, u32[]{:S(2)}, u32[]{:S(2)}) collective-permute-start(bf16[320,1536]{1,0:T(8,128)(2,1)} %collective-permute-done.8.refs_7_), channel_id=1, source_target_pairs={{0,4},{4,0},{8,12},{12,8},{1,5},{5,1},{9,13},{13,9},{2,6},{6,2},{1... | collective-permute-start | bytes 2949128 | tf_op jit(solution)/shard_map/ppermute | solution.py:298
  213.8 56.8 %collective-permute-start.21 = (bf16[320,1536]{1,0:T(8,128)(2,1)}, bf16[320,1536]{1,0:T(8,128)(2,1)S(1)}, u32[]{:S(2)}, u32[]{:S(2)}) collective-permute-start(bf16[320,1536]{1,0:T(8,128)(2,1)} %copy-done.10), channel_id=1, source_target_pairs={{0,4},{4,0},{8,12},{12,8},{1,5},{5,1},{9,13},{13,9},{2,6},{6,2},{1... | collective-permute-start | bytes 2949128 | tf_op jit(solution)/shard_map/ppermute | solution.py:298
  213.8 59.9 %collective-permute-start.22 = (bf16[320,1536]{1,0:T(8,128)(2,1)}, bf16[320,1536]{1,0:T(8,128)(2,1)}, u32[]{:S(2)}, u32[]{:S(2)}) collective-permute-start(bf16[320,1536]{1,0:T(8,128)(2,1)} %copy-done.21), channel_id=1, source_target_pairs={{0,4},{4,0},{8,12},{12,8},{1,5},{5,1},{9,13},{13,9},{2,6},{6,2},{1... | collective-permute-start | bytes 2949128 | tf_op jit(solution)/shard_map/ppermute | solution.py:298
  234.0 39.7 %collective-permute-start.23 = (bf16[320,1536]{1,0:T(8,128)(2,1)}, bf16[320,1536]{1,0:T(8,128)(2,1)}, u32[]{:S(2)}, u32[]{:S(2)}) collective-permute-start(bf16[320,1536]{1,0:T(8,128)(2,1)} %collective-permute-done.15.refs_10_), channel_id=1, source_target_pairs={{0,4},{4,0},{8,12},{12,8},{1,5},{5,1},{9,13},{13,9},{2,6},{6,2},{1... | collective-permute-start | bytes 2949128 | tf_op jit(solution)/shard_map/ppermute | solution.py:298
  234.0 39.7 %collective-permute-start.24 = (bf16[320,1536]{1,0:T(8,128)(2,1)}, bf16[320,1536]{1,0:T(8,128)(2,1)}, u32[]{:S(2)}, u32[]{:S(2)}) collective-permute-start(bf16[320,1536]{1,0:T(8,128)(2,1)} %collective-permute-done.16.refs_11_), channel_id=1, source_target_pairs={{0,4},{4,0},{8,12},{12,8},{1,5},{5,1},{9,13},{13,9},{2,6},{6,2},{1... | collective-permute-start | bytes 2949128 | tf_op jit(solution)/shard_map/ppermute | solution.py:298
  269.2 1.3 copy-start.29
  269.2 63.1 %collective-permute-start.33 = (bf16[512,1536]{1,0:T(8,128)(2,1)}, bf16[512,1536]{1,0:T(8,128)(2,1)}, u32[]{:S(2)}, u32[]{:S(2)}) collective-permute-start(bf16[512,1536]{1,0:T(8,128)(2,1)} %project.4), channel_id=1, source_target_pairs={{1,0},{2,3},{5,4},{6,7},{9,8},{10,11},{13,12},{14,15},{17,16},{18,... | collective-permute-start | bytes 4718600 | tf_op jit(solution)/shard_map/ppermute | solution.py:295
  270.5 1.0 copy-start.30
  271.5 94.3 %collective-permute-start.34 = (bf16[512,1536]{1,0:T(8,128)(2,1)}, bf16[512,1536]{1,0:T(8,128)(2,1)}, u32[]{:S(2)}, u32[]{:S(2)}) collective-permute-start(bf16[512,1536]{1,0:T(8,128)(2,1)} %project.5), channel_id=1, source_target_pairs={{1,0},{2,3},{5,4},{6,7},{9,8},{10,11},{13,12},{14,15},{17,16},{18,... | collective-permute-start | bytes 4718600 | tf_op jit(solution)/shard_map/ppermute | solution.py:295
  273.6 1.2 copy-start.1
  274.8 1.2 copy-start.11
  (2 other events, 1.9 us)
where the time goes:
time: 390 us; the launch traced here: 384 us
  waiting for transfers between devices  218 us (56%)
  Pallas kernels  84.7 us (22%)
  starting transfers between devices  65.5 us (17%)
  local copies, waits for them, and re-layouts  9.26 us (2%)
  other arithmetic  5.1 us (1%)
    ppermute x11, waiting for transfers between devices, across(): return lax.ppermute(x, 'tensor', pairs)  155 us
    pallas_call x3, Pallas kernels, project(): pl.pallas_call(functools.partial(project_kernel, counts, tile), out_shape...  67.2 us
    ppermute x24, waiting for transfers between devices, beside(): return lax.ppermute(x, 'fsdp', [(i, i ^ bit) for i in range(4)])  63 us
    ppermute x11, starting transfers between devices, across(): return lax.ppermute(x, 'tensor', pairs)  51 us
    pallas_call x1, Pallas kernels, attend_blocks(): pl.pallas_call(functools.partial(attend_kernel, near_parts, far_parts, 25...  17.6 us
    ppermute x24, starting transfers between devices, beside(): return lax.ppermute(x, 'fsdp', [(i, i ^ bit) for i in range(4)])  14.5 us
  transfers between devices with their start and end apart: 35, of which 11 were waited for; matrix products, arithmetic and copies ran while one was open for 1% of the time, Pallas kernels for 17%

commit v1 on v0

--- a/solution.py
+++ b/solution.py
@@ -71,23 +71,24 @@
     return attend(qkv, q_gain, k_gain, lengths[0])
 
 
-def project_kernel(counts, tile, scal, *refs):
+def project_kernel(counts, sources, tile, scal, *refs):
     blocks = len(counts)
+    arrays = max(source[0] for source in sources) + 1
     rows_refs = refs[:blocks]
-    pieces = refs[blocks : blocks + 16]
-    cos_ref, sin_ref, gain_ref, out = refs[blocks + 16 : blocks + 20]
-    taken, held, made, row_sems, sems, out_sems = refs[blocks + 20 :]
-    depth = pieces[0].shape[0]
+    pieces = refs[blocks : blocks + arrays]
+    cos_ref, sin_ref, gain_ref, out = refs[blocks + arrays : blocks + arrays + 4]
+    taken, held, made, row_sems, sems, out_sems = refs[blocks + arrays + 4 :]
+    depth = taken.shape[1] // 16
     columns = made.shape[1]
     steps = columns // tile
 
     def copies(step):
         listed = []
-        for index in range(16):
-            start = pl.multiple_of((scal[4 + index // 4] * 4 + scal[index % 4]) * depth, 16)
+        for index, (array, first, group, slot) in enumerate(sources):
+            start = pl.multiple_of((scal[group] * 4 + scal[slot]) * depth, 16)
             listed.append(
                 pltpu.make_async_copy(
-                    pieces[index].at[:, step * tile : (step + 1) * tile],
+                    pieces[array].at[first : first + depth, step * tile : (step + 1) * tile],
                     held.at[step % 2, pl.ds(start, depth), :],
                     sems.at[step % 2, index],
                 )
@@ -113,7 +114,7 @@
             copy.wait()
         total = jnp.dot(taken[...], held[step % 2], preferred_element_type=jnp.float32)
         for number, (first, rows) in enumerate(zip(starts, counts)):
-            place = pl.ds(pl.multiple_of(scal[8 + number], 128), rows)
+            place = pl.ds(pl.multiple_of(scal[12 + number], 128), rows)
             cosine = cos_ref[place, :]
             sine = sin_ref[place, :]
             for head in range(tile // HD):
@@ -133,7 +134,15 @@
         copy.wait()
 
 
-def project(rows_list, places, pieces, scal, cos, sin, gains):
+def project(rows_list, places, spread_pieces, own_pieces, scal, cos, sin, gains):
+    pieces, sources = [], []
+    depth = rows_list[0].shape[1] // 16
+    for slot, array in spread_pieces:
+        sources += [(len(pieces), m * depth, 8 + m, slot) for m in range(4)]
+        pieces.append(array)
+    for slot, four in own_pieces:
+        sources += [(len(pieces) + m, 0, 4 + m, slot) for m in range(4)]
+        pieces += four
     counts = [r.shape[0] for r in rows_list]
     columns = pieces[0].shape[1]
     steps = 3
@@ -144,10 +153,10 @@
     vmem = pl.BlockSpec(memory_space=pltpu.VMEM)
     hbm = pl.BlockSpec(memory_space=pltpu.HBM)
     return pl.pallas_call(
-        functools.partial(project_kernel, counts, tile),
+        functools.partial(project_kernel, counts, sources, tile),
         out_shape=pltpu.HBM((count, columns), jnp.bfloat16),
         in_specs=[pl.BlockSpec(memory_space=pltpu.SMEM)]
-        + [hbm] * (len(counts) + 16)
+        + [hbm] * (len(counts) + len(pieces))
         + [vmem] * 3,
         out_specs=hbm,
         scratch_shapes=[
@@ -297,6 +306,9 @@
     def beside(x, bit):
         return lax.ppermute(x, "fsdp", [(i, i ^ bit) for i in range(4)])
 
+    def spread(x):
+        return lax.all_gather(x, "fsdp", axis=0, tiled=True)
+
     inward = [(0, 1), (3, 2)]
     swap = [(1, 2), (2, 1)]
     far = [(0, 2), (3, 1)]
@@ -305,26 +317,45 @@
     same_e, same_o, other_e, other_o = slab(end), slab(mid), slab(far_end), slab(far_mid)
     normed = head_norm(tokens.astype(jnp.float32), norm_gain).astype(jnp.bfloat16)
 
+    def core_pair(piece, over):
+        return [piece, over, beside(piece, 1), beside(over, 1)]
+
+    own_e, own_o = spread(same_e), spread(same_o)
     swap_e = across(other_e, swap)
     far_e = across(other_e, far)
     end_e = across(same_e, inward)
-    swap_o = across(after(other_o, swap_e), swap)
-    rows_b = across(after(normed, swap_o), swap)
-    rows_a = across(after(normed, far_e, end_e), inward)
-    far_o = across(after(other_o, far_e, end_e), far)
-    end_o = across(after(same_o, far_o), inward)
-    rows_c = across(rows_a, swap)
-
-    over = []
-    for piece in (same_e, swap_e, far_e, end_e, same_o, swap_o, far_o, end_o):
-        over.append(beside(after(piece, *over[-2:-1]), 2))
-
-    def all_pieces(mine, theirs):
-        return mine + theirs + [beside(x, 1) for x in mine] + [beside(x, 1) for x in theirs]
-
-    end_pieces = all_pieces([same_e, swap_e, far_e, end_e], over[:4])
-    mid_pieces = all_pieces([same_o, swap_o, far_o, end_o], over[4:])
-    scal = jnp.stack([mid, far_mid, far_end, end] + [jnp.bitwise_xor(f, m) for m in (0, 2, 1, 3)])
+    swap_o = across(other_o, swap)
+    swap_e, far_e, end_e, swap_o = lax.optimization_barrier((swap_e, far_e, end_e, swap_o))
+    far_o = across(after(other_o, swap_e), far)
+    end_o = across(after(same_o, swap_e), inward)
+    over_swap_e = beside(swap_e, 2)
+    over_far_e = beside(far_e, 2)
+    far_o, end_o, over_swap_e, over_far_e = lax.optimization_barrier(
+        (far_o, end_o, over_swap_e, over_far_e)
+    )
+    rows_a = across(after(normed, far_o), inward)
+    rows_b = across(after(normed, far_o), swap)
+    over_end_e = beside(after(end_e, far_o), 2)
+    over_swap_o = beside(after(swap_o, over_end_e), 2)
+    rows_c = across(after(rows_a, over_swap_o), swap)
+
+    end_pieces = (
+        [(0, own_e)],
+        [
+            (1, core_pair(swap_e, over_swap_e)),
+            (2, core_pair(far_e, over_far_e)),
+            (3, core_pair(end_e, over_end_e)),
+        ],
+    )
+    mid_pieces = (
+        [(0, own_o), (2, spread(far_o)), (3, spread(end_o))],
+        [(1, core_pair(swap_o, over_swap_o))],
+    )
+    scal = jnp.stack(
+        [mid, far_mid, far_end, end]
+        + [jnp.bitwise_xor(f, m) for m in (0, 2, 1, 3)]
+        + [jnp.int32(m) for m in range(4)]
+    )
 
     positions = jnp.arange(4 * rows, dtype=jnp.int32)
     angle = angles(positions)
@@ -337,7 +368,7 @@
 
     def run(picked, pieces):
         return project(
-            [blocks[i] for i in picked], [places[i] for i in picked], pieces, scal, cos, sin, gains
+            [blocks[i] for i in picked], [places[i] for i in picked], *pieces, scal, cos, sin, gains
         )
 
     sent = [across(run(picked, end_pieces), outward) for picked in ([0, 1], [2, 3])]

time: 390 us -> 373 us (0.956)
  the two profiles are of different devices: /device:TPU:0 before, /device:TPU:14 now
where the time goes in v1:
time: 373 us; the launch traced here: 369 us
  waiting for transfers between devices  222 us (60%)
  Pallas kernels  86.5 us (23%)
  starting transfers between devices  29.4 us (8%)
  between operations  14.4 us (4%)
  local copies, waits for them, and re-layouts  9.76 us (3%)
  other arithmetic  6.99 us (2%)
    ppermute x11, waiting for transfers between devices, across(): return lax.ppermute(x, 'tensor', pairs)  151 us
    ppermute x12, waiting for transfers between devices, beside(): return lax.ppermute(x, 'fsdp', [(i, i ^ bit) for i in range(4)])  70.5 us
    pallas_call x3, Pallas kernels, project(): pl.pallas_call(functools.partial(project_kernel, counts, sources, tile),...  69 us
    ppermute x11, starting transfers between devices, across(): return lax.ppermute(x, 'tensor', pairs)  22.1 us
    pallas_call x1, Pallas kernels, attend_blocks(): pl.pallas_call(functools.partial(attend_kernel, near_parts, far_parts, 25...  17.6 us
  transfers between devices with their start and end apart: 27, of which 10 were waited for; matrix products, arithmetic and copies ran while one was open for 2% of the time, Pallas kernels for 19%

profile of v1, /device:TPU:14, one launch (start us, length us, event | category | flops | bytes accessed | tf_op | source)
XLA Modules:
  0.0 369.5 jit_solution(3136387212750221138)
XLA Ops:
  6.5 3.8 %constant_dynamic-slice_fusion = (bf16[320,1536]{1,0:T(8,128)(2,1)}, bf16[320,1536]{1,0:T(8,128)(2,1)}, bf16[320,1536]{1,0:T(8,128)(2,1)S(1)}, bf16[320,1536]{1,0:T(8,128)(2,1)}) fusion(bf16[320,6144]{1,0:T(8,128)(2,1)} %param.7, s32[]{:T(128)S(6)} %select_n.26, s32[]{:T(128)S(6)} %select_n.24, s32[]{:T(128)S(6)} %select_n.23, s32[]{:T(128)S(6)} %select_n.25), kind=kLoop, calls=%fused_computation.13 | loop fusion | bytes 7864336 | tf_op jit(solution)/shard_map/dynamic_slice | solution.py:301
  10.3 0.0 all-gather.11.cloned.1.call-update
  10.4 0.0 all-gather.5.cloned.1.call-start
  10.4 0.7 all-gather.5.cloned.1.call-update
  11.1 0.0 all-gather.7.cloned.1.call-start
  11.2 3.5 collective-permute-start
  14.7 1.3 collective-permute-start.1
  16.0 1.3 collective-permute-start.2
  17.3 2.4 collective-permute-start.3
  19.6 39.4 %collective-permute-done.refs_3_ = bf16[320,1536]{1,0:T(8,128)(2,1)S(1)} collective-permute-done((bf16[320,1536]{1,0:T(8,128)(2,1)}, bf16[320,1536]{1,0:T(8,128)(2,1)S(1)}, u32[]{:S(2)}, u32[]{:S(2)}) %collective-permute-start) | collective-permute-done | bytes 983072 | tf_op jit(solution)/shard_map/ppermute | solution.py:304
  59.0 0.0 collective-permute-done.1.refs_7_
  59.0 2.0 collective-permute-done.2.refs_11_
  61.0 18.0 %collective-permute-done.3.refs_7_ = bf16[320,1536]{1,0:T(8,128)(2,1)} collective-permute-done((bf16[320,1536]{1,0:T(8,128)(2,1)S(1)}, bf16[320,1536]{1,0:T(8,128)(2,1)}, u32[]{:S(2)}, u32[]{:S(2)}) %collective-permute-start.3) | collective-permute-done | bytes 983072 | tf_op jit(solution)/shard_map/ppermute | solution.py:304
  79.0 0.5 collective-permute-start.6
  79.5 1.3 collective-permute-start.5
  80.8 1.3 collective-permute-start.4
  82.1 1.6 collective-permute-start.7
  83.7 22.6 %collective-permute-done.5 = bf16[320,1536]{1,0:T(8,128)(2,1)S(1)} collective-permute-done((bf16[320,1536]{1,0:T(8,128)(2,1)}, bf16[320,1536]{1,0:T(8,128)(2,1)S(1)}, u32[]{:S(2)}, u32[]{:S(2)}) %collective-permute-start.5) | collective-permute-done | bytes 983072 | tf_op jit(solution)/shard_map/ppermute | solution.py:304
  106.3 19.8 %collective-permute-done.4 = bf16[320,1536]{1,0:T(8,128)(2,1)} collective-permute-done((bf16[320,1536]{1,0:T(8,128)(2,1)}, bf16[320,1536]{1,0:T(8,128)(2,1)}, u32[]{:S(2)}, u32[]{:S(2)}) %collective-permute-start.4) | collective-permute-done | bytes 983072 | tf_op jit(solution)/shard_map/ppermute | solution.py:304
  126.1 0.0 all-gather.7.cloned.1.call-update
  126.2 0.0 all-gather.9.cloned.1.call-start
  126.2 0.0 copy-start.7
  126.2 2.5 fusion
  128.7 0.0 copy-done.7
  128.7 0.0 copy-start.12
  128.8 2.2 fusion.2.refs_0_
  131.0 1.3 collective-permute-start.9
  132.3 0.0 all-gather.9.cloned.1.call-update
  132.3 1.6 collective-permute-start.10
  133.9 42.5 %collective-permute-done.10.refs_12_ = bf16[320,1536]{1,0:T(8,128)(2,1)} collective-permute-done((bf16[320,1536]{1,0:T(8,128)(2,1)}, bf16[320,1536]{1,0:T(8,128)(2,1)}, u32[]{:S(2)}, u32[]{:S(2)}) %collective-permute-start.10) | collective-permute-done | bytes 983072 | tf_op jit(solution)/shard_map/ppermute | solution.py:307
  176.4 1.5 collective-permute-start.11
  177.9 3.1 collective-permute-start.8
  181.0 0.1 collective-permute-start.15
  181.1 0.5 collective-permute-start.17
  181.6 27.0 %collective-permute-done.11.refs_8_ = bf16[320,1536]{1,0:T(8,128)(2,1)} collective-permute-done((bf16[320,1536]{1,0:T(8,128)(2,1)}, bf16[320,1536]{1,0:T(8,128)(2,1)}, u32[]{:S(2)}, u32[]{:S(2)}) %collective-permute-start.11) | collective-permute-done | bytes 983072 | tf_op jit(solution)/shard_map/ppermute | solution.py:307
  208.6 2.6 collective-permute-start.12
  211.2 1.0 copy-done.4
  212.2 0.4 collective-permute-start.16
  212.6 1.0 copy-done.14
  213.5 0.1 collective-permute-start.18
  213.7 0.4 collective-permute-start.20
  214.0 0.1 concatenate.22.scal
  214.1 0.1 concatenate.21.scal
  214.3 1.9 fusion.3
  216.2 0.3 pad_maximum_fusion
  216.5 0.2 collective-permute-start.13
  216.8 0.4 collective-permute-start.14
  217.1 1.0 collective-permute-done.20.refs_14_
  218.1 21.9 %collective-permute-done.8.refs_1_ = bf16[256,5120]{1,0:T(8,128)(2,1)} collective-permute-done((bf16[256,5120]{1,0:T(8,128)(2,1)}, bf16[256,5120]{1,0:T(8,128)(2,1)}, u32[]{:S(2)}, u32[]{:S(2)}) %collective-permute-start.8) | collective-permute-done | bytes 2621472 | tf_op jit(solution)/shard_map/ppermute | solution.py:304
  240.0 1.2 copy-done.5
  241.2 17.4 %project.4 = bf16[512,1536]{1,0:T(8,128)(2,1)} custom-call(s32[14]{0:T(128)S(1)} %concatenate.21.scal, bf16[256,5120]{1,0:T(8,128)(2,1)} %fusion.2.refs_0_, bf16[256,5120]{1,0:T(8,128)(2,1)} %collective-permute-done.8.refs_1_, bf16[1280,1536]{1,0:T(8,128)(2,1)} %all-gather.11.cloned.1.call-done.refs_2_, bf16[320,1536]{1,0:T(8,128)(2,1)S(1)} %collective-permute-done.refs_3_, ...), custom_call_target="tpu_custom_call" | custom-call | flops 8053063680 | bytes 22544384 | tf_op jit(solution)/shard_map/project/pallas_call | solution.py:155
  258.6 1.6 collective-permute-start.21
  260.2 27.4 %collective-permute-done.12.refs_3_.refs_1_ = bf16[256,5120]{1,0:T(8,128)(2,1)} collective-permute-done((bf16[256,5120]{1,0:T(8,128)(2,1)}, bf16[256,5120]{1,0:T(8,128)(2,1)}, u32[]{:S(2)}, u32[]{:S(2)}) %collective-permute-start.12) | collective-permute-done | bytes 2621472 | tf_op jit(solution)/shard_map/ppermute | solution.py:304
  287.6 1.2 copy-done.1
  288.8 1.2 copy-done.3
  290.0 17.5 %project.5 = bf16[512,1536]{1,0:T(8,128)(2,1)} custom-call(s32[14]{0:T(128)S(1)} %concatenate.22.scal, bf16[256,5120]{1,0:T(8,128)(2,1)} %collective-permute-done.9.refs_2_.refs_0_, bf16[256,5120]{1,0:T(8,128)(2,1)} %collective-permute-done.12.refs_3_.refs_1_, bf16[1280,1536]{1,0:T(8,128)(2,1)} %all-gather.11.cloned.1.call-done.refs_2_, ...), custom_call_target="tpu_custom_call" | custom-call | flops 8053063680 | bytes 22544384 | tf_op jit(solution)/shard_map/project/pallas_call | solution.py:155
  307.4 2.6 collective-permute-start.22
  310.1 0.1 concatenate.18.scal
  310.8 0.1 stack.65.scal
  310.9 0.0 all-gather.5.cloned.1.call-done.refs_4_
  311.0 0.0 all-gather.7.cloned.1.call-done.refs_5_
  311.0 0.0 all-gather.9.cloned.1.call-done.refs_6_
  311.0 34.1 %project.3.refs_0_ = bf16[1024,1536]{1,0:T(8,128)(2,1)} custom-call(s32[16]{0:T(128)S(1)} %concatenate.18.scal, bf16[256,5120]{1,0:T(8,128)(2,1)} %fusion.2.refs_0_, bf16[256,5120]{1,0:T(8,128)(2,1)} %collective-permute-done.8.refs_1_, bf16[256,5120]{1,0:T(8,128)(2,1)} %collective-permute-done.9.refs_2_.refs_0_, ...), custom_call_target="tpu_custom_call" | custom-call | flops 16106127360 | bytes 29360128 | tf_op jit(solution)/shard_map/project/pallas_call | solution.py:155
  345.1 17.6 %attend.1 = bf16[1024,1024]{1,0:T(8,128)(2,1)} custom-call(s32[6]{0:T(128)S(1)} %stack.65.scal, bf16[1024,1536]{1,0:T(8,128)(2,1)} %project.3.refs_0_, bf16[512,1536]{1,0:T(8,128)(2,1)S(1)} %collective-permute-done.21.refs_1_, bf16[512,1536]{1,0:T(8,128)(2,1)} %collective-permute-done.22.refs_2_), custom_call_target="tpu_custom_call" | custom-call | flops 4294967296 | bytes 5242880 | tf_op jit(solution)/shard_map/attend/pallas_call | solution.py:266
  (41 shorter events, 0.1 us)
Async XLA Ops:
  6.5 233.4 %all-gather.11.cloned.1.call-start = ((), (), s32[]{:S(2)}) async-start(), calls=%async_computation.3 | async-start | bytes 4915200 | tf_op jit(solution)/shard_map/all_gather | solution.py:310
  10.3 68.7 %copy-start.9 = (bf16[320,1536]{1,0:T(8,128)(2,1)}, bf16[320,1536]{1,0:T(8,128)(2,1)S(1)}, u32[]{:S(2)}) copy-start(bf16[320,1536]{1,0:T(8,128)(2,1)S(1)} %get-tuple-element.20) | copy-start | bytes 2949124
  10.3 118.4 %copy-start.10 = (f32[5120]{0:T(1024)S(1)}, f32[5120]{0:T(1024)}, u32[]{:S(2)}) copy-start(f32[5120]{0:T(1024)} %param.8) | copy-start | bytes 61444
  10.4 300.6 %all-gather.5.cloned.1.call-start = ((), (), s32[]{:S(2)}) async-start(), calls=%async_computation | async-start | bytes 4915200 | tf_op jit(solution)/shard_map/all_gather | solution.py:310
  11.1 299.9 %all-gather.7.cloned.1.call-start = ((), (), s32[]{:S(2)}) async-start(), calls=%async_computation.1 | async-start | bytes 4915200 | tf_op jit(solution)/shard_map/all_gather | solution.py:310
  11.2 47.8 %collective-permute-start = (bf16[320,1536]{1,0:T(8,128)(2,1)}, bf16[320,1536]{1,0:T(8,128)(2,1)S(1)}, u32[]{:S(2)}, u32[]{:S(2)}) collective-permute-start(bf16[320,1536]{1,0:T(8,128)(2,1)} %get-tuple-element.34), channel_id=1, source_target_pairs={{1,2},{2,1},{5,6},{6,5},{9,10},{10,9},{13,14},{14,13},{17,18},{18,... | collective-permute-start | bytes 2949128 | tf_op jit(solution)/shard_map/ppermute | solution.py:304
  14.7 44.3 %collective-permute-start.1 = (bf16[320,1536]{1,0:T(8,128)(2,1)}, bf16[320,1536]{1,0:T(8,128)(2,1)S(1)}, u32[]{:S(2)}, u32[]{:S(2)}) collective-permute-start(bf16[320,1536]{1,0:T(8,128)(2,1)} %get-tuple-element.34), channel_id=1, source_target_pairs={{0,2},{3,1},{4,6},{7,5},{8,10},{11,9},{12,14},{15,13},{16,18},{19,... | collective-permute-start | bytes 2949128 | tf_op jit(solution)/shard_map/ppermute | solution.py:304
  16.0 45.0 %collective-permute-start.2 = (bf16[320,1536]{1,0:T(8,128)(2,1)}, bf16[320,1536]{1,0:T(8,128)(2,1)S(1)}, u32[]{:S(2)}, u32[]{:S(2)}) collective-permute-start(bf16[320,1536]{1,0:T(8,128)(2,1)} %get-tuple-element.36), channel_id=1, source_target_pairs={{0,1},{3,2},{4,5},{7,6},{8,9},{11,10},{12,13},{15,14},{16,17},{19,... | collective-permute-start | bytes 2949128 | tf_op jit(solution)/shard_map/ppermute | solution.py:304
  17.3 61.7 %collective-permute-start.3 = (bf16[320,1536]{1,0:T(8,128)(2,1)S(1)}, bf16[320,1536]{1,0:T(8,128)(2,1)}, u32[]{:S(2)}, u32[]{:S(2)}) collective-permute-start(bf16[320,1536]{1,0:T(8,128)(2,1)S(1)} %get-tuple-element.20), channel_id=1, source_target_pairs={{1,2},{2,1},{5,6},{6,5},{9,10},{10,9},{13,14},{14,13},{17,18},{18,... | collective-permute-start | bytes 2949128 | tf_op jit(solution)/shard_map/ppermute | solution.py:304
  59.0 181.0 %copy-start = (bf16[320,1536]{1,0:T(8,128)(2,1)}, bf16[320,1536]{1,0:T(8,128)(2,1)S(1)}, u32[]{:S(2)}) copy-start(bf16[320,1536]{1,0:T(8,128)(2,1)S(1)} %collective-permute-done.refs_3_) | copy-start | bytes 2949124
  59.0 181.0 %copy-start.2 = (bf16[320,1536]{1,0:T(8,128)(2,1)}, bf16[320,1536]{1,0:T(8,128)(2,1)S(1)}, u32[]{:S(2)}) copy-start(bf16[320,1536]{1,0:T(8,128)(2,1)S(1)} %collective-permute-done.1.refs_7_) | copy-start | bytes 2949124
  61.0 21.1 %copy-start.13 = (bf16[320,1536]{1,0:T(8,128)(2,1)}, bf16[320,1536]{1,0:T(8,128)(2,1)S(1)}, u32[]{:S(2)}) copy-start(bf16[320,1536]{1,0:T(8,128)(2,1)S(1)} %collective-permute-done.2.refs_11_) | copy-start | bytes 2949124
  79.0 47.1 %collective-permute-start.6 = (bf16[320,1536]{1,0:T(8,128)(2,1)S(1)}, bf16[320,1536]{1,0:T(8,128)(2,1)}, u32[]{:S(2)}, u32[]{:S(2)}) collective-permute-start(bf16[320,1536]{1,0:T(8,128)(2,1)S(1)} %collective-permute-done.refs_3_), channel_id=1, source_target_pairs={{0,8},{4,12},{8,0},{12,4},{1,9},{5,13},{9,1},{13,5},{2,10},{6,14},... | collective-permute-start | bytes 2949128 | tf_op jit(solution)/shard_map/ppermute | solution.py:307
  79.5 26.8 %collective-permute-start.5 = (bf16[320,1536]{1,0:T(8,128)(2,1)}, bf16[320,1536]{1,0:T(8,128)(2,1)S(1)}, u32[]{:S(2)}, u32[]{:S(2)}) collective-permute-start(bf16[320,1536]{1,0:T(8,128)(2,1)} %get-tuple-element.21), channel_id=1, source_target_pairs={{0,1},{3,2},{4,5},{7,6},{8,9},{11,10},{12,13},{15,14},{16,17},{19,... | collective-permute-start | bytes 2949128 | tf_op jit(solution)/shard_map/ppermute | solution.py:304
  80.8 45.3 %collective-permute-start.4 = (bf16[320,1536]{1,0:T(8,128)(2,1)}, bf16[320,1536]{1,0:T(8,128)(2,1)}, u32[]{:S(2)}, u32[]{:S(2)}) collective-permute-start(bf16[320,1536]{1,0:T(8,128)(2,1)} %copy-done.9), channel_id=1, source_target_pairs={{0,2},{3,1},{4,6},{7,5},{8,10},{11,9},{12,14},{15,13},{16,18},{19,... | collective-permute-start | bytes 2949128 | tf_op jit(solution)/shard_map/ppermute | solution.py:304
  82.1 44.0 %collective-permute-start.7 = (bf16[320,1536]{1,0:T(8,128)(2,1)S(1)}, bf16[320,1536]{1,0:T(8,128)(2,1)}, u32[]{:S(2)}, u32[]{:S(2)}) collective-permute-start(bf16[320,1536]{1,0:T(8,128)(2,1)S(1)} %collective-permute-done.1.refs_7_), channel_id=1, source_target_pairs={{0,8},{4,12},{8,0},{12,4},{1,9},{5,13},{9,1},{13,5},{2,10},{6,14},... | collective-permute-start | bytes 2949128 | tf_op jit(solution)/shard_map/ppermute | solution.py:307
  106.3 24.7 %copy-start.8 = (bf16[320,1536]{1,0:T(8,128)(2,1)}, bf16[320,1536]{1,0:T(8,128)(2,1)S(1)}, u32[]{:S(2)}) copy-start(bf16[320,1536]{1,0:T(8,128)(2,1)S(1)} %collective-permute-done.5) | copy-start | bytes 2949124
  126.2 184.8 %all-gather.9.cloned.1.call-start = ((), (), s32[]{:S(2)}) async-start(), calls=%async_computation.2 | async-start | bytes 4915200 | tf_op jit(solution)/shard_map/all_gather | solution.py:310
  126.2 2.5 copy-start.7
  128.7 85.5 %copy-start.11 = (f32[128]{0:T(128)S(1)}, f32[128]{0:T(128)}, u32[]{:S(2)}) copy-start(f32[128]{0:T(128)} %param.10) | copy-start | bytes 1540
  128.7 85.5 %copy-start.12 = (f32[128]{0:T(128)S(1)}, f32[128]{0:T(128)}, u32[]{:S(2)}) copy-start(f32[128]{0:T(128)} %param.9) | copy-start | bytes 1540
  131.0 77.6 %collective-permute-start.9 = (bf16[256,5120]{1,0:T(8,128)(2,1)}, bf16[256,5120]{1,0:T(8,128)(2,1)}, u32[]{:S(2)}, u32[]{:S(2)}) collective-permute-start(bf16[256,5120]{1,0:T(8,128)(2,1)} %fusion.2.refs_0_), channel_id=1, source_target_pairs={{0,1},{3,2},{4,5},{7,6},{8,9},{11,10},{12,13},{15,14},{16,17},{19,... | collective-permute-start | bytes 7864328 | tf_op jit(solution)/shard_map/ppermute | solution.py:304
  132.3 44.1 %collective-permute-start.10 = (bf16[320,1536]{1,0:T(8,128)(2,1)}, bf16[320,1536]{1,0:T(8,128)(2,1)}, u32[]{:S(2)}, u32[]{:S(2)}) collective-permute-start(bf16[320,1536]{1,0:T(8,128)(2,1)} %copy-done.13), channel_id=1, source_target_pairs={{0,8},{4,12},{8,0},{12,4},{1,9},{5,13},{9,1},{13,5},{2,10},{6,14},... | collective-permute-start | bytes 2949128 | tf_op jit(solution)/shard_map/ppermute | solution.py:307
  176.4 32.2 %collective-permute-start.11 = (bf16[320,1536]{1,0:T(8,128)(2,1)}, bf16[320,1536]{1,0:T(8,128)(2,1)}, u32[]{:S(2)}, u32[]{:S(2)}) collective-permute-start(bf16[320,1536]{1,0:T(8,128)(2,1)} %collective-permute-done.3.refs_7_), channel_id=1, source_target_pairs={{0,8},{4,12},{8,0},{12,4},{1,9},{5,13},{9,1},{13,5},{2,10},{6,14},... | collective-permute-start | bytes 2949128 | tf_op jit(solution)/shard_map/ppermute | solution.py:307
  177.9 62.0 %collective-permute-start.8 = (bf16[256,5120]{1,0:T(8,128)(2,1)}, bf16[256,5120]{1,0:T(8,128)(2,1)}, u32[]{:S(2)}, u32[]{:S(2)}) collective-permute-start(bf16[256,5120]{1,0:T(8,128)(2,1)} %fusion.2.refs_0_), channel_id=1, source_target_pairs={{1,2},{2,1},{5,6},{6,5},{9,10},{10,9},{13,14},{14,13},{17,18},{18,... | collective-permute-start | bytes 7864328 | tf_op jit(solution)/shard_map/ppermute | solution.py:304
  181.0 30.2 %collective-permute-start.15 = (bf16[320,1536]{1,0:T(8,128)(2,1)S(1)}, bf16[320,1536]{1,0:T(8,128)(2,1)S(1)}, u32[]{:S(2)}, u32[]{:S(2)}) collective-permute-start(bf16[320,1536]{1,0:T(8,128)(2,1)S(1)} %collective-permute-done.refs_3_), channel_id=1, source_target_pairs={{0,4},{4,0},{8,12},{12,8},{1,5},{5,1},{9,13},{13,9},{2,6},{6,2},{1... | collective-permute-start | bytes 2949128 | tf_op jit(solution)/shard_map/ppermute | solution.py:307
  181.1 31.5 %collective-permute-start.17 = (bf16[320,1536]{1,0:T(8,128)(2,1)S(1)}, bf16[320,1536]{1,0:T(8,128)(2,1)S(1)}, u32[]{:S(2)}, u32[]{:S(2)}) collective-permute-start(bf16[320,1536]{1,0:T(8,128)(2,1)S(1)} %collective-permute-done.1.refs_7_), channel_id=1, source_target_pairs={{0,4},{4,0},{8,12},{12,8},{1,5},{5,1},{9,13},{13,9},{2,6},{6,2},{1... | collective-permute-start | bytes 2949128 | tf_op jit(solution)/shard_map/ppermute | solution.py:307
  208.6 5.1 %collective-permute-start.19 = (bf16[320,1536]{1,0:T(8,128)(2,1)}, bf16[320,1536]{1,0:T(8,128)(2,1)}, u32[]{:S(2)}, u32[]{:S(2)}) collective-permute-start(bf16[320,1536]{1,0:T(8,128)(2,1)} %copy-done.13), channel_id=1, source_target_pairs={{0,4},{4,0},{8,12},{12,8},{1,5},{5,1},{9,13},{13,9},{2,6},{6,2},{1... | collective-permute-start | bytes 2949128 | tf_op jit(solution)/shard_map/ppermute | solution.py:307
  208.6 79.0 %collective-permute-start.12 = (bf16[256,5120]{1,0:T(8,128)(2,1)}, bf16[256,5120]{1,0:T(8,128)(2,1)}, u32[]{:S(2)}, u32[]{:S(2)}) collective-permute-start(bf16[256,5120]{1,0:T(8,128)(2,1)} %collective-permute-done.9.refs_2_.refs_0_), channel_id=1, source_target_pairs={{1,2},{2,1},{5,6},{6,5},{9,10},{10,9},{13,14},{14,13},{17,18},{18,... | collective-permute-start | bytes 7864328 | tf_op jit(solution)/shard_map/ppermute | solution.py:304
  211.2 1.0 copy-start.4
  212.2 4.4 %collective-permute-start.16 = (bf16[320,1536]{1,0:T(8,128)(2,1)}, bf16[320,1536]{1,0:T(8,128)(2,1)}, u32[]{:S(2)}, u32[]{:S(2)}) collective-permute-start(bf16[320,1536]{1,0:T(8,128)(2,1)} %collective-permute-done.6.refs_4_), channel_id=1, source_target_pairs={{0,4},{4,0},{8,12},{12,8},{1,5},{5,1},{9,13},{13,9},{2,6},{6,2},{1... | collective-permute-start | bytes 2949128 | tf_op jit(solution)/shard_map/ppermute | solution.py:307
  212.6 1.0 copy-start.14
  213.5 3.2 collective-permute-start.18
  213.7 4.4 %collective-permute-start.20 = (bf16[320,1536]{1,0:T(8,128)(2,1)}, bf16[320,1536]{1,0:T(8,128)(2,1)}, u32[]{:S(2)}, u32[]{:S(2)}) collective-permute-start(bf16[320,1536]{1,0:T(8,128)(2,1)} %collective-permute-done.10.refs_12_), channel_id=1, source_target_pairs={{0,4},{4,0},{8,12},{12,8},{1,5},{5,1},{9,13},{13,9},{2,6},{6,2},{1... | collective-permute-start | bytes 2949128 | tf_op jit(solution)/shard_map/ppermute | solution.py:307
  216.5 94.4 %collective-permute-start.13 = (bf16[320,1536]{1,0:T(8,128)(2,1)}, bf16[320,1536]{1,0:T(8,128)(2,1)}, u32[]{:S(2)}, u32[]{:S(2)}) collective-permute-start(bf16[320,1536]{1,0:T(8,128)(2,1)} %collective-permute-done.3.refs_7_), channel_id=1, source_target_pairs={{0,4},{4,0},{8,12},{12,8},{1,5},{5,1},{9,13},{13,9},{2,6},{6,2},{1... | collective-permute-start | bytes 2949128 | tf_op jit(solution)/shard_map/ppermute | solution.py:307
  216.8 94.2 %collective-permute-start.14 = (bf16[320,1536]{1,0:T(8,128)(2,1)}, bf16[320,1536]{1,0:T(8,128)(2,1)}, u32[]{:S(2)}, u32[]{:S(2)}) collective-permute-start(bf16[320,1536]{1,0:T(8,128)(2,1)} %collective-permute-done.11.refs_8_), channel_id=1, source_target_pairs={{0,4},{4,0},{8,12},{12,8},{1,5},{5,1},{9,13},{13,9},{2,6},{6,2},{1... | collective-permute-start | bytes 2949128 | tf_op jit(solution)/shard_map/ppermute | solution.py:307
  240.0 1.2 copy-start.5
  241.2 46.4 %copy-start.6 = (bf16[320,1536]{1,0:T(8,128)(2,1)S(1)}, bf16[320,1536]{1,0:T(8,128)(2,1)}, u32[]{:S(2)}) copy-start(bf16[320,1536]{1,0:T(8,128)(2,1)} %copy-done.4) | copy-start | bytes 2949124
  258.6 86.5 %collective-permute-start.21 = (bf16[512,1536]{1,0:T(8,128)(2,1)}, bf16[512,1536]{1,0:T(8,128)(2,1)S(1)}, u32[]{:S(2)}, u32[]{:S(2)}) collective-permute-start(bf16[512,1536]{1,0:T(8,128)(2,1)} %project.4), channel_id=1, source_target_pairs={{1,0},{2,3},{5,4},{6,7},{9,8},{10,11},{13,12},{14,15},{17,16},{18,... | collective-permute-start | bytes 4718600 | tf_op jit(solution)/shard_map/ppermute | solution.py:304
  287.6 1.2 copy-start.1
  288.8 1.2 copy-start.3
  307.4 37.6 %collective-permute-start.22 = (bf16[512,1536]{1,0:T(8,128)(2,1)}, bf16[512,1536]{1,0:T(8,128)(2,1)}, u32[]{:S(2)}, u32[]{:S(2)}) collective-permute-start(bf16[512,1536]{1,0:T(8,128)(2,1)} %project.5), channel_id=1, source_target_pairs={{1,0},{2,3},{5,4},{6,7},{9,8},{10,11},{13,12},{14,15},{17,16},{18,... | collective-permute-start | bytes 4718600 | tf_op jit(solution)/shard_map/ppermute | solution.py:304
Sparse Core Ops, SparseCore 0:
  10.5 33.1 all-gather.10
  45.2 32.9 all-gather.4
  126.3 51.0 all-gather.6
  178.8 40.9 all-gather.8

commit v2 on v1

--- a/solution.py
+++ b/solution.py
@@ -84,11 +84,12 @@
 
     def copies(step):
         listed = []
-        for index, (array, first, group, slot) in enumerate(sources):
+        for index, (array, first, base, group, slot) in enumerate(sources):
             start = pl.multiple_of((scal[group] * 4 + scal[slot]) * depth, 16)
+            low = base + step * tile
             listed.append(
                 pltpu.make_async_copy(
-                    pieces[array].at[first : first + depth, step * tile : (step + 1) * tile],
+                    pieces[array].at[first : first + depth, low : low + tile],
                     held.at[step % 2, pl.ds(start, depth), :],
                     sems.at[step % 2, index],
                 )
@@ -134,17 +135,16 @@
         copy.wait()
 
 
-def project(rows_list, places, spread_pieces, own_pieces, scal, cos, sin, gains):
+def project(rows_list, places, columns, spread_pieces, own_pieces, scal, cos, sin, gains):
     pieces, sources = [], []
     depth = rows_list[0].shape[1] // 16
-    for slot, array in spread_pieces:
-        sources += [(len(pieces), m * depth, 8 + m, slot) for m in range(4)]
+    for slot, base, array in spread_pieces:
+        sources += [(len(pieces), m * depth, base, 8 + m, slot) for m in range(4)]
         pieces.append(array)
-    for slot, four in own_pieces:
-        sources += [(len(pieces) + m, 0, 4 + m, slot) for m in range(4)]
+    for slot, base, four in own_pieces:
+        sources += [(len(pieces) + m, 0, base, 4 + m, slot) for m in range(4)]
         pieces += four
     counts = [r.shape[0] for r in rows_list]
-    columns = pieces[0].shape[1]
     steps = 3
     tile = columns // steps
     count = sum(counts)
@@ -314,42 +314,41 @@
     far = [(0, 2), (3, 1)]
     outward = [(1, 0), (2, 3)]
 
-    same_e, same_o, other_e, other_o = slab(end), slab(mid), slab(far_end), slab(far_mid)
+    same = jnp.concatenate([slab(end), slab(mid)], axis=1)
+    other = jnp.concatenate([slab(far_end), slab(far_mid)], axis=1)
     normed = head_norm(tokens.astype(jnp.float32), norm_gain).astype(jnp.bfloat16)
 
     def core_pair(piece, over):
         return [piece, over, beside(piece, 1), beside(over, 1)]
 
-    own_e, own_o = spread(same_e), spread(same_o)
-    swap_e = across(other_e, swap)
-    far_e = across(other_e, far)
-    end_e = across(same_e, inward)
-    swap_o = across(other_o, swap)
-    swap_e, far_e, end_e, swap_o = lax.optimization_barrier((swap_e, far_e, end_e, swap_o))
-    far_o = across(after(other_o, swap_e), far)
-    end_o = across(after(same_o, swap_e), inward)
-    over_swap_e = beside(swap_e, 2)
+    own = spread(same)
+    swap_w = across(other, swap)
+    far_w = across(other, far)
+    end_w = across(same, inward)
+    rows_b = across(after(normed, swap_w), swap)
+    rows_a = across(after(normed, swap_w), inward)
+    over_swap = beside(after(swap_w, rows_b), 2)
+    far_e, end_e = far_w[:, :columns], end_w[:, :columns]
     over_far_e = beside(far_e, 2)
-    far_o, end_o, over_swap_e, over_far_e = lax.optimization_barrier(
-        (far_o, end_o, over_swap_e, over_far_e)
-    )
-    rows_a = across(after(normed, far_o), inward)
-    rows_b = across(after(normed, far_o), swap)
-    over_end_e = beside(after(end_e, far_o), 2)
-    over_swap_o = beside(after(swap_o, over_end_e), 2)
-    rows_c = across(after(rows_a, over_swap_o), swap)
-
+    over_end_e = beside(after(end_e, over_swap), 2)
+    rows_c = across(after(rows_a, over_end_e), swap)
+
+    swap_pieces = core_pair(swap_w, over_swap)
     end_pieces = (
-        [(0, own_e)],
+        [(0, 0, own)],
         [
-            (1, core_pair(swap_e, over_swap_e)),
-            (2, core_pair(far_e, over_far_e)),
-            (3, core_pair(end_e, over_end_e)),
+            (1, 0, swap_pieces),
+            (2, 0, core_pair(far_e, over_far_e)),
+            (3, 0, core_pair(end_e, over_end_e)),
         ],
     )
     mid_pieces = (
-        [(0, own_o), (2, spread(far_o)), (3, spread(end_o))],
-        [(1, core_pair(swap_o, over_swap_o))],
+        [
+            (0, columns, own),
+            (2, 0, spread(far_w[:, columns:])),
+            (3, 0, spread(end_w[:, columns:])),
+        ],
+        [(1, columns, swap_pieces)],
     )
     scal = jnp.stack(
         [mid, far_mid, far_end, end]
@@ -368,7 +367,14 @@
 
     def run(picked, pieces):
         return project(
-            [blocks[i] for i in picked], [places[i] for i in picked], *pieces, scal, cos, sin, gains
+            [blocks[i] for i in picked],
+            [places[i] for i in picked],
+            columns,
+            *pieces,
+            scal,
+            cos,
+            sin,
+            gains,
         )
 
     sent = [across(run(picked, end_pieces), outward) for picked in ([0, 1], [2, 3])]

time: 373 us -> 409 us (1.097)
  the two profiles are of different devices: /device:TPU:14 before, /device:TPU:22 now
where the time goes in v2:
time: 409 us; the launch traced here: 405 us
  waiting for transfers between devices  267 us (65%)
  Pallas kernels  87.3 us (21%)
  starting transfers between devices  19.6 us (5%)
  between operations  14.3 us (3%)
  local copies, waits for them, and re-layouts  8.95 us (2%)
  other arithmetic  8.67 us (2%)
    ppermute x8, waiting for transfers between devices, across(): return lax.ppermute(x, 'tensor', pairs)  166 us
    ppermute x9, waiting for transfers between devices, beside(): return lax.ppermute(x, 'fsdp', [(i, i ^ bit) for i in range(4)])  100 us
    pallas_call x3, Pallas kernels, project(): pl.pallas_call(functools.partial(project_kernel, counts, sources, tile),...  69.7 us
    pallas_call x1, Pallas kernels, attend_blocks(): pl.pallas_call(functools.partial(attend_kernel, near_parts, far_parts, 25...  17.6 us
    ppermute x8, starting transfers between devices, across(): return lax.ppermute(x, 'tensor', pairs)  15.9 us
  transfers between devices with their start and end apart: 20, of which 8 were waited for; matrix products, arithmetic and copies ran while one was open for 2% of the time, Pallas kernels for 17%

profile of v2, /device:TPU:22, one launch (start us, length us, event | category | flops | bytes accessed | tf_op | source)
XLA Modules:
  0.0 405.5 jit_solution(3130513653216614393)
XLA Ops:
  6.5 0.0 all-gather.4.cloned.1.call-start
  6.5 2.4 constant_dynamic-slice_fusion.1
  9.0 1.5 pad_maximum_fusion.1
  10.5 0.0 all-gather.4.cloned.1.call-update
  10.6 0.0 all-gather.6.cloned.1.call-start
  10.6 0.2 pad_maximum_fusion
  10.8 1.3 collective-permute-start.7
  12.1 0.0 copy-done.7
  12.2 46.0 %collective-permute-done.7 = bf16[320,3072]{1,0:T(8,128)(2,1)S(1)} collective-permute-done((bf16[320,3072]{1,0:T(8,128)(2,1)S(1)}, bf16[320,3072]{1,0:T(8,128)(2,1)S(1)}, u32[]{:S(2)}, u32[]{:S(2)}) %collective-permute-start.7) | collective-permute-done | bytes 1966112 | tf_op jit(solution)/shard_map/ppermute | solution.py:304
  58.2 1.1 fusion.4
  59.3 0.0 all-gather.6.cloned.1.call-update
  59.3 0.0 all-gather.8.cloned.1.call-start
  59.4 0.7 copy-done.8
  60.1 2.6 collective-permute-start
  62.7 2.3 fusion
  65.1 0.0 copy-start.4
  65.1 2.3 fusion.2.refs_0_
  67.4 38.6 %collective-permute-done.refs_7_.refs_3_ = bf16[320,3072]{1,0:T(8,128)(2,1)} collective-permute-done((bf16[320,3072]{1,0:T(8,128)(2,1)S(1)}, bf16[320,3072]{1,0:T(8,128)(2,1)}, u32[]{:S(2)}, u32[]{:S(2)}) %collective-permute-start) | collective-permute-done | bytes 1966112 | tf_op jit(solution)/shard_map/ppermute | solution.py:304
  106.0 2.3 collective-permute-start.1
  108.4 0.0 copy-done.4
  108.4 1.3 collective-permute-start.3
  109.7 55.2 %collective-permute-done.1.refs_1_ = bf16[256,5120]{1,0:T(8,128)(2,1)S(1)} collective-permute-done((bf16[256,5120]{1,0:T(8,128)(2,1)}, bf16[256,5120]{1,0:T(8,128)(2,1)S(1)}, u32[]{:S(2)}, u32[]{:S(2)}) %collective-permute-start.1) | collective-permute-done | bytes 2621472 | tf_op jit(solution)/shard_map/ppermute | solution.py:304
  165.0 0.5 collective-permute-start.4
  165.5 1.3 collective-permute-start.2
  166.8 0.0 collective-permute-done.3
  166.8 1.1 fusion.5
  167.9 0.0 all-gather.8.cloned.1.call-update
  167.9 61.3 %collective-permute-done.4.refs_8_.refs_4_ = bf16[320,3072]{1,0:T(8,128)(2,1)} collective-permute-done((bf16[320,3072]{1,0:T(8,128)(2,1)}, bf16[320,3072]{1,0:T(8,128)(2,1)}, u32[]{:S(2)}, u32[]{:S(2)}) %collective-permute-start.4) | collective-permute-done | bytes 1966112 | tf_op jit(solution)/shard_map/ppermute | solution.py:307
  229.2 0.6 collective-permute-start.5
  229.9 1.4 collective-permute-start.10
  231.2 0.0 collective-permute-start.11
  231.2 0.5 collective-permute-start.8
  231.8 0.0 collective-permute-done.2.refs_2_.refs_0_
  231.8 0.0 collective-permute-start.13
  231.8 22.3 %collective-permute-done.5.refs_12_ = bf16[320,1536]{1,0:T(8,128)(2,1)} collective-permute-done((bf16[320,1536]{1,0:T(8,128)(2,1)S(1)}, bf16[320,1536]{1,0:T(8,128)(2,1)}, u32[]{:S(2)}, u32[]{:S(2)}) %collective-permute-start.5) | collective-permute-done | bytes 983072 | tf_op jit(solution)/shard_map/ppermute | solution.py:307
  254.0 0.0 collective-permute-start.9
  254.0 16.3 %collective-permute-done.10.refs_8_ = bf16[320,1536]{1,0:T(8,128)(2,1)} collective-permute-done((bf16[320,1536]{1,0:T(8,128)(2,1)S(1)}, bf16[320,1536]{1,0:T(8,128)(2,1)}, u32[]{:S(2)}, u32[]{:S(2)}) %collective-permute-start.10) | collective-permute-done | bytes 983072 | tf_op jit(solution)/shard_map/ppermute | solution.py:307
  270.3 2.9 collective-permute-start.6
  273.2 0.0 collective-permute-done.11.refs_9_
  273.2 1.0 copy-done
  274.2 0.0 collective-permute-start.12
  274.2 0.0 collective-permute-done.13.refs_13_
  274.2 1.0 copy-done.5
  275.2 0.5 collective-permute-start.14
  275.7 0.1 concatenate.29.scal
  275.8 0.1 concatenate.30.scal
  275.9 1.9 fusion.3
  277.8 0.3 pad_maximum_fusion.2
  278.2 0.0 collective-permute-done.8.refs_9_.refs_5_
  278.2 0.0 collective-permute-done.12.refs_10_
  278.2 0.3 collective-permute-done.14.refs_14_
  278.5 0.0 collective-permute-done.9.refs_10_.refs_6_
  278.5 1.2 copy-done.1
  279.7 17.8 %project.4 = bf16[512,1536]{1,0:T(8,128)(2,1)} custom-call(s32[14]{0:T(128)S(1)} %concatenate.29.scal, bf16[256,5120]{1,0:T(8,128)(2,1)} %fusion.2.refs_0_, bf16[256,5120]{1,0:T(8,128)(2,1)} %copy-done.6, bf16[1280,3072]{1,0:T(8,128)(2,1)} %all-gather.4.cloned.1.call-done.refs_4_.refs_2_, bf16[320,3072]{1,0:T(8,128)(2,1)} %collective-permute-done.refs_7_.refs_3_, ...), custom_call_target="tpu_custom_call" | custom-call | flops 8053063680 | bytes 22544384 | tf_op jit(solution)/shard_map/project/pallas_call | solution.py:155
  297.5 2.6 collective-permute-start.15
  300.1 26.5 %collective-permute-done.6.refs_3_.refs_1_ = bf16[256,5120]{1,0:T(8,128)(2,1)} collective-permute-done((bf16[256,5120]{1,0:T(8,128)(2,1)}, bf16[256,5120]{1,0:T(8,128)(2,1)}, u32[]{:S(2)}, u32[]{:S(2)}) %collective-permute-start.6) | collective-permute-done | bytes 2621472 | tf_op jit(solution)/shard_map/ppermute | solution.py:304
  326.6 17.8 %project.5 = bf16[512,1536]{1,0:T(8,128)(2,1)} custom-call(s32[14]{0:T(128)S(1)} %concatenate.30.scal, bf16[256,5120]{1,0:T(8,128)(2,1)} %collective-permute-done.2.refs_2_.refs_0_, bf16[256,5120]{1,0:T(8,128)(2,1)} %collective-permute-done.6.refs_3_.refs_1_, bf16[1280,3072]{1,0:T(8,128)(2,1)} %all-gather.4.cloned.1.call-done.refs_4_.refs_2_, ...), custom_call_target="tpu_custom_call" | custom-call | flops 8053063680 | bytes 22544384 | tf_op jit(solution)/shard_map/project/pallas_call | solution.py:155
  344.5 1.6 collective-permute-start.16
  346.1 0.1 concatenate.24.scal
  346.9 0.1 stack.65.scal
  346.9 34.1 %project.3.refs_0_ = bf16[1024,1536]{1,0:T(8,128)(2,1)} custom-call(s32[16]{0:T(128)S(1)} %concatenate.24.scal, bf16[256,5120]{1,0:T(8,128)(2,1)} %fusion.2.refs_0_, bf16[256,5120]{1,0:T(8,128)(2,1)} %copy-done.6, bf16[256,5120]{1,0:T(8,128)(2,1)} %collective-permute-done.2.refs_2_.refs_0_, bf16[256,5120]{1,0:T(8,128)(2,1)} %collective-permute-done.6.refs_3_.refs_1_, ...), custom_call_target="tpu_custom_call" | custom-call | flops 16106127360 | bytes 29360128 | tf_op jit(solution)/shard_map/project/pallas_call | solution.py:155
  381.1 0.0 collective-permute-done.15.refs_1_
  381.1 0.0 collective-permute-done.16.refs_2_
  381.1 17.6 %attend.1 = bf16[1024,1024]{1,0:T(8,128)(2,1)} custom-call(s32[6]{0:T(128)S(1)} %stack.65.scal, bf16[1024,1536]{1,0:T(8,128)(2,1)} %project.3.refs_0_, bf16[512,1536]{1,0:T(8,128)(2,1)} %collective-permute-done.15.refs_1_, bf16[512,1536]{1,0:T(8,128)(2,1)S(1)} %collective-permute-done.16.refs_2_), custom_call_target="tpu_custom_call" | custom-call | flops 4294967296 | bytes 5242880 | tf_op jit(solution)/shard_map/attend/pallas_call | solution.py:266
  (24 shorter events, 0.1 us)
Async XLA Ops:
  6.5 272.0 %all-gather.4.cloned.1.call-start = ((), (), s32[]{:S(2)}) async-start(), calls=%async_computation | async-start | bytes 9830400 | tf_op jit(solution)/shard_map/all_gather | solution.py:310
  10.6 336.4 %all-gather.6.cloned.1.call-start = ((), (), s32[]{:S(2)}) async-start(), calls=%async_computation.1 | async-start | bytes 4915200 | tf_op jit(solution)/shard_map/all_gather | solution.py:310
  10.8 1.3 copy-start.7
  10.8 47.4 %collective-permute-start.7 = (bf16[320,3072]{1,0:T(8,128)(2,1)S(1)}, bf16[320,3072]{1,0:T(8,128)(2,1)S(1)}, u32[]{:S(2)}, u32[]{:S(2)}) collective-permute-start(bf16[320,3072]{1,0:T(8,128)(2,1)S(1)} %pad_maximum_fusion), channel_id=1, source_target_pairs={{0,2},{3,1},{4,6},{7,5},{8,10},{11,9},{12,14},{15,13},{16,18},{19,... | collective-permute-start | bytes 5898248 | tf_op jit(solution)/shard_map/ppermute | solution.py:304
  58.2 1.9 copy-start.8
  59.3 5.8 %copy-start.9 = (f32[5120]{0:T(1024)S(1)}, f32[5120]{0:T(1024)}, u32[]{:S(2)}) copy-start(f32[5120]{0:T(1024)} %param.8) | copy-start | bytes 61444
  59.3 287.6 %all-gather.8.cloned.1.call-start = ((), (), s32[]{:S(2)}) async-start(), calls=%async_computation.2 | async-start | bytes 4915200 | tf_op jit(solution)/shard_map/all_gather | solution.py:310
  60.1 5.0 %copy-start.3 = (bf16[256,5120]{1,0:T(8,128)(2,1)S(1)}, bf16[256,5120]{1,0:T(8,128)(2,1)}, u32[]{:S(2)}) copy-start(bf16[256,5120]{1,0:T(8,128)(2,1)} %param.6) | copy-start | bytes 7864324
  60.1 45.9 %collective-permute-start = (bf16[320,3072]{1,0:T(8,128)(2,1)S(1)}, bf16[320,3072]{1,0:T(8,128)(2,1)}, u32[]{:S(2)}, u32[]{:S(2)}) collective-permute-start(bf16[320,3072]{1,0:T(8,128)(2,1)S(1)} %copy-done.8), channel_id=1, source_target_pairs={{1,2},{2,1},{5,6},{6,5},{9,10},{10,9},{13,14},{14,13},{17,18},{18,... | collective-permute-start | bytes 5898248 | tf_op jit(solution)/shard_map/ppermute | solution.py:304
  65.1 43.3 %copy-start.4 = (bf16[320,3072]{1,0:T(8,128)(2,1)S(1)}, bf16[320,3072]{1,0:T(8,128)(2,1)}, u32[]{:S(2)}) copy-start(bf16[320,3072]{1,0:T(8,128)(2,1)} %pad_maximum_fusion.1) | copy-start | bytes 5898244
  67.4 208.5 %copy-start.10 = (f32[128]{0:T(128)S(1)}, f32[128]{0:T(128)}, u32[]{:S(2)}) copy-start(f32[128]{0:T(128)} %param.10) | copy-start | bytes 1540
  67.4 208.5 %copy-start.11 = (f32[128]{0:T(128)S(1)}, f32[128]{0:T(128)}, u32[]{:S(2)}) copy-start(f32[128]{0:T(128)} %param.9) | copy-start | bytes 1540
  106.0 58.9 %collective-permute-start.1 = (bf16[256,5120]{1,0:T(8,128)(2,1)}, bf16[256,5120]{1,0:T(8,128)(2,1)S(1)}, u32[]{:S(2)}, u32[]{:S(2)}) collective-permute-start(bf16[256,5120]{1,0:T(8,128)(2,1)} %fusion.2.refs_0_), channel_id=1, source_target_pairs={{1,2},{2,1},{5,6},{6,5},{9,10},{10,9},{13,14},{14,13},{17,18},{18,... | collective-permute-start | bytes 7864328 | tf_op jit(solution)/shard_map/ppermute | solution.py:304
  108.4 58.4 %collective-permute-start.3 = (bf16[320,3072]{1,0:T(8,128)(2,1)S(1)}, bf16[320,3072]{1,0:T(8,128)(2,1)S(1)}, u32[]{:S(2)}, u32[]{:S(2)}) collective-permute-start(bf16[320,3072]{1,0:T(8,128)(2,1)S(1)} %copy-done.4), channel_id=1, source_target_pairs={{0,1},{3,2},{4,5},{7,6},{8,9},{11,10},{12,13},{15,14},{16,17},{19,... | collective-permute-start | bytes 5898248 | tf_op jit(solution)/shard_map/ppermute | solution.py:304
  165.0 1.8 copy-start.6
  165.0 64.3 %collective-permute-start.4 = (bf16[320,3072]{1,0:T(8,128)(2,1)}, bf16[320,3072]{1,0:T(8,128)(2,1)}, u32[]{:S(2)}, u32[]{:S(2)}) collective-permute-start(bf16[320,3072]{1,0:T(8,128)(2,1)} %collective-permute-done.refs_7_.refs_3_), channel_id=1, source_target_pairs={{0,8},{4,12},{8,0},{12,4},{1,9},{5,13},{9,1},{13,5},{2,10},{6,14},... | collective-permute-start | bytes 5898248 | tf_op jit(solution)/shard_map/ppermute | solution.py:307
  165.5 66.3 %collective-permute-start.2 = (bf16[256,5120]{1,0:T(8,128)(2,1)}, bf16[256,5120]{1,0:T(8,128)(2,1)}, u32[]{:S(2)}, u32[]{:S(2)}) collective-permute-start(bf16[256,5120]{1,0:T(8,128)(2,1)} %fusion.2.refs_0_), channel_id=1, source_target_pairs={{0,1},{3,2},{4,5},{7,6},{8,9},{11,10},{12,13},{15,14},{16,17},{19,... | collective-permute-start | bytes 7864328 | tf_op jit(solution)/shard_map/ppermute | solution.py:304
  229.2 24.8 %collective-permute-start.5 = (bf16[320,1536]{1,0:T(8,128)(2,1)S(1)}, bf16[320,1536]{1,0:T(8,128)(2,1)}, u32[]{:S(2)}, u32[]{:S(2)}) collective-permute-start(bf16[320,1536]{1,0:T(8,128)(2,1)S(1)} %get-tuple-element.11.refs_11_), channel_id=1, source_target_pairs={{0,8},{4,12},{8,0},{12,4},{1,9},{5,13},{9,1},{13,5},{2,10},{6,14},... | collective-permute-start | bytes 2949128 | tf_op jit(solution)/shard_map/ppermute | solution.py:307
  229.9 40.5 %collective-permute-start.10 = (bf16[320,1536]{1,0:T(8,128)(2,1)S(1)}, bf16[320,1536]{1,0:T(8,128)(2,1)}, u32[]{:S(2)}, u32[]{:S(2)}) collective-permute-start(bf16[320,1536]{1,0:T(8,128)(2,1)S(1)} %get-tuple-element.17.refs_7_), channel_id=1, source_target_pairs={{0,8},{4,12},{8,0},{12,4},{1,9},{5,13},{9,1},{13,5},{2,10},{6,14},... | collective-permute-start | bytes 2949128 | tf_op jit(solution)/shard_map/ppermute | solution.py:307
  231.2 42.0 %collective-permute-start.11 = (bf16[320,1536]{1,0:T(8,128)(2,1)S(1)}, bf16[320,1536]{1,0:T(8,128)(2,1)S(1)}, u32[]{:S(2)}, u32[]{:S(2)}) collective-permute-start(bf16[320,1536]{1,0:T(8,128)(2,1)S(1)} %get-tuple-element.17.refs_7_), channel_id=1, source_target_pairs={{0,4},{4,0},{8,12},{12,8},{1,5},{5,1},{9,13},{13,9},{2,6},{6,2},{1... | collective-permute-start | bytes 2949128 | tf_op jit(solution)/shard_map/ppermute | solution.py:307
  231.2 46.9 %collective-permute-start.8 = (bf16[320,3072]{1,0:T(8,128)(2,1)}, bf16[320,3072]{1,0:T(8,128)(2,1)}, u32[]{:S(2)}, u32[]{:S(2)}) collective-permute-start(bf16[320,3072]{1,0:T(8,128)(2,1)} %collective-permute-done.refs_7_.refs_3_), channel_id=1, source_target_pairs={{0,4},{4,0},{8,12},{12,8},{1,5},{5,1},{9,13},{13,9},{2,6},{6,2},{1... | collective-permute-start | bytes 5898248 | tf_op jit(solution)/shard_map/ppermute | solution.py:307
  231.8 42.4 %collective-permute-start.13 = (bf16[320,1536]{1,0:T(8,128)(2,1)S(1)}, bf16[320,1536]{1,0:T(8,128)(2,1)S(1)}, u32[]{:S(2)}, u32[]{:S(2)}) collective-permute-start(bf16[320,1536]{1,0:T(8,128)(2,1)S(1)} %get-tuple-element.11.refs_11_), channel_id=1, source_target_pairs={{0,4},{4,0},{8,12},{12,8},{1,5},{5,1},{9,13},{13,9},{2,6},{6,2},{1... | collective-permute-start | bytes 2949128 | tf_op jit(solution)/shard_map/ppermute | solution.py:307
  254.0 24.5 %collective-permute-start.9 = (bf16[320,3072]{1,0:T(8,128)(2,1)}, bf16[320,3072]{1,0:T(8,128)(2,1)}, u32[]{:S(2)}, u32[]{:S(2)}) collective-permute-start(bf16[320,3072]{1,0:T(8,128)(2,1)} %collective-permute-done.4.refs_8_.refs_4_), channel_id=1, source_target_pairs={{0,4},{4,0},{8,12},{12,8},{1,5},{5,1},{9,13},{13,9},{2,6},{6,2},{1... | collective-permute-start | bytes 5898248 | tf_op jit(solution)/shard_map/ppermute | solution.py:307
  270.3 56.3 %collective-permute-start.6 = (bf16[256,5120]{1,0:T(8,128)(2,1)}, bf16[256,5120]{1,0:T(8,128)(2,1)}, u32[]{:S(2)}, u32[]{:S(2)}) collective-permute-start(bf16[256,5120]{1,0:T(8,128)(2,1)} %collective-permute-done.2.refs_2_.refs_0_), channel_id=1, source_target_pairs={{1,2},{2,1},{5,6},{6,5},{9,10},{10,9},{13,14},{14,13},{17,18},{18,... | collective-permute-start | bytes 7864328 | tf_op jit(solution)/shard_map/ppermute | solution.py:304
  273.2 1.0 copy-start
  274.2 4.0 collective-permute-start.12
  274.2 1.0 copy-start.5
  275.2 3.3 collective-permute-start.14
  278.5 1.2 copy-start.1
  279.7 46.9 %copy-start.2 = (bf16[320,1536]{1,0:T(8,128)(2,1)S(1)}, bf16[320,1536]{1,0:T(8,128)(2,1)}, u32[]{:S(2)}) copy-start(bf16[320,1536]{1,0:T(8,128)(2,1)} %copy-done) | copy-start | bytes 2949124
  297.5 83.6 %collective-permute-start.15 = (bf16[512,1536]{1,0:T(8,128)(2,1)}, bf16[512,1536]{1,0:T(8,128)(2,1)}, u32[]{:S(2)}, u32[]{:S(2)}) collective-permute-start(bf16[512,1536]{1,0:T(8,128)(2,1)} %project.4), channel_id=1, source_target_pairs={{1,0},{2,3},{5,4},{6,7},{9,8},{10,11},{13,12},{14,15},{17,16},{18,... | collective-permute-start | bytes 4718600 | tf_op jit(solution)/shard_map/ppermute | solution.py:304
  344.5 36.6 %collective-permute-start.16 = (bf16[512,1536]{1,0:T(8,128)(2,1)}, bf16[512,1536]{1,0:T(8,128)(2,1)S(1)}, u32[]{:S(2)}, u32[]{:S(2)}) collective-permute-start(bf16[512,1536]{1,0:T(8,128)(2,1)} %project.5), channel_id=1, source_target_pairs={{1,0},{2,3},{5,4},{6,7},{9,8},{10,11},{13,12},{14,15},{17,16},{18,... | collective-permute-start | bytes 4718600 | tf_op jit(solution)/shard_map/ppermute | solution.py:304
Sparse Core Ops, SparseCore 0:
  10.7 55.3 all-gather.3
  67.7 32.9 all-gather.5
  168.0 56.8 all-gather.7

commit v3 on v0

--- a/solution.py
+++ b/solution.py
@@ -71,23 +71,26 @@
     return attend(qkv, q_gain, k_gain, lengths[0])
 
 
-def project_kernel(counts, tile, scal, *refs):
+def project_kernel(counts, sources, tile, scal, *refs):
     blocks = len(counts)
-    rows_refs = refs[:blocks]
-    pieces = refs[blocks : blocks + 16]
-    cos_ref, sin_ref, gain_ref, out = refs[blocks + 16 : blocks + 20]
-    taken, held, made, row_sems, sems, out_sems = refs[blocks + 20 :]
-    depth = pieces[0].shape[0]
+    arrays = max(source[0] for source in sources) + 1
+    middle_rows, end_rows = refs[:blocks], refs[blocks : 2 * blocks]
+    refs = refs[2 * blocks :]
+    pieces = refs[:arrays]
+    cos_ref, sin_ref, gain_ref, out = refs[arrays : arrays + 4]
+    taken, held, made, row_sems, sems, out_sems = refs[arrays + 4 :]
+    depth = taken.shape[1] // 16
     columns = made.shape[1]
     steps = columns // tile
 
     def copies(step):
         listed = []
-        for index in range(16):
-            start = pl.multiple_of((scal[4 + index // 4] * 4 + scal[index % 4]) * depth, 16)
+        for index, (array, first, group, slot) in enumerate(sources):
+            start = pl.multiple_of((scal[group] * 4 + scal[slot]) * depth, 16)
+            low = step * tile
             listed.append(
                 pltpu.make_async_copy(
-                    pieces[index].at[:, step * tile : (step + 1) * tile],
+                    pieces[array].at[first : first + depth, low : low + tile],
                     held.at[step % 2, pl.ds(start, depth), :],
                     sems.at[step % 2, index],
                 )
@@ -96,24 +99,30 @@
 
     starts = [sum(counts[:n]) for n in range(blocks)]
     row_copies = [
-        pltpu.make_async_copy(ref, taken.at[first : first + rows, :], row_sems.at[number])
-        for number, (ref, first, rows) in enumerate(zip(rows_refs, starts, counts))
+        [
+            pltpu.make_async_copy(ref, taken.at[first : first + rows, :], row_sems.at[number])
+            for ref in (middle_rows[number], end_rows[number])
+        ]
+        for number, (first, rows) in enumerate(zip(starts, counts))
     ]
     out_copies = []
-    for copy in copies(0) + row_copies:
+    for copy in copies(0):
         copy.start()
+    for in_middle, in_end in row_copies:
+        pl.when(scal[8] == 1)(in_middle.start)
+        pl.when(scal[8] == 0)(in_end.start)
     for step in range(steps):
         if step + 1 < steps:
             for copy in copies(step + 1):
                 copy.start()
         if step == 0:
-            for copy in row_copies:
-                copy.wait()
+            for in_middle, _ in row_copies:
+                in_middle.wait()
         for copy in copies(step):
             copy.wait()
         total = jnp.dot(taken[...], held[step % 2], preferred_element_type=jnp.float32)
         for number, (first, rows) in enumerate(zip(starts, counts)):
-            place = pl.ds(pl.multiple_of(scal[8 + number], 128), rows)
+            place = pl.ds(pl.multiple_of(scal[9 + number], 128), rows)
             cosine = cos_ref[place, :]
             sine = sin_ref[place, :]
             for head in range(tile // HD):
@@ -134,20 +143,22 @@
 
 
 def project(rows_list, places, pieces, scal, cos, sin, gains):
-    counts = [r.shape[0] for r in rows_list]
+    depth = rows_list[0][0].shape[1] // 16
     columns = pieces[0].shape[1]
+    sources = [(n, m * depth, 4 + m, n) for n in range(4) for m in range(4)]
+    counts = [r.shape[0] for r, _ in rows_list]
     steps = 3
     tile = columns // steps
     count = sum(counts)
-    width = rows_list[0].shape[1]
+    width = rows_list[0][0].shape[1]
     scal = jnp.concatenate([scal, jnp.stack(places)]).astype(jnp.int32)
     vmem = pl.BlockSpec(memory_space=pltpu.VMEM)
     hbm = pl.BlockSpec(memory_space=pltpu.HBM)
     return pl.pallas_call(
-        functools.partial(project_kernel, counts, tile),
+        functools.partial(project_kernel, counts, sources, tile),
         out_shape=pltpu.HBM((count, columns), jnp.bfloat16),
         in_specs=[pl.BlockSpec(memory_space=pltpu.SMEM)]
-        + [hbm] * (len(counts) + 16)
+        + [hbm] * (2 * len(counts) + len(pieces))
         + [vmem] * 3,
         out_specs=hbm,
         scratch_shapes=[
@@ -165,38 +176,26 @@
             transcendentals=0,
         ),
         name="project",
-    )(scal, *rows_list, *pieces, cos, sin, gains)
-
-
-def attend_kernel(near_parts, far_parts, block, scal, *refs):
-    near = refs[: len(near_parts)]
-    far = refs[len(near_parts) : len(near_parts) + len(far_parts)]
-    out, held, sems = refs[len(near_parts) + len(far_parts) :]
-    middle = scal[0]
-    length = scal[1]
-
-    def fetch(sources, parts):
-        copies = []
-        for ref, blocks in zip(sources, parts):
-            for first, rows, number in blocks:
-                place = pl.ds(pl.multiple_of(scal[2 + number], 128), rows)
-                copies.append(
-                    pltpu.make_async_copy(
-                        ref.at[first : first + rows, :], held.at[place, :], sems.at[number]
-                    )
+    )(scal, *[r for r, _ in rows_list], *[r for _, r in rows_list], *pieces, cos, sin, gains)
+
+
+def attend_kernel(parts, block, scal, *refs):
+    out, held, sems = refs[len(parts) :]
+    length = scal[0]
+
+    copies = []
+    for ref, blocks in zip(refs, parts):
+        for first, rows, number in blocks:
+            place = pl.ds(pl.multiple_of(scal[1 + number], 128), rows)
+            copies.append(
+                pltpu.make_async_copy(
+                    ref.at[first : first + rows, :], held.at[place, :], sems.at[number]
                 )
-        for copy in copies:
-            copy.start()
-        for copy in copies:
-            copy.wait()
-
-    @pl.when(middle == 1)
-    def _():
-        fetch(near, near_parts)
-
-    @pl.when(middle == 0)
-    def _():
-        fetch(far, far_parts)
+            )
+    for copy in copies:
+        copy.start()
+    for copy in copies:
+        copy.wait()
 
     total = held.shape[0]
     heads = held.shape[1] // ((GQ + 2) * HD)
@@ -248,16 +247,16 @@
                 out[low:high, out_at] = (value / norm).astype(out.dtype)
 
 
-def attend_blocks(near, far, near_parts, far_parts, places, middle, length):
-    rows = sum(n.shape[0] for n in near)
-    columns = near[0].shape[1]
+def attend_blocks(arrays, parts, places, length):
+    rows = sum(a.shape[0] for a in arrays)
+    columns = arrays[0].shape[1]
     wide = columns // (GQ + 2) * GQ
-    scal = jnp.stack([middle, length] + list(places)).astype(jnp.int32)
+    scal = jnp.stack([length] + list(places)).astype(jnp.int32)
     hbm = pl.BlockSpec(memory_space=pltpu.HBM)
     return pl.pallas_call(
-        functools.partial(attend_kernel, near_parts, far_parts, 256),
+        functools.partial(attend_kernel, parts, 256),
         out_shape=jax.ShapeDtypeStruct((rows, wide), jnp.bfloat16),
-        in_specs=[pl.BlockSpec(memory_space=pltpu.SMEM)] + [hbm] * (len(near) + len(far)),
+        in_specs=[pl.BlockSpec(memory_space=pltpu.SMEM)] + [hbm] * len(arrays),
         out_specs=pl.BlockSpec(memory_space=pltpu.VMEM),
         scratch_shapes=[
             pltpu.VMEM((rows, columns), jnp.bfloat16),
@@ -270,7 +269,7 @@
             transcendentals=rows * rows * wide // HD // 2,
         ),
         name="attend",
-    )(scal, *near, *far)
+    )(scal, *arrays)
 
 
 def after(x, *earlier):
@@ -279,12 +278,10 @@
 
 def four_planes(tokens, w_qkv, norm_gain, q_gain, k_gain, lengths):
     t = lax.axis_index("tensor")
-    f = lax.axis_index("fsdp")
     rows = tokens.shape[0]
+    half = rows // 2
     columns = w_qkv.shape[1] // 4
     side = t // 2
-    end = 3 * side
-    mid = 1 + side
     far_end = 3 * (1 - side)
     far_mid = 2 - side
 
@@ -294,37 +291,34 @@
     def across(x, pairs):
         return lax.ppermute(x, "tensor", pairs)
 
-    def beside(x, bit):
-        return lax.ppermute(x, "fsdp", [(i, i ^ bit) for i in range(4)])
-
-    inward = [(0, 1), (3, 2)]
+    def exchange(x, bits):
+        return across(x, [(i, i ^ bits) for i in range(4)])
+
+    def spread(x):
+        return lax.all_gather(x, "fsdp", axis=0, tiled=True)
+
     swap = [(1, 2), (2, 1)]
     far = [(0, 2), (3, 1)]
     outward = [(1, 0), (2, 3)]
 
-    same_e, same_o, other_e, other_o = slab(end), slab(mid), slab(far_end), slab(far_mid)
+    planes = [t] + [jnp.bitwise_xor(t, m) for m in (1, 2, 3)]
+    own, out1, out2, out3 = [slab(p) for p in planes]
     normed = head_norm(tokens.astype(jnp.float32), norm_gain).astype(jnp.bfloat16)
-
-    swap_e = across(other_e, swap)
-    far_e = across(other_e, far)
-    end_e = across(same_e, inward)
-    swap_o = across(after(other_o, swap_e), swap)
-    rows_b = across(after(normed, swap_o), swap)
-    rows_a = across(after(normed, far_e, end_e), inward)
-    far_o = across(after(other_o, far_e, end_e), far)
-    end_o = across(after(same_o, far_o), inward)
-    rows_c = across(rows_a, swap)
-
-    over = []
-    for piece in (same_e, swap_e, far_e, end_e, same_o, swap_o, far_o, end_o):
-        over.append(beside(after(piece, *over[-2:-1]), 2))
-
-    def all_pieces(mine, theirs):
-        return mine + theirs + [beside(x, 1) for x in mine] + [beside(x, 1) for x in theirs]
-
-    end_pieces = all_pieces([same_e, swap_e, far_e, end_e], over[:4])
-    mid_pieces = all_pieces([same_o, swap_o, far_o, end_o], over[4:])
-    scal = jnp.stack([mid, far_mid, far_end, end] + [jnp.bitwise_xor(f, m) for m in (0, 2, 1, 3)])
+    first, second = normed[:half], normed[half:]
+
+    in2, in3, in1 = exchange(out2, 2), exchange(out3, 3), exchange(out1, 1)
+    in1, in2, in3 = lax.optimization_barrier((in1, in2, in3))
+    paired = exchange(normed, 1)
+    swap1 = across(first, swap)
+    swap2 = across(after(second, in1), swap)
+    far1 = across(after(first, in2), far)
+    far2 = across(after(second, in3), far)
+    on1, on2 = across(swap1, outward), across(swap2, outward)
+    on3, on4 = across(far1, outward), across(far2, outward)
+
+    pieces = [spread(x) for x in (own, in1, in2, in3)]
+    middle = jnp.where((t == 1) | (t == 2), 1, 0)
+    scal = jnp.stack(planes + [jnp.int32(m) for m in range(4)] + [middle])
 
     positions = jnp.arange(4 * rows, dtype=jnp.int32)
     angle = angles(positions)
@@ -332,20 +326,23 @@
     sin = jnp.concatenate([-jnp.sin(angle), jnp.sin(angle)], axis=1)
     gains = jnp.stack([q_gain, k_gain])
 
-    blocks = [normed, rows_b, rows_a, rows_c]
-    places = [mid * rows, far_mid * rows, end * rows, far_end * rows]
-
-    def run(picked, pieces):
-        return project(
-            [blocks[i] for i in picked], [places[i] for i in picked], pieces, scal, cos, sin, gains
+    calls = [
+        [((normed, normed), t * rows), ((paired, paired), planes[1] * rows)],
+        [((swap1, on1), far_mid * rows), ((swap2, on2), far_mid * rows + half)],
+        [((far1, on3), far_end * rows), ((far2, on4), far_end * rows + half)],
+    ]
+    made, parts, places = [], [], []
+    for call in calls:
+        listed, first_row = [], 0
+        for (block, _), place in call:
+            listed.append((first_row, block.shape[0], len(places)))
+            first_row += block.shape[0]
+            places.append(place)
+        parts.append(listed)
+        made.append(
+            project([b for b, _ in call], [p for _, p in call], pieces, scal, cos, sin, gains)
         )
-
-    sent = [across(run(picked, end_pieces), outward) for picked in ([0, 1], [2, 3])]
-    near = [run([0, 1, 2, 3], mid_pieces)]
-    near_parts = [[(i * rows, rows, i) for i in range(4)]]
-    far_parts = [[(i * rows, rows, 2 * n + i) for i in range(2)] for n in range(2)]
-    middle = jnp.where((t == 1) | (t == 2), 1, 0)
-    return attend_blocks(near, sent, near_parts, far_parts, places, middle, lengths[0])
+    return attend_blocks(made, parts, places, lengths[0])
 
 
 def solution(mesh):

time: 390 us -> 317 us (0.81)
  the two profiles are of different devices: /device:TPU:0 before, /device:TPU:24 now
where the time goes in v3:
time: 317 us; the launch traced here: 314 us
  waiting for transfers between devices  207 us (65%)
  Pallas kernels  59.7 us (19%)
  starting transfers between devices  18.2 us (6%)
  between operations  14.1 us (4%)
  local copies, waits for them, and re-layouts  7.94 us (3%)
  other arithmetic  7.2 us (2%)
    ppermute x12, waiting for transfers between devices, across(): return lax.ppermute(x, 'tensor', pairs)  205 us
    pallas_call x3, Pallas kernels, project(): pl.pallas_call(functools.partial(project_kernel, counts, sources, tile),...  42.9 us
    ppermute x12, starting transfers between devices, across(): return lax.ppermute(x, 'tensor', pairs)  18 us
    pallas_call x1, Pallas kernels, attend_blocks(): pl.pallas_call(functools.partial(attend_kernel, parts, 256), out_shape=ja...  16.8 us
  transfers between devices with their start and end apart: 16, of which 8 were waited for; matrix products, arithmetic and copies ran while one was open for 2% of the time, Pallas kernels for 10%

profile of v3, /device:TPU:24, one launch (start us, length us, event | category | flops | bytes accessed | tf_op | source)
XLA Modules:
  0.0 313.7 jit_solution(10632375972067556497)
XLA Ops:
  6.5 0.0 all-gather.5.cloned.1.call-start
  6.5 4.1 %constant_dynamic-slice_fusion = (bf16[320,1536]{1,0:T(8,128)(2,1)}, bf16[320,1536]{1,0:T(8,128)(2,1)}, bf16[320,1536]{1,0:T(8,128)(2,1)}, bf16[320,1536]{1,0:T(8,128)(2,1)}) fusion(bf16[320,6144]{1,0:T(8,128)(2,1)} %param.7, s32[]{:T(128)S(6)} %select_n.26, s32[]{:T(128)S(6)} %select_n.24, s32[]{:T(128)S(6)} %select_n.23, s32[]{:T(128)S(6)} %select_n.25), kind=kLoop, calls=%fused_computation.13 | loop fusion | bytes 7864336 | tf_op jit(solution)/shard_map/dynamic_slice | solution.py:289
  10.6 0.0 all-gather.5.cloned.1.call-update
  10.7 0.0 all-gather.7.cloned.1.call-start
  10.7 0.1 collective-permute-start.3
  10.8 0.9 collective-permute-start.1
  11.7 3.5 %collective-permute-start.2 = (bf16[320,1536]{1,0:T(8,128)(2,1)}, bf16[320,1536]{1,0:T(8,128)(2,1)}, u32[]{:S(2)}, u32[]{:S(2)}) collective-permute-start(bf16[320,1536]{1,0:T(8,128)(2,1)} %get-tuple-element.20), channel_id=1, source_target_pairs={{0,2},{1,3},{2,0},{3,1},{4,6},{5,7},{6,4},{7,5},{8,10},{9,11},{10,... | collective-permute-start | bytes 2949128 | tf_op jit(solution)/shard_map/ppermute | solution.py:292
  15.2 22.4 %collective-permute-done.3 = bf16[320,1536]{1,0:T(8,128)(2,1)} collective-permute-done((bf16[320,1536]{1,0:T(8,128)(2,1)}, bf16[320,1536]{1,0:T(8,128)(2,1)}, u32[]{:S(2)}, u32[]{:S(2)}) %collective-permute-start.3) | collective-permute-done | bytes 983072 | tf_op jit(solution)/shard_map/ppermute | solution.py:292
  37.5 19.3 %collective-permute-done.1 = bf16[320,1536]{1,0:T(8,128)(2,1)} collective-permute-done((bf16[320,1536]{1,0:T(8,128)(2,1)}, bf16[320,1536]{1,0:T(8,128)(2,1)}, u32[]{:S(2)}, u32[]{:S(2)}) %collective-permute-start.1) | collective-permute-done | bytes 983072 | tf_op jit(solution)/shard_map/ppermute | solution.py:292
  56.9 40.8 %collective-permute-done.2 = bf16[320,1536]{1,0:T(8,128)(2,1)} collective-permute-done((bf16[320,1536]{1,0:T(8,128)(2,1)}, bf16[320,1536]{1,0:T(8,128)(2,1)}, u32[]{:S(2)}, u32[]{:S(2)}) %collective-permute-start.2) | collective-permute-done | bytes 983072 | tf_op jit(solution)/shard_map/ppermute | solution.py:292
  97.7 0.0 all-gather.7.cloned.1.call-update
  97.7 0.0 all-gather.9.cloned.1.call-start
  97.8 0.7 all-gather.9.cloned.1.call-update
  98.4 0.0 all-gather.11.cloned.1.call-start
  98.5 0.5 all-gather.11.cloned.1.call-update
  99.0 0.0 copy-done.5
  99.0 0.0 copy-start.6
  99.0 0.6 fusion
  99.7 0.0 copy-done.7
  99.7 1.1 copy-done.6
  100.8 0.8 fusion.2.refs_0_.refs_2_
  101.5 0.0 copy-start.8
  101.6 0.0 copy-start.9
  101.6 0.2 fusion.4
  101.7 2.6 collective-permute-start.9
  104.4 2.4 collective-permute-start.8
  106.8 0.0 collective-permute-start
  106.8 1.7 collective-permute-start.4
  108.5 1.7 collective-permute-start.5
  110.2 22.3 %collective-permute-done.9.refs_1_ = bf16[128,5120]{1,0:T(8,128)(2,1)} collective-permute-done((bf16[128,5120]{1,0:T(8,128)(2,1)S(1)}, bf16[128,5120]{1,0:T(8,128)(2,1)}, u32[]{:S(2)}, u32[]{:S(2)}) %collective-permute-start.9) | collective-permute-done | bytes 1310752 | tf_op jit(solution)/shard_map/ppermute | solution.py:292
  132.5 1.3 collective-permute-start.11
  133.7 26.8 %collective-permute-done.8.refs_0_ = bf16[128,5120]{1,0:T(8,128)(2,1)} collective-permute-done((bf16[128,5120]{1,0:T(8,128)(2,1)S(1)}, bf16[128,5120]{1,0:T(8,128)(2,1)}, u32[]{:S(2)}, u32[]{:S(2)}) %collective-permute-start.8) | collective-permute-done | bytes 1310752 | tf_op jit(solution)/shard_map/ppermute | solution.py:292
  160.5 1.3 collective-permute-start.10
  161.9 3.1 %fusion.3 = (f32[1024,64]{1,0:T(8,128)}, f32[1024,64]{1,0:T(8,128)}, f32[1024,64]{1,0:T(8,128)}) fusion(f32[64]{0:T(128)S(1)} %multiply_power_fusion, f32[1024]{0:T(1024)S(1)} %iota_convert_fusion), kind=kLoop, calls=%fused_computation.9 | loop fusion | flops 131072 | bytes 790784 | tf_op jit(solution)/shard_map/neg | solution.py:326
  165.0 0.0 collective-permute-done.4.refs_0_
  165.0 1.3 collective-permute-start.6
  166.3 0.0 collective-permute-done.5.refs_1_
  166.3 1.3 collective-permute-start.7
  167.6 0.0 copy-done.8
  167.6 0.0 copy-done.9
  168.3 0.1 concatenate.22.scal
  168.4 0.1 concatenate.21.scal
  168.5 0.1 concatenate.18.scal
  168.6 0.1 stack.58.scal
  168.7 2.7 pad_maximum_fusion
  171.3 23.4 %collective-permute-done.11.refs_3_ = bf16[128,5120]{1,0:T(8,128)(2,1)} collective-permute-done((bf16[128,5120]{1,0:T(8,128)(2,1)}, bf16[128,5120]{1,0:T(8,128)(2,1)}, u32[]{:S(2)}, u32[]{:S(2)}) %collective-permute-start.11) | collective-permute-done | bytes 1310752 | tf_op jit(solution)/shard_map/ppermute | solution.py:292
  194.8 28.1 %collective-permute-done.10.refs_2_ = bf16[128,5120]{1,0:T(8,128)(2,1)} collective-permute-done((bf16[128,5120]{1,0:T(8,128)(2,1)}, bf16[128,5120]{1,0:T(8,128)(2,1)}, u32[]{:S(2)}, u32[]{:S(2)}) %collective-permute-start.10) | collective-permute-done | bytes 1310752 | tf_op jit(solution)/shard_map/ppermute | solution.py:292
  222.9 0.0 all-gather.11.cloned.1.call-done.refs_7_
  222.9 0.0 copy-start
  222.9 1.0 copy-done
  223.9 12.3 %project.5.refs_2_ = bf16[256,1536]{1,0:T(8,128)(2,1)} custom-call(s32[11]{0:T(128)S(1)} %concatenate.22.scal, bf16[128,5120]{1,0:T(8,128)(2,1)} %collective-permute-done.8.refs_0_, bf16[128,5120]{1,0:T(8,128)(2,1)} %collective-permute-done.9.refs_1_, bf16[128,5120]{1,0:T(8,128)(2,1)} %collective-permute-done.10.refs_2_, ...), custom_call_target="tpu_custom_call" | custom-call | flops 4026531840 | bytes 19136512 | tf_op jit(solution)/shard_map/project/pallas_call | solution.py:157
  236.3 0.0 collective-permute-done.refs_1_.refs_3_
  236.3 0.0 copy-done.1
  236.3 18.2 %project.3.refs_0_ = bf16[512,1536]{1,0:T(8,128)(2,1)} custom-call(s32[11]{0:T(128)S(1)} %concatenate.18.scal, bf16[256,5120]{1,0:T(8,128)(2,1)S(1)} %fusion.2.refs_0_.refs_2_, bf16[256,5120]{1,0:T(8,128)(2,1)} %collective-permute-done.refs_1_.refs_3_, bf16[256,5120]{1,0:T(8,128)(2,1)S(1)} %fusion.2.refs_0_.refs_2_, ...), custom_call_target="tpu_custom_call" | custom-call | flops 8053063680 | bytes 22544384 | tf_op jit(solution)/shard_map/project/pallas_call | solution.py:157
  254.5 0.0 copy-start.2
  254.5 0.0 copy-start.4
  254.5 0.0 collective-permute-done.6.refs_2_
  254.5 22.3 %collective-permute-done.7.refs_3_ = bf16[128,5120]{1,0:T(8,128)(2,1)} collective-permute-done((bf16[128,5120]{1,0:T(8,128)(2,1)}, bf16[128,5120]{1,0:T(8,128)(2,1)}, u32[]{:S(2)}, u32[]{:S(2)}) %collective-permute-start.7) | collective-permute-done | bytes 1310752 | tf_op jit(solution)/shard_map/ppermute | solution.py:292
  276.8 12.3 %project.4.refs_1_ = bf16[256,1536]{1,0:T(8,128)(2,1)} custom-call(s32[11]{0:T(128)S(1)} %concatenate.21.scal, bf16[128,5120]{1,0:T(8,128)(2,1)} %collective-permute-done.4.refs_0_, bf16[128,5120]{1,0:T(8,128)(2,1)} %collective-permute-done.5.refs_1_, bf16[128,5120]{1,0:T(8,128)(2,1)} %collective-permute-done.6.refs_2_, ...), custom_call_target="tpu_custom_call" | custom-call | flops 4026531840 | bytes 19136512 | tf_op jit(solution)/shard_map/project/pallas_call | solution.py:157
  289.2 0.0 copy-done.2
  289.2 0.0 copy-done.4
  289.2 0.0 copy-start.3
  289.2 1.1 copy-done.3
  290.3 16.8 %attend.1 = bf16[1024,1024]{1,0:T(8,128)(2,1)} custom-call(s32[7]{0:T(128)S(1)} %stack.58.scal, bf16[512,1536]{1,0:T(8,128)(2,1)S(1)} %copy-done.4, bf16[256,1536]{1,0:T(8,128)(2,1)S(1)} %copy-done.3, bf16[256,1536]{1,0:T(8,128)(2,1)S(1)} %copy-done.2), custom_call_target="tpu_custom_call" | custom-call | flops 4294967296 | bytes 5242880 | tf_op jit(solution)/shard_map/attend/pallas_call | solution.py:256
  (10 shorter events, 0.0 us)
Async XLA Ops:
  6.5 216.3 %all-gather.5.cloned.1.call-start = ((), (), s32[]{:S(2)}) async-start(), calls=%async_computation | async-start | bytes 4915200 | tf_op jit(solution)/shard_map/all_gather | solution.py:298
  10.6 88.4 %copy-start.5 = (bf16[256,5120]{1,0:T(8,128)(2,1)S(1)}, bf16[256,5120]{1,0:T(8,128)(2,1)}, u32[]{:S(2)}) copy-start(bf16[256,5120]{1,0:T(8,128)(2,1)} %param.6) | copy-start | bytes 7864324
  10.7 212.2 %all-gather.7.cloned.1.call-start = ((), (), s32[]{:S(2)}) async-start(), calls=%async_computation.1 | async-start | bytes 4915200 | tf_op jit(solution)/shard_map/all_gather | solution.py:298
  10.7 26.8 %collective-permute-start.3 = (bf16[320,1536]{1,0:T(8,128)(2,1)}, bf16[320,1536]{1,0:T(8,128)(2,1)}, u32[]{:S(2)}, u32[]{:S(2)}) collective-permute-start(bf16[320,1536]{1,0:T(8,128)(2,1)} %get-tuple-element.17), channel_id=1, source_target_pairs={{0,3},{1,2},{2,1},{3,0},{4,7},{5,6},{6,5},{7,4},{8,11},{9,10},{10,... | collective-permute-start | bytes 2949128 | tf_op jit(solution)/shard_map/ppermute | solution.py:292
  10.8 46.1 %collective-permute-start.1 = (bf16[320,1536]{1,0:T(8,128)(2,1)}, bf16[320,1536]{1,0:T(8,128)(2,1)}, u32[]{:S(2)}, u32[]{:S(2)}) collective-permute-start(bf16[320,1536]{1,0:T(8,128)(2,1)} %get-tuple-element.18), channel_id=1, source_target_pairs={{0,1},{1,0},{2,3},{3,2},{4,5},{5,4},{6,7},{7,6},{8,9},{9,8},{10,11... | collective-permute-start | bytes 2949128 | tf_op jit(solution)/shard_map/ppermute | solution.py:292
  11.7 86.0 %collective-permute-start.2 = (bf16[320,1536]{1,0:T(8,128)(2,1)}, bf16[320,1536]{1,0:T(8,128)(2,1)}, u32[]{:S(2)}, u32[]{:S(2)}) collective-permute-start(bf16[320,1536]{1,0:T(8,128)(2,1)} %get-tuple-element.20), channel_id=1, source_target_pairs={{0,2},{1,3},{2,0},{3,1},{4,6},{5,7},{6,4},{7,5},{8,10},{9,11},{10,... | collective-permute-start | bytes 2949128 | tf_op jit(solution)/shard_map/ppermute | solution.py:292
  97.7 2.0 copy-start.7
  97.7 125.1 %all-gather.9.cloned.1.call-start = ((), (), s32[]{:S(2)}) async-start(), calls=%async_computation.2 | async-start | bytes 4915200 | tf_op jit(solution)/shard_map/all_gather | solution.py:298
  98.4 124.4 %all-gather.11.cloned.1.call-start = ((), (), s32[]{:S(2)}) async-start(), calls=%async_computation.3 | async-start | bytes 4915200 | tf_op jit(solution)/shard_map/all_gather | solution.py:298
  99.0 1.7 copy-start.6
  101.5 66.1 %copy-start.8 = (f32[128]{0:T(128)S(1)}, f32[128]{0:T(128)}, u32[]{:S(2)}) copy-start(f32[128]{0:T(128)} %param.10) | copy-start | bytes 1540
  101.6 66.1 %copy-start.9 = (f32[128]{0:T(128)S(1)}, f32[128]{0:T(128)}, u32[]{:S(2)}) copy-start(f32[128]{0:T(128)} %param.9) | copy-start | bytes 1540
  101.7 30.7 %collective-permute-start.9 = (bf16[128,5120]{1,0:T(8,128)(2,1)S(1)}, bf16[128,5120]{1,0:T(8,128)(2,1)}, u32[]{:S(2)}, u32[]{:S(2)}) collective-permute-start(bf16[128,5120]{1,0:T(8,128)(2,1)S(1)} %get-tuple-element.16), channel_id=1, source_target_pairs={{0,2},{3,1},{4,6},{7,5},{8,10},{11,9},{12,14},{15,13},{16,18},{19,... | collective-permute-start | bytes 3932168 | tf_op jit(solution)/shard_map/ppermute | solution.py:292
  104.4 56.2 %collective-permute-start.8 = (bf16[128,5120]{1,0:T(8,128)(2,1)S(1)}, bf16[128,5120]{1,0:T(8,128)(2,1)}, u32[]{:S(2)}, u32[]{:S(2)}) collective-permute-start(bf16[128,5120]{1,0:T(8,128)(2,1)S(1)} %get-tuple-element.15), channel_id=1, source_target_pairs={{0,2},{3,1},{4,6},{7,5},{8,10},{11,9},{12,14},{15,13},{16,18},{19,... | collective-permute-start | bytes 3932168 | tf_op jit(solution)/shard_map/ppermute | solution.py:292
  106.8 129.5 %collective-permute-start = (bf16[256,5120]{1,0:T(8,128)(2,1)S(1)}, bf16[256,5120]{1,0:T(8,128)(2,1)}, u32[]{:S(2)}, u32[]{:S(2)}) collective-permute-start(bf16[256,5120]{1,0:T(8,128)(2,1)S(1)} %fusion.2.refs_0_.refs_2_), channel_id=1, source_target_pairs={{0,1},{1,0},{2,3},{3,2},{4,5},{5,4},{6,7},{7,6},{8,9},{9,8},{10,11... | collective-permute-start | bytes 7864328 | tf_op jit(solution)/shard_map/ppermute | solution.py:292
  106.8 58.2 %collective-permute-start.4 = (bf16[128,5120]{1,0:T(8,128)(2,1)S(1)}, bf16[128,5120]{1,0:T(8,128)(2,1)}, u32[]{:S(2)}, u32[]{:S(2)}) collective-permute-start(bf16[128,5120]{1,0:T(8,128)(2,1)S(1)} %get-tuple-element.15), channel_id=1, source_target_pairs={{1,2},{2,1},{5,6},{6,5},{9,10},{10,9},{13,14},{14,13},{17,18},{18,... | collective-permute-start | bytes 3932168 | tf_op jit(solution)/shard_map/ppermute | solution.py:292
  108.5 57.8 %collective-permute-start.5 = (bf16[128,5120]{1,0:T(8,128)(2,1)S(1)}, bf16[128,5120]{1,0:T(8,128)(2,1)}, u32[]{:S(2)}, u32[]{:S(2)}) collective-permute-start(bf16[128,5120]{1,0:T(8,128)(2,1)S(1)} %get-tuple-element.16), channel_id=1, source_target_pairs={{1,2},{2,1},{5,6},{6,5},{9,10},{10,9},{13,14},{14,13},{17,18},{18,... | collective-permute-start | bytes 3932168 | tf_op jit(solution)/shard_map/ppermute | solution.py:292
  132.5 62.3 %collective-permute-start.11 = (bf16[128,5120]{1,0:T(8,128)(2,1)}, bf16[128,5120]{1,0:T(8,128)(2,1)}, u32[]{:S(2)}, u32[]{:S(2)}) collective-permute-start(bf16[128,5120]{1,0:T(8,128)(2,1)} %collective-permute-done.9.refs_1_), channel_id=1, source_target_pairs={{1,0},{2,3},{5,4},{6,7},{9,8},{10,11},{13,12},{14,15},{17,16},{18,... | collective-permute-start | bytes 3932168 | tf_op jit(solution)/shard_map/ppermute | solution.py:292
  160.5 62.3 %collective-permute-start.10 = (bf16[128,5120]{1,0:T(8,128)(2,1)}, bf16[128,5120]{1,0:T(8,128)(2,1)}, u32[]{:S(2)}, u32[]{:S(2)}) collective-permute-start(bf16[128,5120]{1,0:T(8,128)(2,1)} %collective-permute-done.8.refs_0_), channel_id=1, source_target_pairs={{1,0},{2,3},{5,4},{6,7},{9,8},{10,11},{13,12},{14,15},{17,16},{18,... | collective-permute-start | bytes 3932168 | tf_op jit(solution)/shard_map/ppermute | solution.py:292
  165.0 89.5 %collective-permute-start.6 = (bf16[128,5120]{1,0:T(8,128)(2,1)}, bf16[128,5120]{1,0:T(8,128)(2,1)}, u32[]{:S(2)}, u32[]{:S(2)}) collective-permute-start(bf16[128,5120]{1,0:T(8,128)(2,1)} %collective-permute-done.4.refs_0_), channel_id=1, source_target_pairs={{1,0},{2,3},{5,4},{6,7},{9,8},{10,11},{13,12},{14,15},{17,16},{18,... | collective-permute-start | bytes 3932168 | tf_op jit(solution)/shard_map/ppermute | solution.py:292
  166.3 110.5 %collective-permute-start.7 = (bf16[128,5120]{1,0:T(8,128)(2,1)}, bf16[128,5120]{1,0:T(8,128)(2,1)}, u32[]{:S(2)}, u32[]{:S(2)}) collective-permute-start(bf16[128,5120]{1,0:T(8,128)(2,1)} %collective-permute-done.5.refs_1_), channel_id=1, source_target_pairs={{1,0},{2,3},{5,4},{6,7},{9,8},{10,11},{13,12},{14,15},{17,16},{18,... | collective-permute-start | bytes 3932168 | tf_op jit(solution)/shard_map/ppermute | solution.py:292
  222.9 1.0 copy-start
  223.9 12.4 %copy-start.1 = (f32[1024,128]{1,0:T(8,128)S(1)}, f32[1024,128]{1,0:T(8,128)}, u32[]{:S(2)}) copy-start(f32[1024,128]{1,0:T(8,128)} %get-tuple-element.27.refs_9_) | copy-start | bytes 1572868
  254.5 34.6 %copy-start.2 = (bf16[256,1536]{1,0:T(8,128)(2,1)S(1)}, bf16[256,1536]{1,0:T(8,128)(2,1)}, u32[]{:S(2)}) copy-start(bf16[256,1536]{1,0:T(8,128)(2,1)} %project.5.refs_2_) | copy-start | bytes 2359300
  254.5 34.6 %copy-start.4 = (bf16[512,1536]{1,0:T(8,128)(2,1)S(1)}, bf16[512,1536]{1,0:T(8,128)(2,1)}, u32[]{:S(2)}) copy-start(bf16[512,1536]{1,0:T(8,128)(2,1)} %project.3.refs_0_) | copy-start | bytes 4718596
  289.2 1.1 copy-start.3
Sparse Core Ops, SparseCore 0:
  10.8 33.9 all-gather.4
  97.8 33.9 all-gather.6
  133.4 32.9 all-gather.8
  167.9 33.0 all-gather.10

commit v4 on v3

--- a/solution.py
+++ b/solution.py
@@ -307,13 +307,14 @@
     first, second = normed[:half], normed[half:]
 
     in2, in3, in1 = exchange(out2, 2), exchange(out3, 3), exchange(out1, 1)
-    in1, in2, in3 = lax.optimization_barrier((in1, in2, in3))
-    paired = exchange(normed, 1)
-    swap1 = across(first, swap)
+    pair1 = exchange(first, 1)
+    in1, in2, in3, pair1 = lax.optimization_barrier((in1, in2, in3, pair1))
+    pair2 = exchange(after(second, in1), 1)
+    swap1 = across(after(first, in1), swap)
     swap2 = across(after(second, in1), swap)
-    far1 = across(after(first, in2), far)
-    far2 = across(after(second, in3), far)
+    far1 = across(after(first, swap1, pair2), far)
     on1, on2 = across(swap1, outward), across(swap2, outward)
+    far2 = across(after(second, swap2, on1), far)
     on3, on4 = across(far1, outward), across(far2, outward)
 
     pieces = [spread(x) for x in (own, in1, in2, in3)]
@@ -327,9 +328,14 @@
     gains = jnp.stack([q_gain, k_gain])
 
     calls = [
-        [((normed, normed), t * rows), ((paired, paired), planes[1] * rows)],
+        [
+            ((normed, normed), t * rows),
+            ((pair1, pair1), planes[1] * rows),
+            ((pair2, pair2), planes[1] * rows + half),
+        ],
         [((swap1, on1), far_mid * rows), ((swap2, on2), far_mid * rows + half)],
-        [((far1, on3), far_end * rows), ((far2, on4), far_end * rows + half)],
+        [((far1, on3), far_end * rows)],
+        [((far2, on4), far_end * rows + half)],
     ]
     made, parts, places = [], [], []
     for call in calls:

time: 317 us -> 327 us (1.032)
  starting transfers between devices: 18.2 us -> 44.9 us
  waiting for transfers between devices: 207 us -> 185 us
  Pallas kernels: 59.7 us -> 66.6 us
  other arithmetic: 7.2 us -> 3.63 us
    ppermute x12 -> x13, starting transfers between devices: 18 us -> 44.7 us  [across(): return lax.ppermute(x, 'tensor', pairs)]
    ppermute x12 -> x13, waiting for transfers between devices: 205 us -> 183 us  [across(): return lax.ppermute(x, 'tensor', pairs)]
    pallas_call x3 -> x4, Pallas kernels: 42.9 us -> 49.5 us  [project(): pl.pallas_call(functools.partial(project_kernel, counts, sources, tile),...]
  transfers between devices with their start and end apart: 16 -> 17, of which waited for: 8 -> 6; matrix products, arithmetic and copies ran while one was open for 2% -> 2% of each run, Pallas kernels for 10% -> 12%
where the time goes in v4:
time: 327 us; the launch traced here: 324 us
  waiting for transfers between devices  185 us (57%)
  Pallas kernels  66.6 us (20%)
  starting transfers between devices  44.9 us (14%)
  between operations  14.1 us (4%)
  local copies, waits for them, and re-layouts  9.91 us (3%)
  other arithmetic  3.63 us (1%)
    ppermute x13, waiting for transfers between devices, across(): return lax.ppermute(x, 'tensor', pairs)  183 us
    pallas_call x4, Pallas kernels, project(): pl.pallas_call(functools.partial(project_kernel, counts, sources, tile),...  49.5 us
    ppermute x13, starting transfers between devices, across(): return lax.ppermute(x, 'tensor', pairs)  44.7 us
    pallas_call x1, Pallas kernels, attend_blocks(): pl.pallas_call(functools.partial(attend_kernel, parts, 256), out_shape=ja...  17.1 us
  transfers between devices with their start and end apart: 17, of which 6 were waited for; matrix products, arithmetic and copies ran while one was open for 2% of the time, Pallas kernels for 12%

profile of v4, /device:TPU:24, one launch (start us, length us, event | category | flops | bytes accessed | tf_op | source)
XLA Modules:
  0.0 323.7 jit_solution(131889230705271613)
XLA Ops:
  6.5 0.0 all-gather.5.cloned.1.call-start
  6.5 4.2 %constant_dynamic-slice_fusion = (bf16[320,1536]{1,0:T(8,128)(2,1)}, bf16[320,1536]{1,0:T(8,128)(2,1)}, bf16[320,1536]{1,0:T(8,128)(2,1)}, bf16[320,1536]{1,0:T(8,128)(2,1)}) fusion(bf16[320,6144]{1,0:T(8,128)(2,1)} %param.7, s32[]{:T(128)S(6)} %select_n.26, s32[]{:T(128)S(6)} %select_n.24, s32[]{:T(128)S(6)} %select_n.23, s32[]{:T(128)S(6)} %select_n.25), kind=kLoop, calls=%fused_computation.13 | loop fusion | bytes 7864336 | tf_op jit(solution)/shard_map/dynamic_slice | solution.py:289
  10.8 0.0 all-gather.5.cloned.1.call-update
  10.8 0.0 all-gather.7.cloned.1.call-start
  10.8 0.0 copy-done.10
  10.8 0.6 fusion
  11.5 0.0 copy-done.13
  11.5 0.8 fusion.2.refs_0_.refs_3_
  12.3 0.0 copy-start.11
  12.3 1.2 fusion.4
  13.5 0.7 copy-done.11
  14.2 0.4 collective-permute-start.3
  14.6 1.6 collective-permute-start
  16.2 0.3 collective-permute-start.1
  16.6 2.5 collective-permute-start.2
  19.0 89.0 %collective-permute-done = bf16[320,1536]{1,0:T(8,128)(2,1)} collective-permute-done((bf16[320,1536]{1,0:T(8,128)(2,1)S(1)}, bf16[320,1536]{1,0:T(8,128)(2,1)}, u32[]{:S(2)}, u32[]{:S(2)}) %collective-permute-start) | collective-permute-done | bytes 983072 | tf_op jit(solution)/shard_map/ppermute | solution.py:292
  108.0 0.0 collective-permute-done.1
  108.0 0.0 collective-permute-done.2
  108.0 0.0 collective-permute-done.3.refs_1_.refs_4_
  108.0 0.0 all-gather.7.cloned.1.call-update
  108.1 0.0 all-gather.9.cloned.1.call-start
  108.1 0.7 all-gather.9.cloned.1.call-update
  108.8 0.0 all-gather.11.cloned.1.call-start
  108.8 0.5 all-gather.11.cloned.1.call-update
  109.4 0.7 collective-permute-start.5
  110.1 0.1 collective-permute-start.4
  110.2 1.7 collective-permute-start.6
  112.0 0.0 collective-permute-done.5.refs_0_
  112.0 1.3 collective-permute-start.7
  113.2 27.9 %collective-permute-done.4.refs_2_.refs_5_ = bf16[128,5120]{1,0:T(8,128)(2,1)S(1)} collective-permute-done((bf16[128,5120]{1,0:T(8,128)(2,1)}, bf16[128,5120]{1,0:T(8,128)(2,1)S(1)}, u32[]{:S(2)}, u32[]{:S(2)}) %collective-permute-start.4) | collective-permute-done | bytes 1310752 | tf_op jit(solution)/shard_map/ppermute | solution.py:292
  141.1 1.1 copy-done.7
  142.2 3.6 %collective-permute-start.9 = (bf16[128,5120]{1,0:T(8,128)(2,1)S(1)}, bf16[128,5120]{1,0:T(8,128)(2,1)}, u32[]{:S(2)}, u32[]{:S(2)}) collective-permute-start(bf16[128,5120]{1,0:T(8,128)(2,1)S(1)} %get-tuple-element.19), channel_id=1, source_target_pairs={{0,2},{3,1},{4,6},{7,5},{8,10},{11,9},{12,14},{15,13},{16,18},{19,... | collective-permute-start | bytes 3932168 | tf_op jit(solution)/shard_map/ppermute | solution.py:292
  145.8 0.0 collective-permute-done.6.refs_1_
  145.8 22.2 %collective-permute-done.7.refs_2_ = bf16[128,5120]{1,0:T(8,128)(2,1)S(1)} collective-permute-done((bf16[128,5120]{1,0:T(8,128)(2,1)S(1)}, bf16[128,5120]{1,0:T(8,128)(2,1)S(1)}, u32[]{:S(2)}, u32[]{:S(2)}) %collective-permute-start.7) | collective-permute-done | bytes 1310752 | tf_op jit(solution)/shard_map/ppermute | solution.py:292
  168.0 1.2 copy-done
  169.1 28.6 %collective-permute-start.11 = (bf16[128,5120]{1,0:T(8,128)(2,1)}, bf16[128,5120]{1,0:T(8,128)(2,1)}, u32[]{:S(2)}, u32[]{:S(2)}) collective-permute-start(bf16[128,5120]{1,0:T(8,128)(2,1)} %get-tuple-element.20), channel_id=1, source_target_pairs={{0,2},{3,1},{4,6},{7,5},{8,10},{11,9},{12,14},{15,13},{16,18},{19,... | collective-permute-start | bytes 3932168 | tf_op jit(solution)/shard_map/ppermute | solution.py:292
  197.8 0.0 collective-permute-done.9.refs_0_
  197.8 1.3 collective-permute-start.10
  199.1 1.3 collective-permute-start.8
  201.0 0.1 concatenate.26.scal
  201.1 0.1 concatenate.27.scal
  201.2 0.1 concatenate.25.scal
  201.3 0.1 concatenate.22.scal
  201.4 0.1 stack.63.scal
  201.5 0.0 copy-done.15
  201.5 1.9 fusion.3
  203.4 0.3 pad_maximum_fusion
  203.8 21.4 %collective-permute-done.11.refs_0_ = bf16[128,5120]{1,0:T(8,128)(2,1)} collective-permute-done((bf16[128,5120]{1,0:T(8,128)(2,1)}, bf16[128,5120]{1,0:T(8,128)(2,1)}, u32[]{:S(2)}, u32[]{:S(2)}) %collective-permute-start.11) | collective-permute-done | bytes 1310752 | tf_op jit(solution)/shard_map/ppermute | solution.py:292
  225.2 1.3 collective-permute-start.12
  226.5 5.2 %collective-permute-done.10.refs_1_ = bf16[128,5120]{1,0:T(8,128)(2,1)} collective-permute-done((bf16[128,5120]{1,0:T(8,128)(2,1)}, bf16[128,5120]{1,0:T(8,128)(2,1)}, u32[]{:S(2)}, u32[]{:S(2)}) %collective-permute-start.10) | collective-permute-done | bytes 1310752 | tf_op jit(solution)/shard_map/ppermute | solution.py:292
  231.7 0.0 all-gather.11.cloned.1.call-done.refs_9_.refs_7_.refs_5_
  231.7 10.4 %project.6.refs_2_ = bf16[128,1536]{1,0:T(8,128)(2,1)} custom-call(s32[10]{0:T(128)S(1)} %concatenate.26.scal, bf16[128,5120]{1,0:T(8,128)(2,1)} %collective-permute-done.9.refs_0_, bf16[128,5120]{1,0:T(8,128)(2,1)} %collective-permute-done.10.refs_1_, bf16[1280,1536]{1,0:T(8,128)(2,1)} %all-gather.5.cloned.1.call-done.refs_6_.refs_4_.refs_2_, ...), custom_call_target="tpu_custom_call" | custom-call | flops 2013265920 | bytes 17432576 | tf_op jit(solution)/shard_map/project/pallas_call | solution.py:157
  242.1 17.6 %collective-permute-done.8.refs_3_ = bf16[128,5120]{1,0:T(8,128)(2,1)} collective-permute-done((bf16[128,5120]{1,0:T(8,128)(2,1)}, bf16[128,5120]{1,0:T(8,128)(2,1)}, u32[]{:S(2)}, u32[]{:S(2)}) %collective-permute-start.8) | collective-permute-done | bytes 1310752 | tf_op jit(solution)/shard_map/ppermute | solution.py:292
  259.7 12.0 %project.5.refs_1_ = bf16[256,1536]{1,0:T(8,128)(2,1)} custom-call(s32[11]{0:T(128)S(1)} %concatenate.25.scal, bf16[128,5120]{1,0:T(8,128)(2,1)S(1)} %collective-permute-done.5.refs_0_, bf16[128,5120]{1,0:T(8,128)(2,1)} %collective-permute-done.6.refs_1_, bf16[128,5120]{1,0:T(8,128)(2,1)S(1)} %copy-done.1, bf16[128,5120]{1,0:T(8,128)(2,1)} %collective-permute-done.8.refs_3_, ...), custom_call_target="tpu_custom_call" | custom-call | flops 4026531840 | bytes 19136512 | tf_op jit(solution)/shard_map/project/pallas_call | solution.py:157
  271.8 0.0 copy-done.6
  271.8 0.0 copy-done.8
  271.8 16.5 %project.4.refs_0_ = bf16[512,1536]{1,0:T(8,128)(2,1)} custom-call(s32[12]{0:T(128)S(1)} %concatenate.22.scal, bf16[256,5120]{1,0:T(8,128)(2,1)} %copy-done.11, bf16[128,5120]{1,0:T(8,128)(2,1)S(1)} %copy-done.6, bf16[128,5120]{1,0:T(8,128)(2,1)S(1)} %copy-done.8, bf16[256,5120]{1,0:T(8,128)(2,1)} %copy-done.11, bf16[128,5120]{1,0:T(8,128)(2,1)S(1)} %copy-done.6, ...), custom_call_target="tpu_custom_call" | custom-call | flops 8053063680 | bytes 22544384 | tf_op jit(solution)/shard_map/project/pallas_call | solution.py:157
  288.3 0.0 copy-start.2
  288.3 0.0 copy-start.3
  288.3 0.0 copy-start.9
  288.3 0.0 collective-permute-done.12.refs_1_
  288.3 10.6 %project.7.refs_3_ = bf16[128,1536]{1,0:T(8,128)(2,1)} custom-call(s32[10]{0:T(128)S(1)} %concatenate.27.scal, bf16[128,5120]{1,0:T(8,128)(2,1)} %collective-permute-done.11.refs_0_, bf16[128,5120]{1,0:T(8,128)(2,1)} %collective-permute-done.12.refs_1_, bf16[1280,1536]{1,0:T(8,128)(2,1)} %all-gather.5.cloned.1.call-done.refs_6_.refs_4_.refs_2_, ...), custom_call_target="tpu_custom_call" | custom-call | flops 2013265920 | bytes 17432576 | tf_op jit(solution)/shard_map/project/pallas_call | solution.py:157
  299.0 1.0 copy-done.4
  300.0 17.1 %attend.1 = bf16[1024,1024]{1,0:T(8,128)(2,1)} custom-call(s32[8]{0:T(128)S(1)} %stack.63.scal, bf16[512,1536]{1,0:T(8,128)(2,1)S(1)} %copy-done.9, bf16[256,1536]{1,0:T(8,128)(2,1)S(1)} %copy-done.2, bf16[128,1536]{1,0:T(8,128)(2,1)S(1)} %copy-done.3, bf16[128,1536]{1,0:T(8,128)(2,1)S(1)} %copy-done.4), custom_call_target="tpu_custom_call" | custom-call | flops 4294967296 | bytes 5242880 | tf_op jit(solution)/shard_map/attend/pallas_call | solution.py:256
  (26 shorter events, 0.1 us)
Async XLA Ops:
  6.5 225.1 %all-gather.5.cloned.1.call-start = ((), (), s32[]{:S(2)}) async-start(), calls=%async_computation | async-start | bytes 4915200 | tf_op jit(solution)/shard_map/all_gather | solution.py:298
  6.5 4.3 %copy-start.10 = (bf16[256,5120]{1,0:T(8,128)(2,1)S(1)}, bf16[256,5120]{1,0:T(8,128)(2,1)}, u32[]{:S(2)}) copy-start(bf16[256,5120]{1,0:T(8,128)(2,1)} %param.6) | copy-start | bytes 7864324
  10.8 0.7 copy-start.13
  10.8 220.9 %all-gather.7.cloned.1.call-start = ((), (), s32[]{:S(2)}) async-start(), calls=%async_computation.1 | async-start | bytes 4915200 | tf_op jit(solution)/shard_map/all_gather | solution.py:298
  12.3 1.9 copy-start.11
  12.3 2.4 copy-start.12
  13.5 188.0 %copy-start.14 = (f32[128]{0:T(128)S(1)}, f32[128]{0:T(128)}, u32[]{:S(2)}) copy-start(f32[128]{0:T(128)} %param.10) | copy-start | bytes 1540
  13.5 188.0 %copy-start.15 = (f32[128]{0:T(128)S(1)}, f32[128]{0:T(128)}, u32[]{:S(2)}) copy-start(f32[128]{0:T(128)} %param.9) | copy-start | bytes 1540
  14.2 93.8 %collective-permute-start.3 = (bf16[128,5120]{1,0:T(8,128)(2,1)S(1)}, bf16[128,5120]{1,0:T(8,128)(2,1)S(1)}, u32[]{:S(2)}, u32[]{:S(2)}) collective-permute-start(bf16[128,5120]{1,0:T(8,128)(2,1)S(1)} %get-tuple-element.19), channel_id=1, source_target_pairs={{0,1},{1,0},{2,3},{3,2},{4,5},{5,4},{6,7},{7,6},{8,9},{9,8},{10,11... | collective-permute-start | bytes 3932168 | tf_op jit(solution)/shard_map/ppermute | solution.py:292
  14.6 93.4 %collective-permute-start = (bf16[320,1536]{1,0:T(8,128)(2,1)S(1)}, bf16[320,1536]{1,0:T(8,128)(2,1)}, u32[]{:S(2)}, u32[]{:S(2)}) collective-permute-start(bf16[320,1536]{1,0:T(8,128)(2,1)S(1)} %copy-done.12), channel_id=1, source_target_pairs={{0,1},{1,0},{2,3},{3,2},{4,5},{5,4},{6,7},{7,6},{8,9},{9,8},{10,11... | collective-permute-start | bytes 2949128 | tf_op jit(solution)/shard_map/ppermute | solution.py:292
  16.2 91.8 %collective-permute-start.1 = (bf16[320,1536]{1,0:T(8,128)(2,1)}, bf16[320,1536]{1,0:T(8,128)(2,1)}, u32[]{:S(2)}, u32[]{:S(2)}) collective-permute-start(bf16[320,1536]{1,0:T(8,128)(2,1)} %get-tuple-element.22), channel_id=1, source_target_pairs={{0,2},{1,3},{2,0},{3,1},{4,6},{5,7},{6,4},{7,5},{8,10},{9,11},{10,... | collective-permute-start | bytes 2949128 | tf_op jit(solution)/shard_map/ppermute | solution.py:292
  16.6 91.5 %collective-permute-start.2 = (bf16[320,1536]{1,0:T(8,128)(2,1)}, bf16[320,1536]{1,0:T(8,128)(2,1)}, u32[]{:S(2)}, u32[]{:S(2)}) collective-permute-start(bf16[320,1536]{1,0:T(8,128)(2,1)} %get-tuple-element.24), channel_id=1, source_target_pairs={{0,3},{1,2},{2,1},{3,0},{4,7},{5,6},{6,5},{7,4},{8,11},{9,10},{10,... | collective-permute-start | bytes 2949128 | tf_op jit(solution)/shard_map/ppermute | solution.py:292
  108.0 1.4 copy-start.5
  108.1 123.6 %all-gather.9.cloned.1.call-start = ((), (), s32[]{:S(2)}) async-start(), calls=%async_computation.2 | async-start | bytes 4915200 | tf_op jit(solution)/shard_map/all_gather | solution.py:298
  108.8 122.9 %all-gather.11.cloned.1.call-start = ((), (), s32[]{:S(2)}) async-start(), calls=%async_computation.3 | async-start | bytes 4915200 | tf_op jit(solution)/shard_map/all_gather | solution.py:298
  109.4 2.6 collective-permute-start.5
  110.1 31.0 %collective-permute-start.4 = (bf16[128,5120]{1,0:T(8,128)(2,1)}, bf16[128,5120]{1,0:T(8,128)(2,1)S(1)}, u32[]{:S(2)}, u32[]{:S(2)}) collective-permute-start(bf16[128,5120]{1,0:T(8,128)(2,1)} %get-tuple-element.20), channel_id=1, source_target_pairs={{0,1},{1,0},{2,3},{3,2},{4,5},{5,4},{6,7},{7,6},{8,9},{9,8},{10,11... | collective-permute-start | bytes 3932168 | tf_op jit(solution)/shard_map/ppermute | solution.py:292
  110.2 35.6 %collective-permute-start.6 = (bf16[128,5120]{1,0:T(8,128)(2,1)}, bf16[128,5120]{1,0:T(8,128)(2,1)}, u32[]{:S(2)}, u32[]{:S(2)}) collective-permute-start(bf16[128,5120]{1,0:T(8,128)(2,1)} %get-tuple-element.20), channel_id=1, source_target_pairs={{1,2},{2,1},{5,6},{6,5},{9,10},{10,9},{13,14},{14,13},{17,18},{18,... | collective-permute-start | bytes 3932168 | tf_op jit(solution)/shard_map/ppermute | solution.py:292
  112.0 56.0 %collective-permute-start.7 = (bf16[128,5120]{1,0:T(8,128)(2,1)S(1)}, bf16[128,5120]{1,0:T(8,128)(2,1)S(1)}, u32[]{:S(2)}, u32[]{:S(2)}) collective-permute-start(bf16[128,5120]{1,0:T(8,128)(2,1)S(1)} %collective-permute-done.5.refs_0_), channel_id=1, source_target_pairs={{1,0},{2,3},{5,4},{6,7},{9,8},{10,11},{13,12},{14,15},{17,16},{18,... | collective-permute-start | bytes 3932168 | tf_op jit(solution)/shard_map/ppermute | solution.py:292
  141.1 1.1 copy-start.7
  142.2 55.5 %collective-permute-start.9 = (bf16[128,5120]{1,0:T(8,128)(2,1)S(1)}, bf16[128,5120]{1,0:T(8,128)(2,1)}, u32[]{:S(2)}, u32[]{:S(2)}) collective-permute-start(bf16[128,5120]{1,0:T(8,128)(2,1)S(1)} %get-tuple-element.19), channel_id=1, source_target_pairs={{0,2},{3,1},{4,6},{7,5},{8,10},{11,9},{12,14},{15,13},{16,18},{19,... | collective-permute-start | bytes 3932168 | tf_op jit(solution)/shard_map/ppermute | solution.py:292
  168.0 1.2 copy-start
  169.1 56.1 %collective-permute-start.11 = (bf16[128,5120]{1,0:T(8,128)(2,1)}, bf16[128,5120]{1,0:T(8,128)(2,1)}, u32[]{:S(2)}, u32[]{:S(2)}) collective-permute-start(bf16[128,5120]{1,0:T(8,128)(2,1)} %get-tuple-element.20), channel_id=1, source_target_pairs={{0,2},{3,1},{4,6},{7,5},{8,10},{11,9},{12,14},{15,13},{16,18},{19,... | collective-permute-start | bytes 3932168 | tf_op jit(solution)/shard_map/ppermute | solution.py:292
  197.8 33.9 %collective-permute-start.10 = (bf16[128,5120]{1,0:T(8,128)(2,1)}, bf16[128,5120]{1,0:T(8,128)(2,1)}, u32[]{:S(2)}, u32[]{:S(2)}) collective-permute-start(bf16[128,5120]{1,0:T(8,128)(2,1)} %collective-permute-done.9.refs_0_), channel_id=1, source_target_pairs={{1,0},{2,3},{5,4},{6,7},{9,8},{10,11},{13,12},{14,15},{17,16},{18,... | collective-permute-start | bytes 3932168 | tf_op jit(solution)/shard_map/ppermute | solution.py:292
  199.1 60.7 %collective-permute-start.8 = (bf16[128,5120]{1,0:T(8,128)(2,1)}, bf16[128,5120]{1,0:T(8,128)(2,1)}, u32[]{:S(2)}, u32[]{:S(2)}) collective-permute-start(bf16[128,5120]{1,0:T(8,128)(2,1)} %collective-permute-done.6.refs_1_), channel_id=1, source_target_pairs={{1,0},{2,3},{5,4},{6,7},{9,8},{10,11},{13,12},{14,15},{17,16},{18,... | collective-permute-start | bytes 3932168 | tf_op jit(solution)/shard_map/ppermute | solution.py:292
  225.2 63.1 %collective-permute-start.12 = (bf16[128,5120]{1,0:T(8,128)(2,1)}, bf16[128,5120]{1,0:T(8,128)(2,1)}, u32[]{:S(2)}, u32[]{:S(2)}) collective-permute-start(bf16[128,5120]{1,0:T(8,128)(2,1)} %collective-permute-done.11.refs_0_), channel_id=1, source_target_pairs={{1,0},{2,3},{5,4},{6,7},{9,8},{10,11},{13,12},{14,15},{17,16},{18,... | collective-permute-start | bytes 3932168 | tf_op jit(solution)/shard_map/ppermute | solution.py:292
  231.7 28.1 %copy-start.1 = (bf16[128,5120]{1,0:T(8,128)(2,1)S(1)}, bf16[128,5120]{1,0:T(8,128)(2,1)}, u32[]{:S(2)}) copy-start(bf16[128,5120]{1,0:T(8,128)(2,1)} %copy-done) | copy-start | bytes 3932164
  242.1 29.7 %copy-start.6 = (bf16[128,5120]{1,0:T(8,128)(2,1)S(1)}, bf16[128,5120]{1,0:T(8,128)(2,1)}, u32[]{:S(2)}) copy-start(bf16[128,5120]{1,0:T(8,128)(2,1)} %copy-done.5) | copy-start | bytes 3932164
  242.1 29.7 %copy-start.8 = (bf16[128,5120]{1,0:T(8,128)(2,1)S(1)}, bf16[128,5120]{1,0:T(8,128)(2,1)}, u32[]{:S(2)}) copy-start(bf16[128,5120]{1,0:T(8,128)(2,1)} %copy-done.7) | copy-start | bytes 3932164
  288.3 10.6 %copy-start.2 = (bf16[256,1536]{1,0:T(8,128)(2,1)S(1)}, bf16[256,1536]{1,0:T(8,128)(2,1)}, u32[]{:S(2)}) copy-start(bf16[256,1536]{1,0:T(8,128)(2,1)} %project.5.refs_1_) | copy-start | bytes 2359300
  288.3 10.6 %copy-start.3 = (bf16[128,1536]{1,0:T(8,128)(2,1)S(1)}, bf16[128,1536]{1,0:T(8,128)(2,1)}, u32[]{:S(2)}) copy-start(bf16[128,1536]{1,0:T(8,128)(2,1)} %project.6.refs_2_) | copy-start | bytes 1179652
  288.3 10.6 %copy-start.9 = (bf16[512,1536]{1,0:T(8,128)(2,1)S(1)}, bf16[512,1536]{1,0:T(8,128)(2,1)}, u32[]{:S(2)}) copy-start(bf16[512,1536]{1,0:T(8,128)(2,1)} %project.4.refs_0_) | copy-start | bytes 4718596
  299.0 1.0 copy-start.4
Sparse Core Ops, SparseCore 0:
  10.9 33.9 all-gather.4
  108.2 33.9 all-gather.6
  143.8 32.9 all-gather.8
  178.2 32.9 all-gather.10

commit v5 on v4

--- a/solution.py
+++ b/solution.py
@@ -309,13 +309,13 @@
     in2, in3, in1 = exchange(out2, 2), exchange(out3, 3), exchange(out1, 1)
     pair1 = exchange(first, 1)
     in1, in2, in3, pair1 = lax.optimization_barrier((in1, in2, in3, pair1))
-    pair2 = exchange(after(second, in1), 1)
     swap1 = across(after(first, in1), swap)
     swap2 = across(after(second, in1), swap)
-    far1 = across(after(first, swap1, pair2), far)
-    on1, on2 = across(swap1, outward), across(swap2, outward)
-    far2 = across(after(second, swap2, on1), far)
-    on3, on4 = across(far1, outward), across(far2, outward)
+    pair2 = exchange(after(second, swap1), 1)
+    far1 = across(after(first, swap1), far)
+    far2 = across(after(second, swap1), far)
+    on1, on2 = across(swap1, outward), across(after(swap2, pair2), outward)
+    on3, on4 = across(after(far1, on1), outward), across(after(far2, on2), outward)
 
     pieces = [spread(x) for x in (own, in1, in2, in3)]
     middle = jnp.where((t == 1) | (t == 2), 1, 0)

time: 327 us -> 329 us (level)
  no operation moved by 1% of the time
where the time goes in v5:
time: 329 us; the launch traced here: 325 us
  waiting for transfers between devices  184 us (56%)
  Pallas kernels  66.8 us (20%)
  starting transfers between devices  46.2 us (14%)
  between operations  14.1 us (4%)
  local copies, waits for them, and re-layouts  10.1 us (3%)
  other arithmetic  3.63 us (1%)
    ppermute x13, waiting for transfers between devices, across(): return lax.ppermute(x, 'tensor', pairs)  183 us
    pallas_call x4, Pallas kernels, project(): pl.pallas_call(functools.partial(project_kernel, counts, sources, tile),...  49.7 us
    ppermute x13, starting transfers between devices, across(): return lax.ppermute(x, 'tensor', pairs)  46.1 us
    pallas_call x1, Pallas kernels, attend_blocks(): pl.pallas_call(functools.partial(attend_kernel, parts, 256), out_shape=ja...  17.1 us
  transfers between devices with their start and end apart: 17, of which 6 were waited for; matrix products, arithmetic and copies ran while one was open for 2% of the time, Pallas kernels for 12%

profile of v5, /device:TPU:24, one launch (start us, length us, event | category | flops | bytes accessed | tf_op | source)
XLA Modules:
  0.0 325.2 jit_solution(9095276343429033863)
XLA Ops:
  6.5 4.2 %constant_dynamic-slice_fusion = (bf16[320,1536]{1,0:T(8,128)(2,1)}, bf16[320,1536]{1,0:T(8,128)(2,1)}, bf16[320,1536]{1,0:T(8,128)(2,1)}, bf16[320,1536]{1,0:T(8,128)(2,1)}) fusion(bf16[320,6144]{1,0:T(8,128)(2,1)} %param.7, s32[]{:T(128)S(6)} %select_n.26, s32[]{:T(128)S(6)} %select_n.24, s32[]{:T(128)S(6)} %select_n.23, s32[]{:T(128)S(6)} %select_n.25), kind=kLoop, calls=%fused_computation.13 | loop fusion | bytes 7864336 | tf_op jit(solution)/shard_map/dynamic_slice | solution.py:289
  10.8 0.0 all-gather.5.cloned.1.call-update
  10.8 0.0 all-gather.7.cloned.1.call-start
  10.8 0.0 copy-done.10
  10.8 0.6 fusion
  11.5 0.0 copy-done.13
  11.5 0.8 fusion.2.refs_0_.refs_3_
  12.3 1.2 fusion.4
  13.5 0.7 copy-done.11
  14.2 0.4 collective-permute-start.3
  14.6 0.0 copy-done.12
  14.6 1.6 collective-permute-start
  16.2 0.3 collective-permute-start.1
  16.6 2.5 collective-permute-start.2
  19.0 89.0 %collective-permute-done = bf16[320,1536]{1,0:T(8,128)(2,1)} collective-permute-done((bf16[320,1536]{1,0:T(8,128)(2,1)S(1)}, bf16[320,1536]{1,0:T(8,128)(2,1)}, u32[]{:S(2)}, u32[]{:S(2)}) %collective-permute-start) | collective-permute-done | bytes 983072 | tf_op jit(solution)/shard_map/ppermute | solution.py:292
  108.0 0.0 collective-permute-done.1
  108.0 0.0 collective-permute-done.2
  108.0 0.0 collective-permute-done.3.refs_1_.refs_4_
  108.0 0.0 all-gather.7.cloned.1.call-update
  108.1 0.0 all-gather.9.cloned.1.call-start
  108.1 0.7 all-gather.9.cloned.1.call-update
  108.8 0.0 all-gather.11.cloned.1.call-start
  108.8 0.3 copy-done.5
  109.1 0.3 all-gather.11.cloned.1.call-update
  109.4 0.7 collective-permute-start.4
  110.1 1.7 collective-permute-start.6
  111.9 0.0 collective-permute-done.4.refs_0_
  111.9 24.6 %collective-permute-start.5 = (bf16[128,5120]{1,0:T(8,128)(2,1)}, bf16[128,5120]{1,0:T(8,128)(2,1)S(1)}, u32[]{:S(2)}, u32[]{:S(2)}) collective-permute-start(bf16[128,5120]{1,0:T(8,128)(2,1)} %get-tuple-element.22), channel_id=1, source_target_pairs={{0,1},{1,0},{2,3},{3,2},{4,5},{5,4},{6,7},{7,6},{8,9},{9,8},{10,11... | collective-permute-start | bytes 3932168 | tf_op jit(solution)/shard_map/ppermute | solution.py:292
  136.5 1.3 collective-permute-start.7
  137.8 6.7 %collective-permute-start.9 = (bf16[128,5120]{1,0:T(8,128)(2,1)S(1)}, bf16[128,5120]{1,0:T(8,128)(2,1)}, u32[]{:S(2)}, u32[]{:S(2)}) collective-permute-start(bf16[128,5120]{1,0:T(8,128)(2,1)S(1)} %get-tuple-element.24), channel_id=1, source_target_pairs={{0,2},{3,1},{4,6},{7,5},{8,10},{11,9},{12,14},{15,13},{16,18},{19,... | collective-permute-start | bytes 3932168 | tf_op jit(solution)/shard_map/ppermute | solution.py:292
  144.5 2.4 collective-permute-start.11
  146.8 0.0 collective-permute-done.6.refs_1_
  146.8 19.4 %collective-permute-done.5.refs_2_.refs_5_ = bf16[128,5120]{1,0:T(8,128)(2,1)S(1)} collective-permute-done((bf16[128,5120]{1,0:T(8,128)(2,1)}, bf16[128,5120]{1,0:T(8,128)(2,1)S(1)}, u32[]{:S(2)}, u32[]{:S(2)}) %collective-permute-start.5) | collective-permute-done | bytes 1310752 | tf_op jit(solution)/shard_map/ppermute | solution.py:292
  166.3 1.1 copy-done.7
  167.4 1.3 collective-permute-start.8
  168.6 25.7 %collective-permute-done.7.refs_2_ = bf16[128,5120]{1,0:T(8,128)(2,1)S(1)} collective-permute-done((bf16[128,5120]{1,0:T(8,128)(2,1)S(1)}, bf16[128,5120]{1,0:T(8,128)(2,1)S(1)}, u32[]{:S(2)}, u32[]{:S(2)}) %collective-permute-start.7) | collective-permute-done | bytes 1310752 | tf_op jit(solution)/shard_map/ppermute | solution.py:292
  194.3 1.1 copy-done
  195.4 0.0 collective-permute-done.9.refs_0_
  195.4 1.3 collective-permute-start.10
  197.4 0.1 concatenate.26.scal
  197.5 0.1 concatenate.27.scal
  197.6 0.1 concatenate.25.scal
  197.6 0.1 concatenate.22.scal
  197.7 0.1 stack.63.scal
  197.8 0.0 copy-done.15
  197.9 1.9 fusion.3
  199.8 0.3 pad_maximum_fusion
  200.1 21.1 %collective-permute-done.11.refs_0_ = bf16[128,5120]{1,0:T(8,128)(2,1)} collective-permute-done((bf16[128,5120]{1,0:T(8,128)(2,1)}, bf16[128,5120]{1,0:T(8,128)(2,1)}, u32[]{:S(2)}, u32[]{:S(2)}) %collective-permute-start.11) | collective-permute-done | bytes 1310752 | tf_op jit(solution)/shard_map/ppermute | solution.py:292
  221.2 1.3 collective-permute-done.8.refs_3_
  222.5 1.3 collective-permute-start.12
  223.8 26.8 %collective-permute-done.10.refs_1_ = bf16[128,5120]{1,0:T(8,128)(2,1)} collective-permute-done((bf16[128,5120]{1,0:T(8,128)(2,1)}, bf16[128,5120]{1,0:T(8,128)(2,1)}, u32[]{:S(2)}, u32[]{:S(2)}) %collective-permute-start.10) | collective-permute-done | bytes 1310752 | tf_op jit(solution)/shard_map/ppermute | solution.py:292
  250.6 0.0 all-gather.11.cloned.1.call-done.refs_9_.refs_7_.refs_5_
  250.7 10.4 %project.6.refs_2_ = bf16[128,1536]{1,0:T(8,128)(2,1)} custom-call(s32[10]{0:T(128)S(1)} %concatenate.26.scal, bf16[128,5120]{1,0:T(8,128)(2,1)} %collective-permute-done.9.refs_0_, bf16[128,5120]{1,0:T(8,128)(2,1)} %collective-permute-done.10.refs_1_, bf16[1280,1536]{1,0:T(8,128)(2,1)} %all-gather.5.cloned.1.call-done.refs_6_.refs_4_.refs_2_, ...), custom_call_target="tpu_custom_call" | custom-call | flops 2013265920 | bytes 17432576 | tf_op jit(solution)/shard_map/project/pallas_call | solution.py:157
  261.1 12.2 %project.5.refs_1_ = bf16[256,1536]{1,0:T(8,128)(2,1)} custom-call(s32[11]{0:T(128)S(1)} %concatenate.25.scal, bf16[128,5120]{1,0:T(8,128)(2,1)S(1)} %collective-permute-done.4.refs_0_, bf16[128,5120]{1,0:T(8,128)(2,1)} %collective-permute-done.6.refs_1_, bf16[128,5120]{1,0:T(8,128)(2,1)S(1)} %copy-done.1, bf16[128,5120]{1,0:T(8,128)(2,1)} %collective-permute-done.8.refs_3_, ...), custom_call_target="tpu_custom_call" | custom-call | flops 4026531840 | bytes 19136512 | tf_op jit(solution)/shard_map/project/pallas_call | solution.py:157
  273.3 16.5 %project.4.refs_0_ = bf16[512,1536]{1,0:T(8,128)(2,1)} custom-call(s32[12]{0:T(128)S(1)} %concatenate.22.scal, bf16[256,5120]{1,0:T(8,128)(2,1)} %copy-done.11, bf16[128,5120]{1,0:T(8,128)(2,1)S(1)} %copy-done.6, bf16[128,5120]{1,0:T(8,128)(2,1)S(1)} %copy-done.8, bf16[256,5120]{1,0:T(8,128)(2,1)} %copy-done.11, bf16[128,5120]{1,0:T(8,128)(2,1)S(1)} %copy-done.6, ...), custom_call_target="tpu_custom_call" | custom-call | flops 8053063680 | bytes 22544384 | tf_op jit(solution)/shard_map/project/pallas_call | solution.py:157
  289.9 0.0 copy-start.9
  289.9 0.0 collective-permute-done.12.refs_1_
  289.9 10.6 %project.7.refs_3_ = bf16[128,1536]{1,0:T(8,128)(2,1)} custom-call(s32[10]{0:T(128)S(1)} %concatenate.27.scal, bf16[128,5120]{1,0:T(8,128)(2,1)} %collective-permute-done.11.refs_0_, bf16[128,5120]{1,0:T(8,128)(2,1)} %collective-permute-done.12.refs_1_, bf16[1280,1536]{1,0:T(8,128)(2,1)} %all-gather.5.cloned.1.call-done.refs_6_.refs_4_.refs_2_, ...), custom_call_target="tpu_custom_call" | custom-call | flops 2013265920 | bytes 17432576 | tf_op jit(solution)/shard_map/project/pallas_call | solution.py:157
  300.5 0.0 copy-done.2
  300.5 0.0 copy-done.3
  300.5 0.0 copy-done.9
  300.5 0.0 copy-start.4
  300.5 1.0 copy-done.4
  301.5 17.1 %attend.1 = bf16[1024,1024]{1,0:T(8,128)(2,1)} custom-call(s32[8]{0:T(128)S(1)} %stack.63.scal, bf16[512,1536]{1,0:T(8,128)(2,1)S(1)} %copy-done.9, bf16[256,1536]{1,0:T(8,128)(2,1)S(1)} %copy-done.2, bf16[128,1536]{1,0:T(8,128)(2,1)S(1)} %copy-done.3, bf16[128,1536]{1,0:T(8,128)(2,1)S(1)} %copy-done.4), custom_call_target="tpu_custom_call" | custom-call | flops 4294967296 | bytes 5242880 | tf_op jit(solution)/shard_map/attend/pallas_call | solution.py:256
  (26 shorter events, 0.1 us)
Async XLA Ops:
  6.5 244.1 %all-gather.5.cloned.1.call-start = ((), (), s32[]{:S(2)}) async-start(), calls=%async_computation | async-start | bytes 4915200 | tf_op jit(solution)/shard_map/all_gather | solution.py:298
  6.5 4.3 %copy-start.10 = (bf16[256,5120]{1,0:T(8,128)(2,1)S(1)}, bf16[256,5120]{1,0:T(8,128)(2,1)}, u32[]{:S(2)}) copy-start(bf16[256,5120]{1,0:T(8,128)(2,1)} %param.6) | copy-start | bytes 7864324
  10.8 0.7 copy-start.13
  10.8 239.8 %all-gather.7.cloned.1.call-start = ((), (), s32[]{:S(2)}) async-start(), calls=%async_computation.1 | async-start | bytes 4915200 | tf_op jit(solution)/shard_map/all_gather | solution.py:298
  12.3 1.9 copy-start.11
  12.3 2.4 copy-start.12
  13.5 184.3 %copy-start.14 = (f32[128]{0:T(128)S(1)}, f32[128]{0:T(128)}, u32[]{:S(2)}) copy-start(f32[128]{0:T(128)} %param.10) | copy-start | bytes 1540
  13.5 184.3 %copy-start.15 = (f32[128]{0:T(128)S(1)}, f32[128]{0:T(128)}, u32[]{:S(2)}) copy-start(f32[128]{0:T(128)} %param.9) | copy-start | bytes 1540
  14.2 93.8 %collective-permute-start.3 = (bf16[128,5120]{1,0:T(8,128)(2,1)S(1)}, bf16[128,5120]{1,0:T(8,128)(2,1)S(1)}, u32[]{:S(2)}, u32[]{:S(2)}) collective-permute-start(bf16[128,5120]{1,0:T(8,128)(2,1)S(1)} %get-tuple-element.24), channel_id=1, source_target_pairs={{0,1},{1,0},{2,3},{3,2},{4,5},{5,4},{6,7},{7,6},{8,9},{9,8},{10,11... | collective-permute-start | bytes 3932168 | tf_op jit(solution)/shard_map/ppermute | solution.py:292
  14.6 93.4 %collective-permute-start = (bf16[320,1536]{1,0:T(8,128)(2,1)S(1)}, bf16[320,1536]{1,0:T(8,128)(2,1)}, u32[]{:S(2)}, u32[]{:S(2)}) collective-permute-start(bf16[320,1536]{1,0:T(8,128)(2,1)S(1)} %copy-done.12), channel_id=1, source_target_pairs={{0,1},{1,0},{2,3},{3,2},{4,5},{5,4},{6,7},{7,6},{8,9},{9,8},{10,11... | collective-permute-start | bytes 2949128 | tf_op jit(solution)/shard_map/ppermute | solution.py:292
  16.2 91.8 %collective-permute-start.1 = (bf16[320,1536]{1,0:T(8,128)(2,1)}, bf16[320,1536]{1,0:T(8,128)(2,1)}, u32[]{:S(2)}, u32[]{:S(2)}) collective-permute-start(bf16[320,1536]{1,0:T(8,128)(2,1)} %get-tuple-element.28), channel_id=1, source_target_pairs={{0,2},{1,3},{2,0},{3,1},{4,6},{5,7},{6,4},{7,5},{8,10},{9,11},{10,... | collective-permute-start | bytes 2949128 | tf_op jit(solution)/shard_map/ppermute | solution.py:292
  16.6 91.5 %collective-permute-start.2 = (bf16[320,1536]{1,0:T(8,128)(2,1)}, bf16[320,1536]{1,0:T(8,128)(2,1)}, u32[]{:S(2)}, u32[]{:S(2)}) collective-permute-start(bf16[320,1536]{1,0:T(8,128)(2,1)} %get-tuple-element.30), channel_id=1, source_target_pairs={{0,3},{1,2},{2,1},{3,0},{4,7},{5,6},{6,5},{7,4},{8,11},{9,10},{10,... | collective-permute-start | bytes 2949128 | tf_op jit(solution)/shard_map/ppermute | solution.py:292
  108.0 1.1 copy-start.5
  108.1 142.6 %all-gather.9.cloned.1.call-start = ((), (), s32[]{:S(2)}) async-start(), calls=%async_computation.2 | async-start | bytes 4915200 | tf_op jit(solution)/shard_map/all_gather | solution.py:298
  108.8 141.8 %all-gather.11.cloned.1.call-start = ((), (), s32[]{:S(2)}) async-start(), calls=%async_computation.3 | async-start | bytes 4915200 | tf_op jit(solution)/shard_map/all_gather | solution.py:298
  109.4 2.5 collective-permute-start.4
  110.1 36.7 %collective-permute-start.6 = (bf16[128,5120]{1,0:T(8,128)(2,1)}, bf16[128,5120]{1,0:T(8,128)(2,1)}, u32[]{:S(2)}, u32[]{:S(2)}) collective-permute-start(bf16[128,5120]{1,0:T(8,128)(2,1)} %get-tuple-element.22), channel_id=1, source_target_pairs={{1,2},{2,1},{5,6},{6,5},{9,10},{10,9},{13,14},{14,13},{17,18},{18,... | collective-permute-start | bytes 3932168 | tf_op jit(solution)/shard_map/ppermute | solution.py:292
  111.9 54.4 %collective-permute-start.5 = (bf16[128,5120]{1,0:T(8,128)(2,1)}, bf16[128,5120]{1,0:T(8,128)(2,1)S(1)}, u32[]{:S(2)}, u32[]{:S(2)}) collective-permute-start(bf16[128,5120]{1,0:T(8,128)(2,1)} %get-tuple-element.22), channel_id=1, source_target_pairs={{0,1},{1,0},{2,3},{3,2},{4,5},{5,4},{6,7},{7,6},{8,9},{9,8},{10,11... | collective-permute-start | bytes 3932168 | tf_op jit(solution)/shard_map/ppermute | solution.py:292
  136.5 57.9 %collective-permute-start.7 = (bf16[128,5120]{1,0:T(8,128)(2,1)S(1)}, bf16[128,5120]{1,0:T(8,128)(2,1)S(1)}, u32[]{:S(2)}, u32[]{:S(2)}) collective-permute-start(bf16[128,5120]{1,0:T(8,128)(2,1)S(1)} %collective-permute-done.4.refs_0_), channel_id=1, source_target_pairs={{1,0},{2,3},{5,4},{6,7},{9,8},{10,11},{13,12},{14,15},{17,16},{18,... | collective-permute-start | bytes 3932168 | tf_op jit(solution)/shard_map/ppermute | solution.py:292
  137.8 57.7 %collective-permute-start.9 = (bf16[128,5120]{1,0:T(8,128)(2,1)S(1)}, bf16[128,5120]{1,0:T(8,128)(2,1)}, u32[]{:S(2)}, u32[]{:S(2)}) collective-permute-start(bf16[128,5120]{1,0:T(8,128)(2,1)S(1)} %get-tuple-element.24), channel_id=1, source_target_pairs={{0,2},{3,1},{4,6},{7,5},{8,10},{11,9},{12,14},{15,13},{16,18},{19,... | collective-permute-start | bytes 3932168 | tf_op jit(solution)/shard_map/ppermute | solution.py:292
  144.5 76.7 %collective-permute-start.11 = (bf16[128,5120]{1,0:T(8,128)(2,1)}, bf16[128,5120]{1,0:T(8,128)(2,1)}, u32[]{:S(2)}, u32[]{:S(2)}) collective-permute-start(bf16[128,5120]{1,0:T(8,128)(2,1)} %get-tuple-element.22), channel_id=1, source_target_pairs={{0,2},{3,1},{4,6},{7,5},{8,10},{11,9},{12,14},{15,13},{16,18},{19,... | collective-permute-start | bytes 3932168 | tf_op jit(solution)/shard_map/ppermute | solution.py:292
  166.3 1.1 copy-start.7
  167.4 55.2 %collective-permute-start.8 = (bf16[128,5120]{1,0:T(8,128)(2,1)}, bf16[128,5120]{1,0:T(8,128)(2,1)}, u32[]{:S(2)}, u32[]{:S(2)}) collective-permute-start(bf16[128,5120]{1,0:T(8,128)(2,1)} %collective-permute-done.6.refs_1_), channel_id=1, source_target_pairs={{1,0},{2,3},{5,4},{6,7},{9,8},{10,11},{13,12},{14,15},{17,16},{18,... | collective-permute-start | bytes 3932168 | tf_op jit(solution)/shard_map/ppermute | solution.py:292
  194.3 1.1 copy-start
  195.4 55.2 %collective-permute-start.10 = (bf16[128,5120]{1,0:T(8,128)(2,1)}, bf16[128,5120]{1,0:T(8,128)(2,1)}, u32[]{:S(2)}, u32[]{:S(2)}) collective-permute-start(bf16[128,5120]{1,0:T(8,128)(2,1)} %collective-permute-done.9.refs_0_), channel_id=1, source_target_pairs={{1,0},{2,3},{5,4},{6,7},{9,8},{10,11},{13,12},{14,15},{17,16},{18,... | collective-permute-start | bytes 3932168 | tf_op jit(solution)/shard_map/ppermute | solution.py:292
  222.5 67.4 %collective-permute-start.12 = (bf16[128,5120]{1,0:T(8,128)(2,1)}, bf16[128,5120]{1,0:T(8,128)(2,1)}, u32[]{:S(2)}, u32[]{:S(2)}) collective-permute-start(bf16[128,5120]{1,0:T(8,128)(2,1)} %collective-permute-done.11.refs_0_), channel_id=1, source_target_pairs={{1,0},{2,3},{5,4},{6,7},{9,8},{10,11},{13,12},{14,15},{17,16},{18,... | collective-permute-start | bytes 3932168 | tf_op jit(solution)/shard_map/ppermute | solution.py:292
  250.7 10.4 %copy-start.1 = (bf16[128,5120]{1,0:T(8,128)(2,1)S(1)}, bf16[128,5120]{1,0:T(8,128)(2,1)}, u32[]{:S(2)}) copy-start(bf16[128,5120]{1,0:T(8,128)(2,1)} %copy-done) | copy-start | bytes 3932164
  261.1 12.3 %copy-start.6 = (bf16[128,5120]{1,0:T(8,128)(2,1)S(1)}, bf16[128,5120]{1,0:T(8,128)(2,1)}, u32[]{:S(2)}) copy-start(bf16[128,5120]{1,0:T(8,128)(2,1)} %copy-done.5) | copy-start | bytes 3932164
  261.1 12.3 %copy-start.8 = (bf16[128,5120]{1,0:T(8,128)(2,1)S(1)}, bf16[128,5120]{1,0:T(8,128)(2,1)}, u32[]{:S(2)}) copy-start(bf16[128,5120]{1,0:T(8,128)(2,1)} %copy-done.7) | copy-start | bytes 3932164
  289.9 10.6 %copy-start.2 = (bf16[256,1536]{1,0:T(8,128)(2,1)S(1)}, bf16[256,1536]{1,0:T(8,128)(2,1)}, u32[]{:S(2)}) copy-start(bf16[256,1536]{1,0:T(8,128)(2,1)} %project.5.refs_1_) | copy-start | bytes 2359300
  289.9 10.6 %copy-start.3 = (bf16[128,1536]{1,0:T(8,128)(2,1)S(1)}, bf16[128,1536]{1,0:T(8,128)(2,1)}, u32[]{:S(2)}) copy-start(bf16[128,1536]{1,0:T(8,128)(2,1)} %project.6.refs_2_) | copy-start | bytes 1179652
  289.9 10.6 %copy-start.9 = (bf16[512,1536]{1,0:T(8,128)(2,1)S(1)}, bf16[512,1536]{1,0:T(8,128)(2,1)}, u32[]{:S(2)}) copy-start(bf16[512,1536]{1,0:T(8,128)(2,1)} %project.4.refs_0_) | copy-start | bytes 4718596
  300.5 1.0 copy-start.4
Sparse Core Ops, SparseCore 0:
  10.9 33.9 all-gather.4
  108.2 33.9 all-gather.6
  143.8 32.9 all-gather.8
  178.2 32.9 all-gather.10

commit v6 on v5

--- a/solution.py
+++ b/solution.py
@@ -122,7 +122,7 @@
             copy.wait()
         total = jnp.dot(taken[...], held[step % 2], preferred_element_type=jnp.float32)
         for number, (first, rows) in enumerate(zip(starts, counts)):
-            place = pl.ds(pl.multiple_of(scal[9 + number], 128), rows)
+            place = pl.ds(pl.multiple_of(scal[9 + number], 16), rows)
             cosine = cos_ref[place, :]
             sine = sin_ref[place, :]
             for head in range(tile // HD):
@@ -186,7 +186,7 @@
     copies = []
     for ref, blocks in zip(refs, parts):
         for first, rows, number in blocks:
-            place = pl.ds(pl.multiple_of(scal[1 + number], 128), rows)
+            place = pl.ds(pl.multiple_of(scal[1 + number], 16), rows)
             copies.append(
                 pltpu.make_async_copy(
                     ref.at[first : first + rows, :], held.at[place, :], sems.at[number]
@@ -307,15 +307,17 @@
     first, second = normed[:half], normed[half:]
 
     in2, in3, in1 = exchange(out2, 2), exchange(out3, 3), exchange(out1, 1)
-    pair1 = exchange(first, 1)
+    pair1 = exchange(normed[: rows // 4], 1)
     in1, in2, in3, pair1 = lax.optimization_barrier((in1, in2, in3, pair1))
     swap1 = across(after(first, in1), swap)
-    swap2 = across(after(second, in1), swap)
-    pair2 = exchange(after(second, swap1), 1)
-    far1 = across(after(first, swap1), far)
-    far2 = across(after(second, swap1), far)
-    on1, on2 = across(swap1, outward), across(after(swap2, pair2), outward)
-    on3, on4 = across(after(far1, on1), outward), across(after(far2, on2), outward)
+    pair2 = exchange(after(normed[rows // 4 : rows // 4 + half], in1), 1)
+    swap2 = across(after(second, swap1, pair2), swap)
+    pair3 = exchange(after(normed[rows // 4 + half :], pair2), 1)
+    on1 = across(swap1, outward)
+    far1 = across(after(first, swap2, on1), far)
+    on2 = across(swap2, outward)
+    far2 = across(after(second, far1, pair3), far)
+    on3, on4 = across(far1, outward), across(after(far2, on2), outward)
 
     pieces = [spread(x) for x in (own, in1, in2, in3)]
     middle = jnp.where((t == 1) | (t == 2), 1, 0)
@@ -331,22 +333,26 @@
         [
             ((normed, normed), t * rows),
             ((pair1, pair1), planes[1] * rows),
-            ((pair2, pair2), planes[1] * rows + half),
+            ((pair2, pair2), planes[1] * rows + rows // 4),
+            ((pair3, pair3), planes[1] * rows + rows // 4 + half),
         ],
         [((swap1, on1), far_mid * rows), ((swap2, on2), far_mid * rows + half)],
         [((far1, on3), far_end * rows)],
         [((far2, on4), far_end * rows + half)],
     ]
     made, parts, places = [], [], []
-    for call in calls:
+    for number, call in enumerate(calls):
         listed, first_row = [], 0
         for (block, _), place in call:
             listed.append((first_row, block.shape[0], len(places)))
             first_row += block.shape[0]
             places.append(place)
         parts.append(listed)
+        arrays = [b for b, _ in call]
+        if number >= 2:
+            arrays = [(after(x, *made[:2]), after(y, *made[:2])) for x, y in arrays]
         made.append(
-            project([b for b, _ in call], [p for _, p in call], pieces, scal, cos, sin, gains)
+            project(arrays, [p for _, p in call], pieces, scal, cos, sin, gains)
         )
     return attend_blocks(made, parts, places, lengths[0])
 

time: 329 us -> 319 us (0.970)
  starting transfers between devices: 46.2 us -> 30.9 us
    ppermute x13 -> x14, starting transfers between devices: 46.1 us -> 30.7 us  [across(): return lax.ppermute(x, 'tensor', pairs)]
    ppermute x13 -> x14, waiting for transfers between devices: 183 us -> 182 us  [across(): return lax.ppermute(x, 'tensor', pairs)]
  transfers between devices with their start and end apart: 17 -> 18, of which waited for: 6 -> 5; matrix products, arithmetic and copies ran while one was open for 2% -> 3% of each run, Pallas kernels for 12% -> 12%
where the time goes in v6:
time: 319 us; the launch traced here: 314 us
  waiting for transfers between devices  183 us (57%)
  Pallas kernels  66.9 us (21%)
  starting transfers between devices  30.9 us (10%)
  between operations  14.2 us (4%)
  local copies, waits for them, and re-layouts  12.7 us (4%)
  other arithmetic  6.42 us (2%)
    ppermute x14, waiting for transfers between devices, across(): return lax.ppermute(x, 'tensor', pairs)  182 us
    pallas_call x4, Pallas kernels, project(): pl.pallas_call(functools.partial(project_kernel, counts, sources, tile),...  49.5 us
    ppermute x14, starting transfers between devices, across(): return lax.ppermute(x, 'tensor', pairs)  30.7 us
    pallas_call x1, Pallas kernels, attend_blocks(): pl.pallas_call(functools.partial(attend_kernel, parts, 256), out_shape=ja...  17.5 us
  transfers between devices with their start and end apart: 18, of which 5 were waited for; matrix products, arithmetic and copies ran while one was open for 3% of the time, Pallas kernels for 12%

profile of v6, /device:TPU:24, one launch (start us, length us, event | category | flops | bytes accessed | tf_op | source)
XLA Modules:
  0.0 314.5 jit_solution(6372331586248595594)
XLA Ops:
  6.5 4.3 %constant_dynamic-slice_fusion = (bf16[320,1536]{1,0:T(8,128)(2,1)}, bf16[320,1536]{1,0:T(8,128)(2,1)}, bf16[320,1536]{1,0:T(8,128)(2,1)}, bf16[320,1536]{1,0:T(8,128)(2,1)}) fusion(bf16[320,6144]{1,0:T(8,128)(2,1)} %param.7, s32[]{:T(128)S(6)} %select_n.26, s32[]{:T(128)S(6)} %select_n.24, s32[]{:T(128)S(6)} %select_n.23, s32[]{:T(128)S(6)} %select_n.25), kind=kLoop, calls=%fused_computation.13 | loop fusion | bytes 7864336 | tf_op jit(solution)/shard_map/dynamic_slice | solution.py:289
  10.8 0.0 all-gather.5.cloned.1.call-update
  10.8 0.0 all-gather.7.cloned.1.call-start
  10.9 0.0 copy-start.12
  10.9 0.5 collective-permute-start
  11.4 0.0 collective-permute-start.1
  11.4 3.9 %collective-permute-start.2 = (bf16[320,1536]{1,0:T(8,128)(2,1)}, bf16[320,1536]{1,0:T(8,128)(2,1)}, u32[]{:S(2)}, u32[]{:S(2)}) collective-permute-start(bf16[320,1536]{1,0:T(8,128)(2,1)} %get-tuple-element.38), channel_id=1, source_target_pairs={{0,3},{1,2},{2,1},{3,0},{4,7},{5,6},{6,5},{7,4},{8,11},{9,10},{10,... | collective-permute-start | bytes 2949128 | tf_op jit(solution)/shard_map/ppermute | solution.py:292
  15.4 0.6 fusion
  16.0 0.8 fusion.2.refs_0_.refs_4_
  16.8 1.0 fusion.5
  17.8 0.0 collective-permute-start.3
  17.8 73.0 %collective-permute-done.3.refs_1_.refs_5_ = bf16[64,5120]{1,0:T(8,128)(2,1)S(1)} collective-permute-done((bf16[64,5120]{1,0:T(8,128)(2,1)S(1)}, bf16[64,5120]{1,0:T(8,128)(2,1)S(1)}, u32[]{:S(2)}, u32[]{:S(2)}) %collective-permute-start.3) | collective-permute-done | bytes 655392 | tf_op jit(solution)/shard_map/ppermute | solution.py:292
  90.8 0.0 collective-permute-done
  90.8 0.0 collective-permute-done.1
  90.9 0.0 collective-permute-done.2
  90.9 0.0 all-gather.7.cloned.1.call-update
  90.9 0.0 all-gather.9.cloned.1.call-start
  90.9 0.7 all-gather.9.cloned.1.call-update
  91.6 0.0 all-gather.11.cloned.1.call-start
  91.7 0.5 all-gather.11.cloned.1.call-update
  92.2 0.0 copy-start.15
  92.2 0.0 copy-start.16
  92.2 1.5 fusion.4
  93.8 8.8 %collective-permute-start.4 = (bf16[128,5120]{1,0:T(8,128)(2,1)S(1)}, bf16[128,5120]{1,0:T(8,128)(2,1)S(1)}, u32[]{:S(2)}, u32[]{:S(2)}) collective-permute-start(bf16[128,5120]{1,0:T(8,128)(2,1)S(1)} %get-tuple-element.22), channel_id=1, source_target_pairs={{0,1},{1,0},{2,3},{3,2},{4,5},{5,4},{6,7},{7,6},{8,9},{9,8},{10,11... | collective-permute-start | bytes 3932168 | tf_op jit(solution)/shard_map/ppermute | solution.py:292
  102.6 0.7 collective-permute-start.6
  103.3 26.9 %collective-permute-done.4.refs_2_.refs_6_ = bf16[128,5120]{1,0:T(8,128)(2,1)S(1)} collective-permute-done((bf16[128,5120]{1,0:T(8,128)(2,1)S(1)}, bf16[128,5120]{1,0:T(8,128)(2,1)S(1)}, u32[]{:S(2)}, u32[]{:S(2)}) %collective-permute-start.4) | collective-permute-done | bytes 1310752 | tf_op jit(solution)/shard_map/ppermute | solution.py:292
  130.2 1.1 copy-done.5
  131.3 0.0 collective-permute-done.6.refs_0_
  131.3 1.7 collective-permute-start.7
  133.1 1.3 collective-permute-start.8
  134.3 0.0 collective-permute-done.7.refs_1_
  134.3 29.6 %collective-permute-done.8.refs_2_ = bf16[128,5120]{1,0:T(8,128)(2,1)S(1)} collective-permute-done((bf16[128,5120]{1,0:T(8,128)(2,1)S(1)}, bf16[128,5120]{1,0:T(8,128)(2,1)S(1)}, u32[]{:S(2)}, u32[]{:S(2)}) %collective-permute-start.8) | collective-permute-done | bytes 1310752 | tf_op jit(solution)/shard_map/ppermute | solution.py:292
  164.0 1.1 copy-done
  165.1 3.6 %collective-permute-start.10 = (bf16[128,5120]{1,0:T(8,128)(2,1)S(1)}, bf16[128,5120]{1,0:T(8,128)(2,1)}, u32[]{:S(2)}, u32[]{:S(2)}) collective-permute-start(bf16[128,5120]{1,0:T(8,128)(2,1)S(1)} %get-tuple-element.28), channel_id=1, source_target_pairs={{0,2},{3,1},{4,6},{7,5},{8,10},{11,9},{12,14},{15,13},{16,18},{19,... | collective-permute-start | bytes 3932168 | tf_op jit(solution)/shard_map/ppermute | solution.py:292
  168.7 0.0 collective-permute-start.5
  168.7 1.3 collective-permute-start.9
  170.0 36.7 %collective-permute-done.5.refs_3_.refs_7_ = bf16[64,5120]{1,0:T(8,128)(2,1)S(1)} collective-permute-done((bf16[64,5120]{1,0:T(8,128)(2,1)S(1)}, bf16[64,5120]{1,0:T(8,128)(2,1)S(1)}, u32[]{:S(2)}, u32[]{:S(2)}) %collective-permute-start.5) | collective-permute-done | bytes 655392 | tf_op jit(solution)/shard_map/ppermute | solution.py:292
  206.7 0.8 copy-done.7
  207.5 0.0 collective-permute-done.10.refs_0_
  207.5 6.3 %collective-permute-start.12 = (bf16[128,5120]{1,0:T(8,128)(2,1)}, bf16[128,5120]{1,0:T(8,128)(2,1)}, u32[]{:S(2)}, u32[]{:S(2)}) collective-permute-start(bf16[128,5120]{1,0:T(8,128)(2,1)} %get-tuple-element.31), channel_id=1, source_target_pairs={{0,2},{3,1},{4,6},{7,5},{8,10},{11,9},{12,14},{15,13},{16,18},{19,... | collective-permute-start | bytes 3932168 | tf_op jit(solution)/shard_map/ppermute | solution.py:292
  213.8 3.2 %fusion.3 = (f32[1024,64]{1,0:T(8,128)}, f32[1024,64]{1,0:T(8,128)}, f32[1024,64]{1,0:T(8,128)}) fusion(f32[64]{0:T(128)S(1)} %multiply_power_fusion, f32[1024]{0:T(1024)S(1)} %iota_convert_fusion), kind=kLoop, calls=%fused_computation.9 | loop fusion | flops 131072 | bytes 790784 | tf_op jit(solution)/shard_map/neg | solution.py:329
  217.0 1.3 collective-permute-start.11
  219.0 0.1 concatenate.26.scal
  219.1 0.1 concatenate.27.scal
  219.2 0.1 concatenate.25.scal
  219.2 0.1 concatenate.22.scal
  219.3 0.1 stack.68.scal
  219.4 1.9 pad_maximum_fusion
  221.3 0.0 collective-permute-done.9.refs_3_
  221.3 15.8 %collective-permute-done.12.refs_0_ = bf16[128,5120]{1,0:T(8,128)(2,1)} collective-permute-done((bf16[128,5120]{1,0:T(8,128)(2,1)}, bf16[128,5120]{1,0:T(8,128)(2,1)}, u32[]{:S(2)}, u32[]{:S(2)}) %collective-permute-start.12) | collective-permute-done | bytes 1310752 | tf_op jit(solution)/shard_map/ppermute | solution.py:292
  237.1 1.3 collective-permute-start.13
  238.4 0.0 all-gather.5.cloned.1.call-done.refs_8_.refs_4_.refs_2_
  238.5 0.0 all-gather.7.cloned.1.call-done.refs_9_.refs_5_.refs_3_
  238.5 0.0 all-gather.9.cloned.1.call-done.refs_10_.refs_6_.refs_4_
  238.5 0.0 all-gather.11.cloned.1.call-done.refs_11_.refs_7_.refs_5_
  238.6 1.3 copy-done.1
  239.9 12.0 %project.5.refs_1_ = bf16[256,1536]{1,0:T(8,128)(2,1)} custom-call(s32[11]{0:T(128)S(1)} %concatenate.25.scal, bf16[128,5120]{1,0:T(8,128)(2,1)S(1)} %collective-permute-done.6.refs_0_, bf16[128,5120]{1,0:T(8,128)(2,1)} %collective-permute-done.7.refs_1_, bf16[128,5120]{1,0:T(8,128)(2,1)S(1)} %copy-done.1, bf16[128,5120]{1,0:T(8,128)(2,1)} %collective-permute-done.9.refs_3_, ...), custom_call_target="tpu_custom_call" | custom-call | flops 4026531840 | bytes 19136512 | tf_op jit(solution)/shard_map/project/pallas_call | solution.py:157
  251.9 16.5 %project.4.refs_0_ = bf16[512,1536]{1,0:T(8,128)(2,1)} custom-call(s32[13]{0:T(128)S(1)} %concatenate.22.scal, bf16[256,5120]{1,0:T(8,128)(2,1)} %copy-done.10, bf16[64,5120]{1,0:T(8,128)(2,1)S(1)} %collective-permute-done.3.refs_1_.refs_5_, bf16[128,5120]{1,0:T(8,128)(2,1)S(1)} %copy-done.6, bf16[64,5120]{1,0:T(8,128)(2,1)S(1)} %copy-done.8, ...), custom_call_target="tpu_custom_call" | custom-call | flops 8053063680 | bytes 22544384 | tf_op jit(solution)/shard_map/project/pallas_call | solution.py:157
  268.4 0.0 collective-permute-done.11.refs_1_
  268.4 10.4 %project.6.refs_2_ = bf16[128,1536]{1,0:T(8,128)(2,1)} custom-call(s32[10]{0:T(128)S(1)} %concatenate.26.scal, bf16[128,5120]{1,0:T(8,128)(2,1)} %collective-permute-done.10.refs_0_, bf16[128,5120]{1,0:T(8,128)(2,1)} %collective-permute-done.11.refs_1_, bf16[1280,1536]{1,0:T(8,128)(2,1)} %all-gather.5.cloned.1.call-done.refs_8_.refs_4_.refs_2_, ...), custom_call_target="tpu_custom_call" | custom-call | flops 2013265920 | bytes 17432576 | tf_op jit(solution)/shard_map/project/pallas_call | solution.py:157
  278.8 0.0 copy-start.9
  278.8 10.6 %project.7.refs_3_ = bf16[128,1536]{1,0:T(8,128)(2,1)} custom-call(s32[10]{0:T(128)S(1)} %concatenate.27.scal, bf16[128,5120]{1,0:T(8,128)(2,1)} %collective-permute-done.12.refs_0_, bf16[128,5120]{1,0:T(8,128)(2,1)} %collective-permute-done.13.refs_1_, bf16[1280,1536]{1,0:T(8,128)(2,1)} %all-gather.5.cloned.1.call-done.refs_8_.refs_4_.refs_2_, ...), custom_call_target="tpu_custom_call" | custom-call | flops 2013265920 | bytes 17432576 | tf_op jit(solution)/shard_map/project/pallas_call | solution.py:157
  289.5 1.0 copy-done.4
  290.5 17.5 %attend.1 = bf16[1024,1024]{1,0:T(8,128)(2,1)} custom-call(s32[9]{0:T(128)S(1)} %stack.68.scal, bf16[512,1536]{1,0:T(8,128)(2,1)S(1)} %copy-done.9, bf16[256,1536]{1,0:T(8,128)(2,1)S(1)} %copy-done.2, bf16[128,1536]{1,0:T(8,128)(2,1)S(1)} %copy-done.3, bf16[128,1536]{1,0:T(8,128)(2,1)S(1)} %copy-done.4), custom_call_target="tpu_custom_call" | custom-call | flops 4294967296 | bytes 5242880 | tf_op jit(solution)/shard_map/attend/pallas_call | solution.py:256
  (31 shorter events, 0.1 us)
Async XLA Ops:
  6.5 231.9 %all-gather.5.cloned.1.call-start = ((), (), s32[]{:S(2)}) async-start(), calls=%async_computation | async-start | bytes 4915200 | tf_op jit(solution)/shard_map/all_gather | solution.py:298
  6.5 8.8 %copy-start.11 = (bf16[256,5120]{1,0:T(8,128)(2,1)S(1)}, bf16[256,5120]{1,0:T(8,128)(2,1)}, u32[]{:S(2)}) copy-start(bf16[256,5120]{1,0:T(8,128)(2,1)} %param.6) | copy-start | bytes 7864324
  10.8 5.2 %copy-start.14 = (f32[5120]{0:T(1024)S(1)}, f32[5120]{0:T(1024)}, u32[]{:S(2)}) copy-start(f32[5120]{0:T(1024)} %param.8) | copy-start | bytes 61444
  10.8 227.6 %all-gather.7.cloned.1.call-start = ((), (), s32[]{:S(2)}) async-start(), calls=%async_computation.1 | async-start | bytes 4915200 | tf_op jit(solution)/shard_map/all_gather | solution.py:298
  10.9 5.1 %copy-start.12 = (bf16[256,5120]{1,0:T(8,128)(2,1)S(1)}, bf16[256,5120]{1,0:T(8,128)(2,1)}, u32[]{:S(2)}) copy-start(bf16[256,5120]{1,0:T(8,128)(2,1)} %param.6) | copy-start | bytes 7864324
  10.9 80.0 %collective-permute-start = (bf16[320,1536]{1,0:T(8,128)(2,1)}, bf16[320,1536]{1,0:T(8,128)(2,1)}, u32[]{:S(2)}, u32[]{:S(2)}) collective-permute-start(bf16[320,1536]{1,0:T(8,128)(2,1)} %get-tuple-element.37), channel_id=1, source_target_pairs={{0,1},{1,0},{2,3},{3,2},{4,5},{5,4},{6,7},{7,6},{8,9},{9,8},{10,11... | collective-permute-start | bytes 2949128 | tf_op jit(solution)/shard_map/ppermute | solution.py:292
  11.4 79.4 %collective-permute-start.1 = (bf16[320,1536]{1,0:T(8,128)(2,1)}, bf16[320,1536]{1,0:T(8,128)(2,1)}, u32[]{:S(2)}, u32[]{:S(2)}) collective-permute-start(bf16[320,1536]{1,0:T(8,128)(2,1)} %get-tuple-element.36), channel_id=1, source_target_pairs={{0,2},{1,3},{2,0},{3,1},{4,6},{5,7},{6,4},{7,5},{8,10},{9,11},{10,... | collective-permute-start | bytes 2949128 | tf_op jit(solution)/shard_map/ppermute | solution.py:292
  11.4 79.4 %collective-permute-start.2 = (bf16[320,1536]{1,0:T(8,128)(2,1)}, bf16[320,1536]{1,0:T(8,128)(2,1)}, u32[]{:S(2)}, u32[]{:S(2)}) collective-permute-start(bf16[320,1536]{1,0:T(8,128)(2,1)} %get-tuple-element.38), channel_id=1, source_target_pairs={{0,3},{1,2},{2,1},{3,0},{4,7},{5,6},{6,5},{7,4},{8,11},{9,10},{10,... | collective-permute-start | bytes 2949128 | tf_op jit(solution)/shard_map/ppermute | solution.py:292
  16.7 75.4 %copy-start.10 = (bf16[256,5120]{1,0:T(8,128)(2,1)}, bf16[256,5120]{1,0:T(8,128)(2,1)S(1)}, u32[]{:S(2)}) copy-start(bf16[256,5120]{1,0:T(8,128)(2,1)S(1)} %fusion.2.refs_0_.refs_4_) | copy-start | bytes 7864324
  17.8 73.0 %collective-permute-start.3 = (bf16[64,5120]{1,0:T(8,128)(2,1)S(1)}, bf16[64,5120]{1,0:T(8,128)(2,1)S(1)}, u32[]{:S(2)}, u32[]{:S(2)}) collective-permute-start(bf16[64,5120]{1,0:T(8,128)(2,1)S(1)} %get-tuple-element.43), channel_id=1, source_target_pairs={{0,1},{1,0},{2,3},{3,2},{4,5},{5,4},{6,7},{7,6},{8,9},{9,8},{10,11... | collective-permute-start | bytes 1966088 | tf_op jit(solution)/shard_map/ppermute | solution.py:292
  90.9 147.6 %all-gather.9.cloned.1.call-start = ((), (), s32[]{:S(2)}) async-start(), calls=%async_computation.2 | async-start | bytes 4915200 | tf_op jit(solution)/shard_map/all_gather | solution.py:298
  91.6 146.9 %all-gather.11.cloned.1.call-start = ((), (), s32[]{:S(2)}) async-start(), calls=%async_computation.3 | async-start | bytes 4915200 | tf_op jit(solution)/shard_map/all_gather | solution.py:298
  92.2 76.5 %copy-start.13 = (bf16[64,5120]{1,0:T(8,128)(2,1)S(1)}, bf16[64,5120]{1,0:T(8,128)(2,1)}, u32[]{:S(2)}) copy-start(bf16[64,5120]{1,0:T(8,128)(2,1)} %get-tuple-element.23) | copy-start | bytes 1966084
  92.2 126.1 %copy-start.15 = (f32[128]{0:T(128)S(1)}, f32[128]{0:T(128)}, u32[]{:S(2)}) copy-start(f32[128]{0:T(128)} %param.10) | copy-start | bytes 1540
  92.2 126.1 %copy-start.16 = (f32[128]{0:T(128)S(1)}, f32[128]{0:T(128)}, u32[]{:S(2)}) copy-start(f32[128]{0:T(128)} %param.9) | copy-start | bytes 1540
  93.8 36.5 %collective-permute-start.4 = (bf16[128,5120]{1,0:T(8,128)(2,1)S(1)}, bf16[128,5120]{1,0:T(8,128)(2,1)S(1)}, u32[]{:S(2)}, u32[]{:S(2)}) collective-permute-start(bf16[128,5120]{1,0:T(8,128)(2,1)S(1)} %get-tuple-element.22), channel_id=1, source_target_pairs={{0,1},{1,0},{2,3},{3,2},{4,5},{5,4},{6,7},{7,6},{8,9},{9,8},{10,11... | collective-permute-start | bytes 3932168 | tf_op jit(solution)/shard_map/ppermute | solution.py:292
  102.6 28.7 %collective-permute-start.6 = (bf16[128,5120]{1,0:T(8,128)(2,1)S(1)}, bf16[128,5120]{1,0:T(8,128)(2,1)S(1)}, u32[]{:S(2)}, u32[]{:S(2)}) collective-permute-start(bf16[128,5120]{1,0:T(8,128)(2,1)S(1)} %get-tuple-element.28), channel_id=1, source_target_pairs={{1,2},{2,1},{5,6},{6,5},{9,10},{10,9},{13,14},{14,13},{17,18},{18,... | collective-permute-start | bytes 3932168 | tf_op jit(solution)/shard_map/ppermute | solution.py:292
  130.2 1.1 copy-start.5
  131.3 3.0 collective-permute-start.7
  133.1 30.9 %collective-permute-start.8 = (bf16[128,5120]{1,0:T(8,128)(2,1)S(1)}, bf16[128,5120]{1,0:T(8,128)(2,1)S(1)}, u32[]{:S(2)}, u32[]{:S(2)}) collective-permute-start(bf16[128,5120]{1,0:T(8,128)(2,1)S(1)} %collective-permute-done.6.refs_0_), channel_id=1, source_target_pairs={{1,0},{2,3},{5,4},{6,7},{9,8},{10,11},{13,12},{14,15},{17,16},{18,... | collective-permute-start | bytes 3932168 | tf_op jit(solution)/shard_map/ppermute | solution.py:292
  164.0 1.1 copy-start
  165.1 42.4 %collective-permute-start.10 = (bf16[128,5120]{1,0:T(8,128)(2,1)S(1)}, bf16[128,5120]{1,0:T(8,128)(2,1)}, u32[]{:S(2)}, u32[]{:S(2)}) collective-permute-start(bf16[128,5120]{1,0:T(8,128)(2,1)S(1)} %get-tuple-element.28), channel_id=1, source_target_pairs={{0,2},{3,1},{4,6},{7,5},{8,10},{11,9},{12,14},{15,13},{16,18},{19,... | collective-permute-start | bytes 3932168 | tf_op jit(solution)/shard_map/ppermute | solution.py:292
  168.7 38.0 %collective-permute-start.5 = (bf16[64,5120]{1,0:T(8,128)(2,1)S(1)}, bf16[64,5120]{1,0:T(8,128)(2,1)S(1)}, u32[]{:S(2)}, u32[]{:S(2)}) collective-permute-start(bf16[64,5120]{1,0:T(8,128)(2,1)S(1)} %copy-done.13), channel_id=1, source_target_pairs={{0,1},{1,0},{2,3},{3,2},{4,5},{5,4},{6,7},{7,6},{8,9},{9,8},{10,11... | collective-permute-start | bytes 1966088 | tf_op jit(solution)/shard_map/ppermute | solution.py:292
  168.7 52.6 %collective-permute-start.9 = (bf16[128,5120]{1,0:T(8,128)(2,1)}, bf16[128,5120]{1,0:T(8,128)(2,1)}, u32[]{:S(2)}, u32[]{:S(2)}) collective-permute-start(bf16[128,5120]{1,0:T(8,128)(2,1)} %collective-permute-done.7.refs_1_), channel_id=1, source_target_pairs={{1,0},{2,3},{5,4},{6,7},{9,8},{10,11},{13,12},{14,15},{17,16},{18,... | collective-permute-start | bytes 3932168 | tf_op jit(solution)/shard_map/ppermute | solution.py:292
  206.7 0.8 copy-start.7
  207.5 29.7 %collective-permute-start.12 = (bf16[128,5120]{1,0:T(8,128)(2,1)}, bf16[128,5120]{1,0:T(8,128)(2,1)}, u32[]{:S(2)}, u32[]{:S(2)}) collective-permute-start(bf16[128,5120]{1,0:T(8,128)(2,1)} %get-tuple-element.31), channel_id=1, source_target_pairs={{0,2},{3,1},{4,6},{7,5},{8,10},{11,9},{12,14},{15,13},{16,18},{19,... | collective-permute-start | bytes 3932168 | tf_op jit(solution)/shard_map/ppermute | solution.py:292
  217.0 51.4 %collective-permute-start.11 = (bf16[128,5120]{1,0:T(8,128)(2,1)}, bf16[128,5120]{1,0:T(8,128)(2,1)}, u32[]{:S(2)}, u32[]{:S(2)}) collective-permute-start(bf16[128,5120]{1,0:T(8,128)(2,1)} %collective-permute-done.10.refs_0_), channel_id=1, source_target_pairs={{1,0},{2,3},{5,4},{6,7},{9,8},{10,11},{13,12},{14,15},{17,16},{18,... | collective-permute-start | bytes 3932168 | tf_op jit(solution)/shard_map/ppermute | solution.py:292
  237.1 41.7 %collective-permute-start.13 = (bf16[128,5120]{1,0:T(8,128)(2,1)}, bf16[128,5120]{1,0:T(8,128)(2,1)}, u32[]{:S(2)}, u32[]{:S(2)}) collective-permute-start(bf16[128,5120]{1,0:T(8,128)(2,1)} %collective-permute-done.12.refs_0_), channel_id=1, source_target_pairs={{1,0},{2,3},{5,4},{6,7},{9,8},{10,11},{13,12},{14,15},{17,16},{18,... | collective-permute-start | bytes 3932168 | tf_op jit(solution)/shard_map/ppermute | solution.py:292
  238.5 1.3 copy-start.1
  239.9 12.0 %copy-start.6 = (bf16[128,5120]{1,0:T(8,128)(2,1)S(1)}, bf16[128,5120]{1,0:T(8,128)(2,1)}, u32[]{:S(2)}) copy-start(bf16[128,5120]{1,0:T(8,128)(2,1)} %copy-done.5) | copy-start | bytes 3932164
  239.9 12.0 %copy-start.8 = (bf16[64,5120]{1,0:T(8,128)(2,1)S(1)}, bf16[64,5120]{1,0:T(8,128)(2,1)}, u32[]{:S(2)}) copy-start(bf16[64,5120]{1,0:T(8,128)(2,1)} %copy-done.7) | copy-start | bytes 1966084
  278.8 10.6 %copy-start.2 = (bf16[256,1536]{1,0:T(8,128)(2,1)S(1)}, bf16[256,1536]{1,0:T(8,128)(2,1)}, u32[]{:S(2)}) copy-start(bf16[256,1536]{1,0:T(8,128)(2,1)} %project.5.refs_1_) | copy-start | bytes 2359300
  278.8 10.6 %copy-start.3 = (bf16[128,1536]{1,0:T(8,128)(2,1)S(1)}, bf16[128,1536]{1,0:T(8,128)(2,1)}, u32[]{:S(2)}) copy-start(bf16[128,1536]{1,0:T(8,128)(2,1)} %project.6.refs_2_) | copy-start | bytes 1179652
  278.8 10.6 %copy-start.9 = (bf16[512,1536]{1,0:T(8,128)(2,1)S(1)}, bf16[512,1536]{1,0:T(8,128)(2,1)}, u32[]{:S(2)}) copy-start(bf16[512,1536]{1,0:T(8,128)(2,1)} %project.4.refs_0_) | copy-start | bytes 4718596
  289.5 1.0 copy-start.4
Sparse Core Ops, SparseCore 0:
  11.0 33.9 all-gather.4
  91.0 41.3 all-gather.6
  134.0 32.9 all-gather.8
  168.4 32.9 all-gather.10

commit v7 on v6

--- a/solution.py
+++ b/solution.py
@@ -314,10 +314,10 @@
     swap2 = across(after(second, swap1, pair2), swap)
     pair3 = exchange(after(normed[rows // 4 + half :], pair2), 1)
     on1 = across(swap1, outward)
-    far1 = across(after(first, swap2, on1), far)
+    far1 = across(after(first, swap2, on1, pair3), far)
     on2 = across(swap2, outward)
-    far2 = across(after(second, far1, pair3), far)
-    on3, on4 = across(far1, outward), across(after(far2, on2), outward)
+    far2 = across(after(second, far1), far)
+    on3 = across(far1, outward)
 
     pieces = [spread(x) for x in (own, in1, in2, in3)]
     middle = jnp.where((t == 1) | (t == 2), 1, 0)
@@ -329,31 +329,33 @@
     sin = jnp.concatenate([-jnp.sin(angle), jnp.sin(angle)], axis=1)
     gains = jnp.stack([q_gain, k_gain])
 
-    calls = [
-        [
-            ((normed, normed), t * rows),
-            ((pair1, pair1), planes[1] * rows),
-            ((pair2, pair2), planes[1] * rows + rows // 4),
-            ((pair3, pair3), planes[1] * rows + rows // 4 + half),
-        ],
-        [((swap1, on1), far_mid * rows), ((swap2, on2), far_mid * rows + half)],
-        [((far1, on3), far_end * rows)],
-        [((far2, on4), far_end * rows + half)],
-    ]
     made, parts, places = [], [], []
-    for number, call in enumerate(calls):
+
+    def run(call):
         listed, first_row = [], 0
         for (block, _), place in call:
             listed.append((first_row, block.shape[0], len(places)))
             first_row += block.shape[0]
             places.append(place)
         parts.append(listed)
-        arrays = [b for b, _ in call]
-        if number >= 2:
-            arrays = [(after(x, *made[:2]), after(y, *made[:2])) for x, y in arrays]
         made.append(
-            project(arrays, [p for _, p in call], pieces, scal, cos, sin, gains)
+            project([b for b, _ in call], [p for _, p in call], pieces, scal, cos, sin, gains)
         )
+
+    pair_place = planes[1] * rows
+    run(
+        [
+            ((normed, normed), t * rows),
+            ((pair1, pair1), pair_place),
+            ((pair2, pair2), pair_place + rows // 4),
+            ((pair3, pair3), pair_place + rows // 4 + half),
+        ]
+    )
+    on4 = across(after(far2, on2, made[0]), outward)
+    run([((swap1, on1), far_mid * rows), ((swap2, on2), far_mid * rows + half)])
+    far1, on3, far2, on4 = [after(x, *made) for x in (far1, on3, far2, on4)]
+    run([((far1, on3), far_end * rows)])
+    run([((far2, on4), far_end * rows + half)])
     return attend_blocks(made, parts, places, lengths[0])
 
 

time: 319 us -> 312 us (0.978)
  waiting for transfers between devices: 183 us -> 175 us
  starting transfers between devices: 30.9 us -> 34.3 us
    ppermute x14, waiting for transfers between devices: 182 us -> 173 us  [across(): return lax.ppermute(x, 'tensor', pairs)]
    ppermute x14, starting transfers between devices: 30.7 us -> 34.2 us  [across(): return lax.ppermute(x, 'tensor', pairs)]
  transfers between devices with their start and end apart: 18 -> 18, of which waited for: 5 -> 6; matrix products, arithmetic and copies ran while one was open for 3% -> 2% of each run, Pallas kernels for 12% -> 13%
where the time goes in v7:
time: 312 us; the launch traced here: 308 us
  waiting for transfers between devices  175 us (56%)
  Pallas kernels  66.7 us (21%)
  starting transfers between devices  34.3 us (11%)
  local copies, waits for them, and re-layouts  15 us (5%)
  between operations  14.1 us (5%)
  other arithmetic  3.63 us (1%)
    ppermute x14, waiting for transfers between devices, across(): return lax.ppermute(x, 'tensor', pairs)  173 us
    pallas_call x4, Pallas kernels, project(): pl.pallas_call(functools.partial(project_kernel, counts, sources, tile),...  49.2 us
    ppermute x14, starting transfers between devices, across(): return lax.ppermute(x, 'tensor', pairs)  34.2 us
    pallas_call x1, Pallas kernels, attend_blocks(): pl.pallas_call(functools.partial(attend_kernel, parts, 256), out_shape=ja...  17.5 us
    unnamed x34, local copies, waits for them, and re-layouts  7.83 us
  transfers between devices with their start and end apart: 18, of which 6 were waited for; matrix products, arithmetic and copies ran while one was open for 2% of the time, Pallas kernels for 13%

profile of v7, /device:TPU:24, one launch (start us, length us, event | category | flops | bytes accessed | tf_op | source)
XLA Modules:
  0.0 308.4 jit_solution(8194383911728417789)
XLA Ops:
  6.5 4.2 %constant_dynamic-slice_fusion = (bf16[320,1536]{1,0:T(8,128)(2,1)}, bf16[320,1536]{1,0:T(8,128)(2,1)}, bf16[320,1536]{1,0:T(8,128)(2,1)}, bf16[320,1536]{1,0:T(8,128)(2,1)}) fusion(bf16[320,6144]{1,0:T(8,128)(2,1)} %param.7, s32[]{:T(128)S(6)} %select_n.26, s32[]{:T(128)S(6)} %select_n.24, s32[]{:T(128)S(6)} %select_n.23, s32[]{:T(128)S(6)} %select_n.25), kind=kLoop, calls=%fused_computation.13 | loop fusion | bytes 7864336 | tf_op jit(solution)/shard_map/dynamic_slice | solution.py:289
  10.8 0.0 all-gather.5.cloned.1.call-update
  10.8 0.0 all-gather.7.cloned.1.call-start
  10.9 0.0 copy-start.12
  10.9 0.5 collective-permute-start
  11.4 0.0 collective-permute-start.1
  11.4 3.9 %collective-permute-start.2 = (bf16[320,1536]{1,0:T(8,128)(2,1)}, bf16[320,1536]{1,0:T(8,128)(2,1)}, u32[]{:S(2)}, u32[]{:S(2)}) collective-permute-start(bf16[320,1536]{1,0:T(8,128)(2,1)} %get-tuple-element.38), channel_id=1, source_target_pairs={{0,3},{1,2},{2,1},{3,0},{4,7},{5,6},{6,5},{7,4},{8,11},{9,10},{10,... | collective-permute-start | bytes 2949128 | tf_op jit(solution)/shard_map/ppermute | solution.py:292
  15.3 0.6 fusion
  15.9 0.8 fusion.2.refs_0_.refs_4_
  16.7 1.0 fusion.5
  17.7 0.0 collective-permute-start.3
  17.8 73.1 %collective-permute-done.3.refs_1_.refs_5_ = bf16[64,5120]{1,0:T(8,128)(2,1)S(1)} collective-permute-done((bf16[64,5120]{1,0:T(8,128)(2,1)S(1)}, bf16[64,5120]{1,0:T(8,128)(2,1)S(1)}, u32[]{:S(2)}, u32[]{:S(2)}) %collective-permute-start.3) | collective-permute-done | bytes 655392 | tf_op jit(solution)/shard_map/ppermute | solution.py:292
  90.8 0.0 collective-permute-done
  90.8 0.0 collective-permute-done.1
  90.8 0.0 collective-permute-done.2
  90.8 0.0 all-gather.7.cloned.1.call-update
  90.9 0.0 all-gather.9.cloned.1.call-start
  90.9 0.7 all-gather.9.cloned.1.call-update
  91.6 0.0 all-gather.11.cloned.1.call-start
  91.6 0.5 all-gather.11.cloned.1.call-update
  92.2 0.0 copy-start.15
  92.2 0.0 copy-start.16
  92.2 1.5 fusion.4
  93.7 8.8 %collective-permute-start.4 = (bf16[128,5120]{1,0:T(8,128)(2,1)S(1)}, bf16[128,5120]{1,0:T(8,128)(2,1)S(1)}, u32[]{:S(2)}, u32[]{:S(2)}) collective-permute-start(bf16[128,5120]{1,0:T(8,128)(2,1)S(1)} %get-tuple-element.22), channel_id=1, source_target_pairs={{0,1},{1,0},{2,3},{3,2},{4,5},{5,4},{6,7},{7,6},{8,9},{9,8},{10,11... | collective-permute-start | bytes 3932168 | tf_op jit(solution)/shard_map/ppermute | solution.py:292
  102.6 0.7 collective-permute-start.6
  103.3 26.9 %collective-permute-done.4.refs_2_.refs_6_ = bf16[128,5120]{1,0:T(8,128)(2,1)S(1)} collective-permute-done((bf16[128,5120]{1,0:T(8,128)(2,1)S(1)}, bf16[128,5120]{1,0:T(8,128)(2,1)S(1)}, u32[]{:S(2)}, u32[]{:S(2)}) %collective-permute-start.4) | collective-permute-done | bytes 1310752 | tf_op jit(solution)/shard_map/ppermute | solution.py:292
  130.2 1.1 copy-done.5
  131.3 0.0 collective-permute-done.6.refs_0_
  131.3 1.7 collective-permute-start.7
  133.0 1.3 collective-permute-start.8
  134.3 3.4 %collective-permute-start.5 = (bf16[64,5120]{1,0:T(8,128)(2,1)S(1)}, bf16[64,5120]{1,0:T(8,128)(2,1)S(1)}, u32[]{:S(2)}, u32[]{:S(2)}) collective-permute-start(bf16[64,5120]{1,0:T(8,128)(2,1)S(1)} %copy-done.13), channel_id=1, source_target_pairs={{0,1},{1,0},{2,3},{3,2},{4,5},{5,4},{6,7},{7,6},{8,9},{9,8},{10,11... | collective-permute-start | bytes 1966088 | tf_op jit(solution)/shard_map/ppermute | solution.py:292
  137.6 40.4 %collective-permute-done.5.refs_3_.refs_7_ = bf16[64,5120]{1,0:T(8,128)(2,1)S(1)} collective-permute-done((bf16[64,5120]{1,0:T(8,128)(2,1)S(1)}, bf16[64,5120]{1,0:T(8,128)(2,1)S(1)}, u32[]{:S(2)}, u32[]{:S(2)}) %collective-permute-start.5) | collective-permute-done | bytes 655392 | tf_op jit(solution)/shard_map/ppermute | solution.py:292
  178.0 0.8 copy-done.7
  178.9 1.2 copy-done
  180.0 3.5 %collective-permute-start.10 = (bf16[128,5120]{1,0:T(8,128)(2,1)S(1)}, bf16[128,5120]{1,0:T(8,128)(2,1)}, u32[]{:S(2)}, u32[]{:S(2)}) collective-permute-start(bf16[128,5120]{1,0:T(8,128)(2,1)S(1)} %get-tuple-element.28), channel_id=1, source_target_pairs={{0,2},{3,1},{4,6},{7,5},{8,10},{11,9},{12,14},{15,13},{16,18},{19,... | collective-permute-start | bytes 3932168 | tf_op jit(solution)/shard_map/ppermute | solution.py:292
  183.5 1.3 collective-permute-start.9
  184.8 22.6 %collective-permute-done.10.refs_0_ = bf16[128,5120]{1,0:T(8,128)(2,1)} collective-permute-done((bf16[128,5120]{1,0:T(8,128)(2,1)S(1)}, bf16[128,5120]{1,0:T(8,128)(2,1)}, u32[]{:S(2)}, u32[]{:S(2)}) %collective-permute-start.10) | collective-permute-done | bytes 1310752 | tf_op jit(solution)/shard_map/ppermute | solution.py:292
  207.4 6.5 %collective-permute-start.12 = (bf16[128,5120]{1,0:T(8,128)(2,1)}, bf16[128,5120]{1,0:T(8,128)(2,1)}, u32[]{:S(2)}, u32[]{:S(2)}) collective-permute-start(bf16[128,5120]{1,0:T(8,128)(2,1)} %get-tuple-element.31), channel_id=1, source_target_pairs={{0,2},{3,1},{4,6},{7,5},{8,10},{11,9},{12,14},{15,13},{16,18},{19,... | collective-permute-start | bytes 3932168 | tf_op jit(solution)/shard_map/ppermute | solution.py:292
  213.9 0.1 concatenate.22.scal
  214.0 1.9 fusion.3
  215.9 0.3 pad_maximum_fusion
  216.3 1.3 collective-permute-start.11
  217.6 0.0 all-gather.5.cloned.1.call-done.refs_8_.refs_4_.refs_2_
  217.6 0.0 all-gather.7.cloned.1.call-done.refs_9_.refs_5_.refs_3_
  217.6 0.0 all-gather.9.cloned.1.call-done.refs_10_.refs_6_.refs_4_
  217.6 0.0 all-gather.11.cloned.1.call-done.refs_11_.refs_7_.refs_5_
  217.7 0.0 copy-start.6
  217.7 1.3 copy-done.6
  219.0 1.1 copy-done.8
  220.1 16.4 %project.4.refs_0_ = bf16[512,1536]{1,0:T(8,128)(2,1)} custom-call(s32[13]{0:T(128)S(1)} %concatenate.22.scal, bf16[256,5120]{1,0:T(8,128)(2,1)} %copy-done.10, bf16[64,5120]{1,0:T(8,128)(2,1)S(1)} %collective-permute-done.3.refs_1_.refs_5_, bf16[128,5120]{1,0:T(8,128)(2,1)S(1)} %copy-done.6, bf16[64,5120]{1,0:T(8,128)(2,1)S(1)} %copy-done.8, ...), custom_call_target="tpu_custom_call" | custom-call | flops 8053063680 | bytes 22544384 | tf_op jit(solution)/shard_map/project/pallas_call | solution.py:157
  236.5 0.7 collective-permute-done.12.refs_0_
  237.2 1.3 collective-permute-start.13
  239.2 0.1 concatenate.26.scal
  239.3 0.1 concatenate.27.scal
  239.4 0.1 concatenate.25.scal
  239.5 0.1 stack.68.scal
  239.6 1.3 copy-done.1
  240.9 12.0 %project.5.refs_1_ = bf16[256,1536]{1,0:T(8,128)(2,1)} custom-call(s32[11]{0:T(128)S(1)} %concatenate.25.scal, bf16[128,5120]{1,0:T(8,128)(2,1)S(1)} %collective-permute-done.6.refs_0_, bf16[128,5120]{1,0:T(8,128)(2,1)} %collective-permute-done.7.refs_1_, bf16[128,5120]{1,0:T(8,128)(2,1)S(1)} %copy-done.1, bf16[128,5120]{1,0:T(8,128)(2,1)} %collective-permute-done.9.refs_3_, ...), custom_call_target="tpu_custom_call" | custom-call | flops 4026531840 | bytes 19136512 | tf_op jit(solution)/shard_map/project/pallas_call | solution.py:157
  252.9 10.4 %project.6.refs_2_ = bf16[128,1536]{1,0:T(8,128)(2,1)} custom-call(s32[10]{0:T(128)S(1)} %concatenate.26.scal, bf16[128,5120]{1,0:T(8,128)(2,1)} %collective-permute-done.10.refs_0_, bf16[128,5120]{1,0:T(8,128)(2,1)} %collective-permute-done.11.refs_1_, bf16[1280,1536]{1,0:T(8,128)(2,1)} %all-gather.5.cloned.1.call-done.refs_8_.refs_4_.refs_2_, ...), custom_call_target="tpu_custom_call" | custom-call | flops 2013265920 | bytes 17432576 | tf_op jit(solution)/shard_map/project/pallas_call | solution.py:157
  263.3 0.0 copy-start.9
  263.3 9.6 %collective-permute-done.13.refs_1_ = bf16[128,5120]{1,0:T(8,128)(2,1)} collective-permute-done((bf16[128,5120]{1,0:T(8,128)(2,1)}, bf16[128,5120]{1,0:T(8,128)(2,1)}, u32[]{:S(2)}, u32[]{:S(2)}) %collective-permute-start.13) | collective-permute-done | bytes 1310752 | tf_op jit(solution)/shard_map/ppermute | solution.py:292
  272.9 10.4 %project.7.refs_3_ = bf16[128,1536]{1,0:T(8,128)(2,1)} custom-call(s32[10]{0:T(128)S(1)} %concatenate.27.scal, bf16[128,5120]{1,0:T(8,128)(2,1)} %collective-permute-done.12.refs_0_, bf16[128,5120]{1,0:T(8,128)(2,1)} %collective-permute-done.13.refs_1_, bf16[1280,1536]{1,0:T(8,128)(2,1)} %all-gather.5.cloned.1.call-done.refs_8_.refs_4_.refs_2_, ...), custom_call_target="tpu_custom_call" | custom-call | flops 2013265920 | bytes 17432576 | tf_op jit(solution)/shard_map/project/pallas_call | solution.py:157
  283.3 1.0 copy-done.4
  284.3 17.5 %attend.1 = bf16[1024,1024]{1,0:T(8,128)(2,1)} custom-call(s32[9]{0:T(128)S(1)} %stack.68.scal, bf16[512,1536]{1,0:T(8,128)(2,1)S(1)} %copy-done.9, bf16[256,1536]{1,0:T(8,128)(2,1)S(1)} %copy-done.2, bf16[128,1536]{1,0:T(8,128)(2,1)S(1)} %copy-done.3, bf16[128,1536]{1,0:T(8,128)(2,1)S(1)} %copy-done.4), custom_call_target="tpu_custom_call" | custom-call | flops 4294967296 | bytes 5242880 | tf_op jit(solution)/shard_map/attend/pallas_call | solution.py:256
  (31 shorter events, 0.1 us)
Async XLA Ops:
  6.5 211.1 %all-gather.5.cloned.1.call-start = ((), (), s32[]{:S(2)}) async-start(), calls=%async_computation | async-start | bytes 4915200 | tf_op jit(solution)/shard_map/all_gather | solution.py:298
  6.5 8.8 %copy-start.11 = (bf16[256,5120]{1,0:T(8,128)(2,1)S(1)}, bf16[256,5120]{1,0:T(8,128)(2,1)}, u32[]{:S(2)}) copy-start(bf16[256,5120]{1,0:T(8,128)(2,1)} %param.6) | copy-start | bytes 7864324
  10.8 5.2 %copy-start.14 = (f32[5120]{0:T(1024)S(1)}, f32[5120]{0:T(1024)}, u32[]{:S(2)}) copy-start(f32[5120]{0:T(1024)} %param.8) | copy-start | bytes 61444
  10.8 206.8 %all-gather.7.cloned.1.call-start = ((), (), s32[]{:S(2)}) async-start(), calls=%async_computation.1 | async-start | bytes 4915200 | tf_op jit(solution)/shard_map/all_gather | solution.py:298
  10.9 5.1 %copy-start.12 = (bf16[256,5120]{1,0:T(8,128)(2,1)S(1)}, bf16[256,5120]{1,0:T(8,128)(2,1)}, u32[]{:S(2)}) copy-start(bf16[256,5120]{1,0:T(8,128)(2,1)} %param.6) | copy-start | bytes 7864324
  10.9 80.0 %collective-permute-start = (bf16[320,1536]{1,0:T(8,128)(2,1)}, bf16[320,1536]{1,0:T(8,128)(2,1)}, u32[]{:S(2)}, u32[]{:S(2)}) collective-permute-start(bf16[320,1536]{1,0:T(8,128)(2,1)} %get-tuple-element.37), channel_id=1, source_target_pairs={{0,1},{1,0},{2,3},{3,2},{4,5},{5,4},{6,7},{7,6},{8,9},{9,8},{10,11... | collective-permute-start | bytes 2949128 | tf_op jit(solution)/shard_map/ppermute | solution.py:292
  11.4 79.4 %collective-permute-start.1 = (bf16[320,1536]{1,0:T(8,128)(2,1)}, bf16[320,1536]{1,0:T(8,128)(2,1)}, u32[]{:S(2)}, u32[]{:S(2)}) collective-permute-start(bf16[320,1536]{1,0:T(8,128)(2,1)} %get-tuple-element.36), channel_id=1, source_target_pairs={{0,2},{1,3},{2,0},{3,1},{4,6},{5,7},{6,4},{7,5},{8,10},{9,11},{10,... | collective-permute-start | bytes 2949128 | tf_op jit(solution)/shard_map/ppermute | solution.py:292
  11.4 79.4 %collective-permute-start.2 = (bf16[320,1536]{1,0:T(8,128)(2,1)}, bf16[320,1536]{1,0:T(8,128)(2,1)}, u32[]{:S(2)}, u32[]{:S(2)}) collective-permute-start(bf16[320,1536]{1,0:T(8,128)(2,1)} %get-tuple-element.38), channel_id=1, source_target_pairs={{0,3},{1,2},{2,1},{3,0},{4,7},{5,6},{6,5},{7,4},{8,11},{9,10},{10,... | collective-permute-start | bytes 2949128 | tf_op jit(solution)/shard_map/ppermute | solution.py:292
  16.7 75.5 %copy-start.10 = (bf16[256,5120]{1,0:T(8,128)(2,1)}, bf16[256,5120]{1,0:T(8,128)(2,1)S(1)}, u32[]{:S(2)}) copy-start(bf16[256,5120]{1,0:T(8,128)(2,1)S(1)} %fusion.2.refs_0_.refs_4_) | copy-start | bytes 7864324
  17.7 73.1 %collective-permute-start.3 = (bf16[64,5120]{1,0:T(8,128)(2,1)S(1)}, bf16[64,5120]{1,0:T(8,128)(2,1)S(1)}, u32[]{:S(2)}, u32[]{:S(2)}) collective-permute-start(bf16[64,5120]{1,0:T(8,128)(2,1)S(1)} %get-tuple-element.43), channel_id=1, source_target_pairs={{0,1},{1,0},{2,3},{3,2},{4,5},{5,4},{6,7},{7,6},{8,9},{9,8},{10,11... | collective-permute-start | bytes 1966088 | tf_op jit(solution)/shard_map/ppermute | solution.py:292
  90.9 126.8 %all-gather.9.cloned.1.call-start = ((), (), s32[]{:S(2)}) async-start(), calls=%async_computation.2 | async-start | bytes 4915200 | tf_op jit(solution)/shard_map/all_gather | solution.py:298
  91.6 126.1 %all-gather.11.cloned.1.call-start = ((), (), s32[]{:S(2)}) async-start(), calls=%async_computation.3 | async-start | bytes 4915200 | tf_op jit(solution)/shard_map/all_gather | solution.py:298
  92.2 42.1 %copy-start.13 = (bf16[64,5120]{1,0:T(8,128)(2,1)S(1)}, bf16[64,5120]{1,0:T(8,128)(2,1)}, u32[]{:S(2)}) copy-start(bf16[64,5120]{1,0:T(8,128)(2,1)} %get-tuple-element.23) | copy-start | bytes 1966084
  92.2 91.3 %copy-start.15 = (f32[128]{0:T(128)S(1)}, f32[128]{0:T(128)}, u32[]{:S(2)}) copy-start(f32[128]{0:T(128)} %param.10) | copy-start | bytes 1540
  92.2 91.3 %copy-start.16 = (f32[128]{0:T(128)S(1)}, f32[128]{0:T(128)}, u32[]{:S(2)}) copy-start(f32[128]{0:T(128)} %param.9) | copy-start | bytes 1540
  93.7 36.5 %collective-permute-start.4 = (bf16[128,5120]{1,0:T(8,128)(2,1)S(1)}, bf16[128,5120]{1,0:T(8,128)(2,1)S(1)}, u32[]{:S(2)}, u32[]{:S(2)}) collective-permute-start(bf16[128,5120]{1,0:T(8,128)(2,1)S(1)} %get-tuple-element.22), channel_id=1, source_target_pairs={{0,1},{1,0},{2,3},{3,2},{4,5},{5,4},{6,7},{7,6},{8,9},{9,8},{10,11... | collective-permute-start | bytes 3932168 | tf_op jit(solution)/shard_map/ppermute | solution.py:292
  102.6 28.7 %collective-permute-start.6 = (bf16[128,5120]{1,0:T(8,128)(2,1)S(1)}, bf16[128,5120]{1,0:T(8,128)(2,1)S(1)}, u32[]{:S(2)}, u32[]{:S(2)}) collective-permute-start(bf16[128,5120]{1,0:T(8,128)(2,1)S(1)} %get-tuple-element.28), channel_id=1, source_target_pairs={{1,2},{2,1},{5,6},{6,5},{9,10},{10,9},{13,14},{14,13},{17,18},{18,... | collective-permute-start | bytes 3932168 | tf_op jit(solution)/shard_map/ppermute | solution.py:292
  130.2 1.1 copy-start.5
  131.3 47.6 %collective-permute-start.7 = (bf16[128,5120]{1,0:T(8,128)(2,1)}, bf16[128,5120]{1,0:T(8,128)(2,1)}, u32[]{:S(2)}, u32[]{:S(2)}) collective-permute-start(bf16[128,5120]{1,0:T(8,128)(2,1)} %get-tuple-element.31), channel_id=1, source_target_pairs={{1,2},{2,1},{5,6},{6,5},{9,10},{10,9},{13,14},{14,13},{17,18},{18,... | collective-permute-start | bytes 3932168 | tf_op jit(solution)/shard_map/ppermute | solution.py:292
  133.0 45.9 %collective-permute-start.8 = (bf16[128,5120]{1,0:T(8,128)(2,1)S(1)}, bf16[128,5120]{1,0:T(8,128)(2,1)S(1)}, u32[]{:S(2)}, u32[]{:S(2)}) collective-permute-start(bf16[128,5120]{1,0:T(8,128)(2,1)S(1)} %collective-permute-done.6.refs_0_), channel_id=1, source_target_pairs={{1,0},{2,3},{5,4},{6,7},{9,8},{10,11},{13,12},{14,15},{17,16},{18,... | collective-permute-start | bytes 3932168 | tf_op jit(solution)/shard_map/ppermute | solution.py:292
  134.3 43.7 %collective-permute-start.5 = (bf16[64,5120]{1,0:T(8,128)(2,1)S(1)}, bf16[64,5120]{1,0:T(8,128)(2,1)S(1)}, u32[]{:S(2)}, u32[]{:S(2)}) collective-permute-start(bf16[64,5120]{1,0:T(8,128)(2,1)S(1)} %copy-done.13), channel_id=1, source_target_pairs={{0,1},{1,0},{2,3},{3,2},{4,5},{5,4},{6,7},{7,6},{8,9},{9,8},{10,11... | collective-permute-start | bytes 1966088 | tf_op jit(solution)/shard_map/ppermute | solution.py:292
  178.0 0.8 copy-start.7
  178.9 1.2 copy-start
  180.0 27.4 %collective-permute-start.10 = (bf16[128,5120]{1,0:T(8,128)(2,1)S(1)}, bf16[128,5120]{1,0:T(8,128)(2,1)}, u32[]{:S(2)}, u32[]{:S(2)}) collective-permute-start(bf16[128,5120]{1,0:T(8,128)(2,1)S(1)} %get-tuple-element.28), channel_id=1, source_target_pairs={{0,2},{3,1},{4,6},{7,5},{8,10},{11,9},{12,14},{15,13},{16,18},{19,... | collective-permute-start | bytes 3932168 | tf_op jit(solution)/shard_map/ppermute | solution.py:292
  183.5 53.0 %collective-permute-start.9 = (bf16[128,5120]{1,0:T(8,128)(2,1)}, bf16[128,5120]{1,0:T(8,128)(2,1)}, u32[]{:S(2)}, u32[]{:S(2)}) collective-permute-start(bf16[128,5120]{1,0:T(8,128)(2,1)} %collective-permute-done.7.refs_1_), channel_id=1, source_target_pairs={{1,0},{2,3},{5,4},{6,7},{9,8},{10,11},{13,12},{14,15},{17,16},{18,... | collective-permute-start | bytes 3932168 | tf_op jit(solution)/shard_map/ppermute | solution.py:292
  207.4 29.8 %collective-permute-start.12 = (bf16[128,5120]{1,0:T(8,128)(2,1)}, bf16[128,5120]{1,0:T(8,128)(2,1)}, u32[]{:S(2)}, u32[]{:S(2)}) collective-permute-start(bf16[128,5120]{1,0:T(8,128)(2,1)} %get-tuple-element.31), channel_id=1, source_target_pairs={{0,2},{3,1},{4,6},{7,5},{8,10},{11,9},{12,14},{15,13},{16,18},{19,... | collective-permute-start | bytes 3932168 | tf_op jit(solution)/shard_map/ppermute | solution.py:292
  216.3 36.6 %collective-permute-start.11 = (bf16[128,5120]{1,0:T(8,128)(2,1)}, bf16[128,5120]{1,0:T(8,128)(2,1)}, u32[]{:S(2)}, u32[]{:S(2)}) collective-permute-start(bf16[128,5120]{1,0:T(8,128)(2,1)} %collective-permute-done.10.refs_0_), channel_id=1, source_target_pairs={{1,0},{2,3},{5,4},{6,7},{9,8},{10,11},{13,12},{14,15},{17,16},{18,... | collective-permute-start | bytes 3932168 | tf_op jit(solution)/shard_map/ppermute | solution.py:292
  217.7 1.3 copy-start.6
  219.0 1.1 copy-start.8
  237.2 35.6 %collective-permute-start.13 = (bf16[128,5120]{1,0:T(8,128)(2,1)}, bf16[128,5120]{1,0:T(8,128)(2,1)}, u32[]{:S(2)}, u32[]{:S(2)}) collective-permute-start(bf16[128,5120]{1,0:T(8,128)(2,1)} %collective-permute-done.12.refs_0_), channel_id=1, source_target_pairs={{1,0},{2,3},{5,4},{6,7},{9,8},{10,11},{13,12},{14,15},{17,16},{18,... | collective-permute-start | bytes 3932168 | tf_op jit(solution)/shard_map/ppermute | solution.py:292
  239.6 1.3 copy-start.1
  263.3 20.0 %copy-start.2 = (bf16[256,1536]{1,0:T(8,128)(2,1)S(1)}, bf16[256,1536]{1,0:T(8,128)(2,1)}, u32[]{:S(2)}) copy-start(bf16[256,1536]{1,0:T(8,128)(2,1)} %project.5.refs_1_) | copy-start | bytes 2359300
  263.3 20.0 %copy-start.3 = (bf16[128,1536]{1,0:T(8,128)(2,1)S(1)}, bf16[128,1536]{1,0:T(8,128)(2,1)}, u32[]{:S(2)}) copy-start(bf16[128,1536]{1,0:T(8,128)(2,1)} %project.6.refs_2_) | copy-start | bytes 1179652
  263.3 20.0 %copy-start.9 = (bf16[512,1536]{1,0:T(8,128)(2,1)S(1)}, bf16[512,1536]{1,0:T(8,128)(2,1)}, u32[]{:S(2)}) copy-start(bf16[512,1536]{1,0:T(8,128)(2,1)} %project.4.refs_0_) | copy-start | bytes 4718596
  283.3 1.0 copy-start.4
Sparse Core Ops, SparseCore 0:
  10.9 33.9 all-gather.4
  91.0 41.3 all-gather.6
  133.9 32.9 all-gather.8
  168.4 32.9 all-gather.10

commit v8 on v7

--- a/solution.py
+++ b/solution.py
@@ -179,14 +179,15 @@
     )(scal, *[r for r, _ in rows_list], *[r for _, r in rows_list], *pieces, cos, sin, gains)
 
 
-def attend_kernel(parts, block, scal, *refs):
-    out, held, sems = refs[len(parts) :]
-    length = scal[0]
-
+FACTOR = LOG2E / float(HD) ** 0.5
+CONTRACT = (((1,), (1,)), ((), ()))
+
+
+def fetch_blocks(refs, parts, places, held, sems):
     copies = []
     for ref, blocks in zip(refs, parts):
         for first, rows, number in blocks:
-            place = pl.ds(pl.multiple_of(scal[1 + number], 16), rows)
+            place = pl.ds(pl.multiple_of(places(number), 16), rows)
             copies.append(
                 pltpu.make_async_copy(
                     ref.at[first : first + rows, :], held.at[place, :], sems.at[number]
@@ -197,79 +198,148 @@
     for copy in copies:
         copy.wait()
 
-    total = held.shape[0]
-    heads = held.shape[1] // ((GQ + 2) * HD)
-    factor = LOG2E / float(HD) ** 0.5
+
+def head_columns(head):
+    base = head // GQ * (GQ + 2) * HD
+    query = base + head % GQ * HD
+    key = base + GQ * HD
+    return (
+        slice(query, query + HD),
+        slice(key, key + HD),
+        slice(key + HD, key + 2 * HD),
+        slice(head * HD, (head + 1) * HD),
+    )
+
+
+def attend_rows(held, head, low, block, length):
+    query_at, key_at, value_at, _ = head_columns(head)
+    high = low + block
     row = lax.broadcasted_iota(jnp.int32, (block, block), 0)
     col = lax.broadcasted_iota(jnp.int32, (block, block), 1)
-    contract = (((1,), (1,)), ((), ()))
-    for group in range(heads):
-        base = group * (GQ + 2) * HD
-        key_at = slice(base + GQ * HD, base + (GQ + 1) * HD)
-        value_at = slice(base + (GQ + 1) * HD, base + (GQ + 2) * HD)
-
-        @pl.loop(0, GQ)
-        def _(j, base=base, key_at=key_at, value_at=value_at, group=group):
-            query_at = pl.ds(pl.multiple_of(base + j * HD, HD), HD)
-            out_at = pl.ds(pl.multiple_of((group * GQ + j) * HD, HD), HD)
-            for step in range(total // block):
-                low = step * block
-                high = low + block
-                query = held[low:high, query_at]
-                last = lax.dot_general(
-                    query, held[low:high, key_at], contract, preferred_element_type=jnp.float32
-                )
-                last = jnp.where((col <= row) & (col + low < length), last, -1e30)
-                top = jnp.max(last, axis=-1, keepdims=True)
-                if step:
-                    rest = lax.dot_general(
-                        query, held[:low, key_at], contract, preferred_element_type=jnp.float32
-                    )
-                    keys = lax.broadcasted_iota(jnp.int32, (1, low), 1)
-                    rest = rest + jnp.where(keys < length, 0.0, -1e30)
-                    top = jnp.maximum(top, jnp.max(rest, axis=-1, keepdims=True))
-                shift = top * factor
-                probs = jnp.exp2(last * factor - shift)
-                norm = jnp.sum(probs, axis=-1, keepdims=True)
-                value = jnp.dot(
-                    probs.astype(jnp.bfloat16),
-                    held[low:high, value_at],
+    query = held[low:high, query_at]
+    last = lax.dot_general(
+        query, held[low:high, key_at], CONTRACT, preferred_element_type=jnp.float32
+    )
+    last = jnp.where((col <= row) & (col + low < length), last, -1e30)
+    top = jnp.max(last, axis=-1, keepdims=True)
+    if low:
+        rest = lax.dot_general(
+            query, held[:low, key_at], CONTRACT, preferred_element_type=jnp.float32
+        )
+        keys = lax.broadcasted_iota(jnp.int32, (1, low), 1)
+        rest = rest + jnp.where(keys < length, 0.0, -1e30)
+        top = jnp.maximum(top, jnp.max(rest, axis=-1, keepdims=True))
+    shift = top * FACTOR
+    probs = jnp.exp2(last * FACTOR - shift)
+    norm = jnp.sum(probs, axis=-1, keepdims=True)
+    value = jnp.dot(
+        probs.astype(jnp.bfloat16), held[low:high, value_at], preferred_element_type=jnp.float32
+    )
+    if low:
+        probs = jnp.exp2(rest * FACTOR - shift)
+        norm = norm + jnp.sum(probs, axis=-1, keepdims=True)
+        value = value + jnp.dot(
+            probs.astype(jnp.bfloat16), held[:low, value_at], preferred_element_type=jnp.float32
+        )
+    return top, norm, value
+
+
+def attend_near_kernel(parts, block, scal, *refs):
+    partial, stats, held, sems = refs[len(parts) :]
+    fetch_blocks(refs, parts, lambda number: scal[2 + number], held, sems)
+    heads = partial.shape[1] // HD
+    for head in range(heads):
+        out_at = head_columns(head)[3]
+        for low in range(0, held.shape[0], block):
+            top, norm, value = attend_rows(held, head, low, block, scal[0])
+            partial[low : low + block, out_at] = value
+            stats[low : low + block, head : head + 1] = top
+            stats[low : low + block, heads + head : heads + head + 1] = norm
+
+
+def attend_far_kernel(parts, block, scal, *refs):
+    partial, stats, out, held, sems = refs[len(parts) :]
+    fetch_blocks(refs, parts, lambda number: scal[2 + number], held, sems)
+    heads = out.shape[1] // HD
+    total = held.shape[0]
+    length = scal[0]
+
+    @pl.when(scal[1] == 0)
+    def _():
+        low = total - block
+        for head in range(heads):
+            out_at = head_columns(head)[3]
+            _, norm, value = attend_rows(held, head, low, block, length)
+            out[low:, out_at] = (value / norm).astype(out.dtype)
+            norm = stats[:, heads + head : heads + head + 1]
+            out[:low, out_at] = (partial[:, out_at] / norm).astype(out.dtype)
+
+    @pl.when(scal[1] == 1)
+    def _():
+        for head in range(heads):
+            query_at, key_at, value_at, out_at = head_columns(head)
+            _, norm, value = attend_rows(held, head, 0, block, length)
+            out[:block, out_at] = (value / norm).astype(out.dtype)
+            for low in range(0, total - block, block):
+                near = slice(low, low + block)
+                scores = lax.dot_general(
+                    held[low + block : low + 2 * block, query_at],
+                    held[:block, key_at],
+                    CONTRACT,
                     preferred_element_type=jnp.float32,
                 )
-                if step:
-                    probs = jnp.exp2(rest * factor - shift)
-                    norm = norm + jnp.sum(probs, axis=-1, keepdims=True)
-                    value = value + jnp.dot(
-                        probs.astype(jnp.bfloat16),
-                        held[:low, value_at],
-                        preferred_element_type=jnp.float32,
-                    )
-                out[low:high, out_at] = (value / norm).astype(out.dtype)
-
-
-def attend_blocks(arrays, parts, places, length):
+                keys = lax.broadcasted_iota(jnp.int32, (1, block), 1)
+                scores = scores + jnp.where(keys < length, 0.0, -1e30)
+                before = stats[near, head : head + 1]
+                top = jnp.maximum(before, jnp.max(scores, axis=-1, keepdims=True))
+                probs = jnp.exp2((scores - top) * FACTOR)
+                scale = jnp.exp2((before - top) * FACTOR)
+                norm = stats[near, heads + head : heads + head + 1] * scale
+                norm = norm + jnp.sum(probs, axis=-1, keepdims=True)
+                value = partial[near, out_at] * scale + jnp.dot(
+                    probs.astype(jnp.bfloat16),
+                    held[:block, value_at],
+                    preferred_element_type=jnp.float32,
+                )
+                out[low + block : low + 2 * block, out_at] = (value / norm).astype(out.dtype)
+
+
+def attend_blocks(arrays, parts, places, length, side, block, partial=None):
     rows = sum(a.shape[0] for a in arrays)
     columns = arrays[0].shape[1]
     wide = columns // (GQ + 2) * GQ
-    scal = jnp.stack([length] + list(places)).astype(jnp.int32)
+    scal = jnp.stack([length, side] + list(places)).astype(jnp.int32)
     hbm = pl.BlockSpec(memory_space=pltpu.HBM)
+    vmem = pl.BlockSpec(memory_space=pltpu.VMEM)
+    if partial is None:
+        body, name = attend_near_kernel, "attend_near"
+        out_shape = [
+            jax.ShapeDtypeStruct((rows, wide), jnp.float32),
+            jax.ShapeDtypeStruct((rows, HD), jnp.float32),
+        ]
+    else:
+        body, name = attend_far_kernel, "attend_far"
+        out_shape = [jax.ShapeDtypeStruct((rows, wide), jnp.bfloat16)]
+    extra = [] if partial is None else list(partial)
     return pl.pallas_call(
-        functools.partial(attend_kernel, parts, 256),
-        out_shape=jax.ShapeDtypeStruct((rows, wide), jnp.bfloat16),
-        in_specs=[pl.BlockSpec(memory_space=pltpu.SMEM)] + [hbm] * len(arrays),
-        out_specs=pl.BlockSpec(memory_space=pltpu.VMEM),
+        functools.partial(body, parts, block),
+        out_shape=out_shape,
+        in_specs=[pl.BlockSpec(memory_space=pltpu.SMEM)]
+        + [hbm] * len(arrays)
+        + [vmem] * len(extra),
+        out_specs=[vmem] * len(out_shape),
         scratch_shapes=[
             pltpu.VMEM((rows, columns), jnp.bfloat16),
             pltpu.SemaphoreType.DMA((len(places),)),
         ],
         compiler_params=pltpu.CompilerParams(vmem_limit_bytes=VMEM_BYTES),
         cost_estimate=pl.CostEstimate(
-            flops=4 * rows * rows * wide,
+            flops=2 * rows * rows * wide,
             bytes_accessed=2 * rows * (columns + wide),
             transcendentals=rows * rows * wide // HD // 2,
         ),
-        name="attend",
-    )(scal, *arrays)
+        name=name,
+    )(scal, *arrays, *extra)
 
 
 def after(x, *earlier):
@@ -353,10 +423,12 @@
     )
     on4 = across(after(far2, on2, made[0]), outward)
     run([((swap1, on1), far_mid * rows), ((swap2, on2), far_mid * rows + half)])
-    far1, on3, far2, on4 = [after(x, *made) for x in (far1, on3, far2, on4)]
+    near_places = [place - side * rows for place in places]
+    partial = attend_blocks(made, parts, near_places, lengths[0] - side * rows, side, rows)
+    far1, on3, far2, on4 = [after(x, *partial) for x in (far1, on3, far2, on4)]
     run([((far1, on3), far_end * rows)])
     run([((far2, on4), far_end * rows + half)])
-    return attend_blocks(made, parts, places, lengths[0])
+    return attend_blocks(made, parts, places, lengths[0], side, rows, partial)[0]
 
 
 def solution(mesh):

time: 312 us -> 321 us (1.029)
  the two profiles are of different devices: /device:TPU:24 before, /device:TPU:20 now
where the time goes in v8:
time: 321 us; the launch traced here: 315 us
  waiting for transfers between devices  172 us (54%)
  Pallas kernels  74.2 us (23%)
  starting transfers between devices  32.4 us (10%)
  local copies, waits for them, and re-layouts  18.8 us (6%)
  between operations  14.5 us (5%)
  other arithmetic  3.63 us (1%)
    ppermute x14, waiting for transfers between devices, across(): return lax.ppermute(x, 'tensor', pairs)  170 us
    pallas_call x4, Pallas kernels, project(): pl.pallas_call(functools.partial(project_kernel, counts, sources, tile),...  49.2 us
    ppermute x14, starting transfers between devices, across(): return lax.ppermute(x, 'tensor', pairs)  32.3 us
    pallas_call x2, Pallas kernels, attend_blocks(): pl.pallas_call(functools.partial(body, parts, block), out_shape=out_shape...  25 us
    unnamed x34, local copies, waits for them, and re-layouts  10.5 us
  transfers between devices with their start and end apart: 18, of which 7 were waited for; matrix products, arithmetic and copies ran while one was open for 2% of the time, Pallas kernels for 15%

profile of v8, /device:TPU:20, one launch (start us, length us, event | category | flops | bytes accessed | tf_op | source)
XLA Modules:
  0.0 315.3 jit_solution(2288007863714928037)
XLA Ops:
  6.5 4.2 %constant_dynamic-slice_fusion = (bf16[320,1536]{1,0:T(8,128)(2,1)}, bf16[320,1536]{1,0:T(8,128)(2,1)}, bf16[320,1536]{1,0:T(8,128)(2,1)}, bf16[320,1536]{1,0:T(8,128)(2,1)}) fusion(bf16[320,6144]{1,0:T(8,128)(2,1)} %param.7, s32[]{:T(128)S(6)} %select_n.26, s32[]{:T(128)S(6)} %select_n.24, s32[]{:T(128)S(6)} %select_n.23, s32[]{:T(128)S(6)} %select_n.25), kind=kLoop, calls=%fused_computation.13 | loop fusion | bytes 7864336 | tf_op jit(solution)/shard_map/dynamic_slice | solution.py:359
  10.8 0.0 all-gather.5.cloned.1.call-update
  10.8 0.0 all-gather.7.cloned.1.call-start
  10.9 1.6 collective-permute-start
  12.5 0.3 collective-permute-start.1
  12.8 1.6 collective-permute-start.2
  14.4 0.6 fusion
  15.0 0.8 fusion.2.refs_0_.refs_4_
  15.8 0.1 fusion.5
  15.9 2.5 collective-permute-start.3
  18.4 72.4 %collective-permute-done.3.refs_1_.refs_5_ = bf16[64,5120]{1,0:T(8,128)(2,1)S(1)} collective-permute-done((bf16[64,5120]{1,0:T(8,128)(2,1)S(1)}, bf16[64,5120]{1,0:T(8,128)(2,1)S(1)}, u32[]{:S(2)}, u32[]{:S(2)}) %collective-permute-start.3) | collective-permute-done | bytes 655392 | tf_op jit(solution)/shard_map/ppermute | solution.py:362
  90.9 0.0 collective-permute-done
  90.9 0.0 collective-permute-done.1
  90.9 8.3 %collective-permute-done.2 = bf16[320,1536]{1,0:T(8,128)(2,1)} collective-permute-done((bf16[320,1536]{1,0:T(8,128)(2,1)}, bf16[320,1536]{1,0:T(8,128)(2,1)}, u32[]{:S(2)}, u32[]{:S(2)}) %collective-permute-start.2) | collective-permute-done | bytes 983072 | tf_op jit(solution)/shard_map/ppermute | solution.py:362
  99.2 0.0 all-gather.7.cloned.1.call-update
  99.2 0.0 all-gather.9.cloned.1.call-start
  99.3 0.7 all-gather.9.cloned.1.call-update
  100.0 0.0 all-gather.11.cloned.1.call-start
  100.0 0.5 all-gather.11.cloned.1.call-update
  100.5 0.0 copy-start.15
  100.6 0.0 copy-start.16
  100.6 3.4 %fusion.4 = (bf16[128,5120]{1,0:T(8,128)(2,1)}, bf16[128,5120]{1,0:T(8,128)(2,1)S(1)}, bf16[128,5120]{1,0:T(8,128)(2,1)S(1)}) fusion(bf16[256,5120]{1,0:T(8,128)(2,1)} %copy-done.12), kind=kLoop, calls=%fused_computation.18 | loop fusion | bytes 7864320 | tf_op jit(solution)/shard_map/slice | solution.py:377
  104.0 0.0 collective-permute-start.4
  104.0 2.3 collective-permute-start.6
  106.4 27.0 %collective-permute-done.4.refs_2_.refs_6_ = bf16[128,5120]{1,0:T(8,128)(2,1)S(1)} collective-permute-done((bf16[128,5120]{1,0:T(8,128)(2,1)S(1)}, bf16[128,5120]{1,0:T(8,128)(2,1)S(1)}, u32[]{:S(2)}, u32[]{:S(2)}) %collective-permute-start.4) | collective-permute-done | bytes 1310752 | tf_op jit(solution)/shard_map/ppermute | solution.py:362
  133.4 1.1 copy-done.8
  134.4 0.8 collective-permute-done.6.refs_0_
  135.3 2.3 collective-permute-start.7
  137.6 1.4 collective-permute-start.8
  139.0 0.1 collective-permute-start.5
  139.1 39.8 %collective-permute-done.5.refs_3_.refs_7_ = bf16[64,5120]{1,0:T(8,128)(2,1)S(1)} collective-permute-done((bf16[64,5120]{1,0:T(8,128)(2,1)S(1)}, bf16[64,5120]{1,0:T(8,128)(2,1)S(1)}, u32[]{:S(2)}, u32[]{:S(2)}) %collective-permute-start.5) | collective-permute-done | bytes 655392 | tf_op jit(solution)/shard_map/ppermute | solution.py:362
  178.9 0.9 copy-done.10
  179.8 0.0 collective-permute-done.8.refs_2_
  179.8 1.1 copy-done.6
  180.9 1.3 collective-permute-start.10
  182.2 7.7 %collective-permute-start.9 = (bf16[128,5120]{1,0:T(8,128)(2,1)}, bf16[128,5120]{1,0:T(8,128)(2,1)}, u32[]{:S(2)}, u32[]{:S(2)}) collective-permute-start(bf16[128,5120]{1,0:T(8,128)(2,1)} %collective-permute-done.7.refs_1_), channel_id=1, source_target_pairs={{1,0},{2,3},{5,4},{6,7},{9,8},{10,11},{13,12},{14,15},{17,16},{18,... | collective-permute-start | bytes 3932168 | tf_op jit(solution)/shard_map/ppermute | solution.py:362
  189.9 21.7 %collective-permute-done.10.refs_0_ = bf16[128,5120]{1,0:T(8,128)(2,1)} collective-permute-done((bf16[128,5120]{1,0:T(8,128)(2,1)S(1)}, bf16[128,5120]{1,0:T(8,128)(2,1)}, u32[]{:S(2)}, u32[]{:S(2)}) %collective-permute-start.10) | collective-permute-done | bytes 1310752 | tf_op jit(solution)/shard_map/ppermute | solution.py:362
  211.6 1.3 collective-permute-start.12
  212.9 0.1 concatenate.22.scal
  213.0 1.9 fusion.3
  214.9 0.3 pad_maximum_fusion
  215.3 7.4 %collective-permute-start.11 = (bf16[128,5120]{1,0:T(8,128)(2,1)}, bf16[128,5120]{1,0:T(8,128)(2,1)}, u32[]{:S(2)}, u32[]{:S(2)}) collective-permute-start(bf16[128,5120]{1,0:T(8,128)(2,1)} %collective-permute-done.10.refs_0_), channel_id=1, source_target_pairs={{1,0},{2,3},{5,4},{6,7},{9,8},{10,11},{13,12},{14,15},{17,16},{18,... | collective-permute-start | bytes 3932168 | tf_op jit(solution)/shard_map/ppermute | solution.py:362
  222.7 1.3 copy-done.9
  224.0 1.1 copy-done.11
  225.1 16.3 %project.4.refs_0_ = bf16[512,1536]{1,0:T(8,128)(2,1)} custom-call(s32[13]{0:T(128)S(1)} %concatenate.22.scal, bf16[256,5120]{1,0:T(8,128)(2,1)} %copy-done.12, bf16[64,5120]{1,0:T(8,128)(2,1)S(1)} %collective-permute-done.3.refs_1_.refs_5_, bf16[128,5120]{1,0:T(8,128)(2,1)S(1)} %copy-done.9, bf16[64,5120]{1,0:T(8,128)(2,1)S(1)} %copy-done.11, ...), custom_call_target="tpu_custom_call" | custom-call | flops 8053063680 | bytes 22544384 | tf_op jit(solution)/shard_map/project/pallas_call | solution.py:157
  241.4 0.2 collective-permute-done.12.refs_0_
  241.7 2.4 collective-permute-start.13
  244.8 0.1 concatenate.26.scal
  244.8 0.1 concatenate.27.scal
  244.9 0.1 concatenate.25.scal
  245.0 0.1 stack.97.scal
  245.1 0.1 stack.113.scal
  245.2 1.3 copy-done.7
  246.5 11.8 %project.5.refs_1_ = bf16[256,1536]{1,0:T(8,128)(2,1)} custom-call(s32[11]{0:T(128)S(1)} %concatenate.25.scal, bf16[128,5120]{1,0:T(8,128)(2,1)S(1)} %collective-permute-done.6.refs_0_, bf16[128,5120]{1,0:T(8,128)(2,1)} %collective-permute-done.7.refs_1_, bf16[128,5120]{1,0:T(8,128)(2,1)S(1)} %copy-done.7, bf16[128,5120]{1,0:T(8,128)(2,1)} %collective-permute-done.9.refs_3_, ...), custom_call_target="tpu_custom_call" | custom-call | flops 4026531840 | bytes 19136512 | tf_op jit(solution)/shard_map/project/pallas_call | solution.py:157
  258.4 1.1 copy-done
  259.5 10.2 %attend_near.1 = (f32[768,1024]{1,0:T(8,128)S(1)}, f32[768,128]{1,0:T(8,128)S(1)}) custom-call(s32[8]{0:T(128)S(1)} %stack.113.scal, bf16[512,1536]{1,0:T(8,128)(2,1)S(1)} %copy-done.5, bf16[256,1536]{1,0:T(8,128)(2,1)S(1)} %copy-done), custom_call_target="tpu_custom_call" | custom-call | flops 1207959552 | bytes 3932160 | tf_op jit(solution)/shard_map/attend_near/pallas_call | solution.py:324
  269.7 1.6 copy-done.2
  271.4 0.0 collective-permute-done.11.refs_1_
  271.4 10.4 %project.6.refs_2_ = bf16[128,1536]{1,0:T(8,128)(2,1)} custom-call(s32[10]{0:T(128)S(1)} %concatenate.26.scal, bf16[128,5120]{1,0:T(8,128)(2,1)} %collective-permute-done.10.refs_0_, bf16[128,5120]{1,0:T(8,128)(2,1)} %collective-permute-done.11.refs_1_, bf16[1280,1536]{1,0:T(8,128)(2,1)} %all-gather.5.cloned.1.call-done.refs_8_.refs_4_.refs_2_, ...), custom_call_target="tpu_custom_call" | custom-call | flops 2013265920 | bytes 17432576 | tf_op jit(solution)/shard_map/project/pallas_call | solution.py:157
  281.7 0.0 copy-start.3
  281.8 0.0 collective-permute-done.13.refs_1_
  281.8 10.6 %project.7.refs_3_ = bf16[128,1536]{1,0:T(8,128)(2,1)} custom-call(s32[10]{0:T(128)S(1)} %concatenate.27.scal, bf16[128,5120]{1,0:T(8,128)(2,1)} %collective-permute-done.12.refs_0_, bf16[128,5120]{1,0:T(8,128)(2,1)} %collective-permute-done.13.refs_1_, bf16[1280,1536]{1,0:T(8,128)(2,1)} %all-gather.5.cloned.1.call-done.refs_8_.refs_4_.refs_2_, ...), custom_call_target="tpu_custom_call" | custom-call | flops 2013265920 | bytes 17432576 | tf_op jit(solution)/shard_map/project/pallas_call | solution.py:157
  292.4 1.0 copy-done.4
  293.4 14.8 %attend_far.1 = bf16[1024,1024]{1,0:T(8,128)(2,1)} custom-call(s32[10]{0:T(128)S(1)} %stack.97.scal, bf16[512,1536]{1,0:T(8,128)(2,1)S(1)} %copy-done.5, bf16[256,1536]{1,0:T(8,128)(2,1)S(1)} %copy-done.1, bf16[128,1536]{1,0:T(8,128)(2,1)S(1)} %copy-done.3, bf16[128,1536]{1,0:T(8,128)(2,1)S(1)} %copy-done.4, f32[768,1024]{1,0:T(8,128)} %copy-done.2, ...), custom_call_target="tpu_custom_call" | custom-call | flops 2147483648 | bytes 5242880 | tf_op jit(solution)/shard_map/attend_far/pallas_call | solution.py:324
  (33 shorter events, 0.1 us)
Async XLA Ops:
  6.5 216.1 %all-gather.5.cloned.1.call-start = ((), (), s32[]{:S(2)}) async-start(), calls=%async_computation | async-start | bytes 4915200 | tf_op jit(solution)/shard_map/all_gather | solution.py:368
  6.5 7.9 %copy-start.13 = (bf16[256,5120]{1,0:T(8,128)(2,1)S(1)}, bf16[256,5120]{1,0:T(8,128)(2,1)}, u32[]{:S(2)}) copy-start(bf16[256,5120]{1,0:T(8,128)(2,1)} %param.6) | copy-start | bytes 7864324
  10.8 4.2 %copy-start.14 = (f32[5120]{0:T(1024)S(1)}, f32[5120]{0:T(1024)}, u32[]{:S(2)}) copy-start(f32[5120]{0:T(1024)} %param.8) | copy-start | bytes 61444
  10.8 211.9 %all-gather.7.cloned.1.call-start = ((), (), s32[]{:S(2)}) async-start(), calls=%async_computation.1 | async-start | bytes 4915200 | tf_op jit(solution)/shard_map/all_gather | solution.py:368
  10.9 80.0 %collective-permute-start = (bf16[320,1536]{1,0:T(8,128)(2,1)}, bf16[320,1536]{1,0:T(8,128)(2,1)}, u32[]{:S(2)}, u32[]{:S(2)}) collective-permute-start(bf16[320,1536]{1,0:T(8,128)(2,1)} %get-tuple-element.41), channel_id=1, source_target_pairs={{0,1},{1,0},{2,3},{3,2},{4,5},{5,4},{6,7},{7,6},{8,9},{9,8},{10,11... | collective-permute-start | bytes 2949128 | tf_op jit(solution)/shard_map/ppermute | solution.py:362
  12.5 78.4 %collective-permute-start.1 = (bf16[320,1536]{1,0:T(8,128)(2,1)}, bf16[320,1536]{1,0:T(8,128)(2,1)}, u32[]{:S(2)}, u32[]{:S(2)}) collective-permute-start(bf16[320,1536]{1,0:T(8,128)(2,1)} %get-tuple-element.40), channel_id=1, source_target_pairs={{0,2},{1,3},{2,0},{3,1},{4,6},{5,7},{6,4},{7,5},{8,10},{9,11},{10,... | collective-permute-start | bytes 2949128 | tf_op jit(solution)/shard_map/ppermute | solution.py:362
  12.8 86.4 %collective-permute-start.2 = (bf16[320,1536]{1,0:T(8,128)(2,1)}, bf16[320,1536]{1,0:T(8,128)(2,1)}, u32[]{:S(2)}, u32[]{:S(2)}) collective-permute-start(bf16[320,1536]{1,0:T(8,128)(2,1)} %get-tuple-element.42), channel_id=1, source_target_pairs={{0,3},{1,2},{2,1},{3,0},{4,7},{5,6},{6,5},{7,4},{8,11},{9,10},{10,... | collective-permute-start | bytes 2949128 | tf_op jit(solution)/shard_map/ppermute | solution.py:362
  15.8 75.1 %copy-start.12 = (bf16[256,5120]{1,0:T(8,128)(2,1)}, bf16[256,5120]{1,0:T(8,128)(2,1)S(1)}, u32[]{:S(2)}) copy-start(bf16[256,5120]{1,0:T(8,128)(2,1)S(1)} %fusion.2.refs_0_.refs_4_) | copy-start | bytes 7864324
  15.9 75.0 %collective-permute-start.3 = (bf16[64,5120]{1,0:T(8,128)(2,1)S(1)}, bf16[64,5120]{1,0:T(8,128)(2,1)S(1)}, u32[]{:S(2)}, u32[]{:S(2)}) collective-permute-start(bf16[64,5120]{1,0:T(8,128)(2,1)S(1)} %get-tuple-element.47), channel_id=1, source_target_pairs={{0,1},{1,0},{2,3},{3,2},{4,5},{5,4},{6,7},{7,6},{8,9},{9,8},{10,11... | collective-permute-start | bytes 1966088 | tf_op jit(solution)/shard_map/ppermute | solution.py:362
  99.2 123.4 %all-gather.9.cloned.1.call-start = ((), (), s32[]{:S(2)}) async-start(), calls=%async_computation.2 | async-start | bytes 4915200 | tf_op jit(solution)/shard_map/all_gather | solution.py:368
  100.0 122.7 %all-gather.11.cloned.1.call-start = ((), (), s32[]{:S(2)}) async-start(), calls=%async_computation.3 | async-start | bytes 4915200 | tf_op jit(solution)/shard_map/all_gather | solution.py:368
  100.5 81.6 %copy-start.15 = (f32[128]{0:T(128)S(1)}, f32[128]{0:T(128)}, u32[]{:S(2)}) copy-start(f32[128]{0:T(128)} %param.10) | copy-start | bytes 1540
  100.6 81.6 %copy-start.16 = (f32[128]{0:T(128)S(1)}, f32[128]{0:T(128)}, u32[]{:S(2)}) copy-start(f32[128]{0:T(128)} %param.9) | copy-start | bytes 1540
  104.0 29.4 %collective-permute-start.4 = (bf16[128,5120]{1,0:T(8,128)(2,1)S(1)}, bf16[128,5120]{1,0:T(8,128)(2,1)S(1)}, u32[]{:S(2)}, u32[]{:S(2)}) collective-permute-start(bf16[128,5120]{1,0:T(8,128)(2,1)S(1)} %get-tuple-element.24), channel_id=1, source_target_pairs={{0,1},{1,0},{2,3},{3,2},{4,5},{5,4},{6,7},{7,6},{8,9},{9,8},{10,11... | collective-permute-start | bytes 3932168 | tf_op jit(solution)/shard_map/ppermute | solution.py:362
  104.0 31.3 %collective-permute-start.6 = (bf16[128,5120]{1,0:T(8,128)(2,1)S(1)}, bf16[128,5120]{1,0:T(8,128)(2,1)S(1)}, u32[]{:S(2)}, u32[]{:S(2)}) collective-permute-start(bf16[128,5120]{1,0:T(8,128)(2,1)S(1)} %get-tuple-element.30), channel_id=1, source_target_pairs={{1,2},{2,1},{5,6},{6,5},{9,10},{10,9},{13,14},{14,13},{17,18},{18,... | collective-permute-start | bytes 3932168 | tf_op jit(solution)/shard_map/ppermute | solution.py:362
  133.4 1.1 copy-start.8
  135.3 44.5 %collective-permute-start.7 = (bf16[128,5120]{1,0:T(8,128)(2,1)}, bf16[128,5120]{1,0:T(8,128)(2,1)}, u32[]{:S(2)}, u32[]{:S(2)}) collective-permute-start(bf16[128,5120]{1,0:T(8,128)(2,1)} %get-tuple-element.35), channel_id=1, source_target_pairs={{1,2},{2,1},{5,6},{6,5},{9,10},{10,9},{13,14},{14,13},{17,18},{18,... | collective-permute-start | bytes 3932168 | tf_op jit(solution)/shard_map/ppermute | solution.py:362
  137.6 42.2 %collective-permute-start.8 = (bf16[128,5120]{1,0:T(8,128)(2,1)S(1)}, bf16[128,5120]{1,0:T(8,128)(2,1)S(1)}, u32[]{:S(2)}, u32[]{:S(2)}) collective-permute-start(bf16[128,5120]{1,0:T(8,128)(2,1)S(1)} %collective-permute-done.6.refs_0_), channel_id=1, source_target_pairs={{1,0},{2,3},{5,4},{6,7},{9,8},{10,11},{13,12},{14,15},{17,16},{18,... | collective-permute-start | bytes 3932168 | tf_op jit(solution)/shard_map/ppermute | solution.py:362
  139.0 39.9 %collective-permute-start.5 = (bf16[64,5120]{1,0:T(8,128)(2,1)S(1)}, bf16[64,5120]{1,0:T(8,128)(2,1)S(1)}, u32[]{:S(2)}, u32[]{:S(2)}) collective-permute-start(bf16[64,5120]{1,0:T(8,128)(2,1)S(1)} %get-tuple-element.25), channel_id=1, source_target_pairs={{0,1},{1,0},{2,3},{3,2},{4,5},{5,4},{6,7},{7,6},{8,9},{9,8},{10,11... | collective-permute-start | bytes 1966088 | tf_op jit(solution)/shard_map/ppermute | solution.py:362
  178.9 0.9 copy-start.10
  179.8 1.1 copy-start.6
  180.9 30.8 %collective-permute-start.10 = (bf16[128,5120]{1,0:T(8,128)(2,1)S(1)}, bf16[128,5120]{1,0:T(8,128)(2,1)}, u32[]{:S(2)}, u32[]{:S(2)}) collective-permute-start(bf16[128,5120]{1,0:T(8,128)(2,1)S(1)} %get-tuple-element.30), channel_id=1, source_target_pairs={{0,2},{3,1},{4,6},{7,5},{8,10},{11,9},{12,14},{15,13},{16,18},{19,... | collective-permute-start | bytes 3932168 | tf_op jit(solution)/shard_map/ppermute | solution.py:362
  182.2 59.3 %collective-permute-start.9 = (bf16[128,5120]{1,0:T(8,128)(2,1)}, bf16[128,5120]{1,0:T(8,128)(2,1)}, u32[]{:S(2)}, u32[]{:S(2)}) collective-permute-start(bf16[128,5120]{1,0:T(8,128)(2,1)} %collective-permute-done.7.refs_1_), channel_id=1, source_target_pairs={{1,0},{2,3},{5,4},{6,7},{9,8},{10,11},{13,12},{14,15},{17,16},{18,... | collective-permute-start | bytes 3932168 | tf_op jit(solution)/shard_map/ppermute | solution.py:362
  211.6 30.0 %collective-permute-start.12 = (bf16[128,5120]{1,0:T(8,128)(2,1)}, bf16[128,5120]{1,0:T(8,128)(2,1)}, u32[]{:S(2)}, u32[]{:S(2)}) collective-permute-start(bf16[128,5120]{1,0:T(8,128)(2,1)} %get-tuple-element.35), channel_id=1, source_target_pairs={{0,2},{3,1},{4,6},{7,5},{8,10},{11,9},{12,14},{15,13},{16,18},{19,... | collective-permute-start | bytes 3932168 | tf_op jit(solution)/shard_map/ppermute | solution.py:362
  215.3 56.1 %collective-permute-start.11 = (bf16[128,5120]{1,0:T(8,128)(2,1)}, bf16[128,5120]{1,0:T(8,128)(2,1)}, u32[]{:S(2)}, u32[]{:S(2)}) collective-permute-start(bf16[128,5120]{1,0:T(8,128)(2,1)} %collective-permute-done.10.refs_0_), channel_id=1, source_target_pairs={{1,0},{2,3},{5,4},{6,7},{9,8},{10,11},{13,12},{14,15},{17,16},{18,... | collective-permute-start | bytes 3932168 | tf_op jit(solution)/shard_map/ppermute | solution.py:362
  222.7 1.3 copy-start.9
  224.0 1.1 copy-start.11
  241.7 40.1 %collective-permute-start.13 = (bf16[128,5120]{1,0:T(8,128)(2,1)}, bf16[128,5120]{1,0:T(8,128)(2,1)}, u32[]{:S(2)}, u32[]{:S(2)}) collective-permute-start(bf16[128,5120]{1,0:T(8,128)(2,1)} %collective-permute-done.12.refs_0_), channel_id=1, source_target_pairs={{1,0},{2,3},{5,4},{6,7},{9,8},{10,11},{13,12},{14,15},{17,16},{18,... | collective-permute-start | bytes 3932168 | tf_op jit(solution)/shard_map/ppermute | solution.py:362
  245.2 1.3 copy-start.7
  246.5 11.8 %copy-start.5 = (bf16[512,1536]{1,0:T(8,128)(2,1)S(1)}, bf16[512,1536]{1,0:T(8,128)(2,1)}, u32[]{:S(2)}) copy-start(bf16[512,1536]{1,0:T(8,128)(2,1)} %project.4.refs_0_) | copy-start | bytes 4718596
  258.4 1.1 copy-start
  269.7 1.6 copy-start.2
  281.7 10.7 %copy-start.1 = (bf16[256,1536]{1,0:T(8,128)(2,1)S(1)}, bf16[256,1536]{1,0:T(8,128)(2,1)}, u32[]{:S(2)}) copy-start(bf16[256,1536]{1,0:T(8,128)(2,1)} %project.5.refs_1_) | copy-start | bytes 2359300
  281.7 10.7 %copy-start.3 = (bf16[128,1536]{1,0:T(8,128)(2,1)S(1)}, bf16[128,1536]{1,0:T(8,128)(2,1)}, u32[]{:S(2)}) copy-start(bf16[128,1536]{1,0:T(8,128)(2,1)} %project.6.refs_2_) | copy-start | bytes 1179652
  292.4 1.0 copy-start.4
Sparse Core Ops, SparseCore 0:
  10.9 33.0 all-gather.4
  99.3 32.0 all-gather.6
  133.0 32.9 all-gather.8
  167.5 32.9 all-gather.10
